TPU v7x, 256 devices: a whole 4x4x8 slice. The times are simulated.
256 devices in a mesh: dp: 8 (over x, core), seq: 32 (over z, y).
Axes of the slice: x: 4, y: 4, z: 8, core: 2. Of those that a mesh axis runs over, the one named last changes fastest.
Arguments:
- frames: bfloat16 [8, 4096, 1024], P('dp', 'seq'), may hold values from -6 to 6
- segment_ids: int32 [8, 4096], P('dp', 'seq'), may hold values from 0 to 15, never falling along the last dimension, each value on 1 to 768 neighbouring positions
- norm_gain: float32 [1024], replicated, may hold values from 0.1 to 1.9
- w_qkv: bfloat16 [1024, 3072], replicated, as said below
- w_out: bfloat16 [1024, 1024], replicated, may hold values from -0.1875 to 0.1875
- cotangent: bfloat16 [8, 4096, 1024], P('dp', 'seq'), may hold values from -6 to 6
Outputs:
- block_out: bfloat16 [8, 4096, 1024], P('dp', 'seq')
- out_grad: float32 [1024, 1024], P('seq', 'dp')
Inputs may be any that keep to these rules, and one draw needn't show every extreme that they name: `segment_ids`: within each data group, utterance numbers never fall along the frames; each utterance covers 1 to 768 frames, and some utterance covers exactly 768. `w_qkv`: projection weights of magnitude below 1; query-key products of some heads can be large.
All inputs are finite; a program needn't handle non-finite values.
Results may differ from a plain program's by a relative error of at most 0.025.
Values may be sent and summed in bfloat16 or wider, within the bound.
No kernel may reach another device: no remote copies, remote signals or barrier semaphores. Data moves between devices by JAX's collectives and lax.ppermute only.
A program may use at most 128 MiB of HBM per device.

v0:
```python
import functools

import jax
import jax.numpy as jnp
from jax import lax
from jax.experimental import pallas as pl
from jax.experimental.pallas import tpu as pltpu
from jax.sharding import PartitionSpec as P

HEADS = 16
ROWS = 128
LANES = 128
WIDTH = 1024
CHUNKS = WIDTH // LANES
PACKED = WIDTH + 16
QUAD = 256
QUADS = WIDTH // QUAD
NEG_BIG = -1e30
EPSILON = 1e-05
LOG2E = 1.4426950408889634
F32 = jnp.float32
BF16 = jnp.bfloat16


def vmem_limit(mib):
    return pltpu.CompilerParams(vmem_limit_bytes=mib * 1024 * 1024)


def shifted(block, distance):
    devices = range(lax.axis_size("seq"))
    route = [(i - distance, i) for i in devices if i - distance in devices]
    return lax.ppermute(block, "seq", route)


def norm_kernel(frames_ref, ids_ref, gain_ref, packed_ref):
    float_frames = frames_ref[...].astype(F32)
    average = jnp.mean(float_frames, axis=-1, keepdims=True)
    centered = float_frames - average
    variance = jnp.mean(centered * centered, axis=-1, keepdims=True)
    normed = (centered * lax.rsqrt(variance + EPSILON) * gain_ref[...]).astype(BF16)
    for c in range(CHUNKS):
        packed_ref[c * ROWS : (c + 1) * ROWS, :] = normed[:, c * LANES : (c + 1) * LANES]
    ids = (ids_ref[...] + 1).astype(F32)
    packed_ref[WIDTH:PACKED, :] = jnp.broadcast_to(ids, (16, LANES)).astype(BF16)


def normalize(frames, ids, gain):
    return pl.pallas_call(
        norm_kernel,
        out_shape=jax.ShapeDtypeStruct((PACKED, LANES), BF16),
        name="layer_norm",
    )(frames, ids, gain)


def unpacked(ref):
    return jnp.concatenate([ref[c * ROWS : (c + 1) * ROWS, :] for c in range(CHUNKS)], axis=1)


def id_row(ref):
    return ref[WIDTH:PACKED, :].astype(F32)[0:1, :]


def id_column(row):
    across = lax.broadcasted_iota(jnp.int32, (ROWS, LANES), 1)
    down = lax.broadcasted_iota(jnp.int32, (ROWS, LANES), 0)
    return jnp.sum(jnp.where(across == down, row, 0.0), axis=1, keepdims=True)


def low_half():
    return lax.broadcasted_iota(jnp.int32, (ROWS, LANES), 1) < LANES // 2


def pair_queries(queries):
    low = low_half()
    zeros = jnp.zeros_like(queries)
    return jnp.concatenate([jnp.where(low, queries, zeros), jnp.where(low, zeros, queries)], axis=0)


def pair_scores(queries, keys, mask):
    scores = lax.dot_general(
        pair_queries(queries), keys, (((1,), (1,)), ((), ())), preferred_element_type=F32
    )
    return jnp.where(jnp.concatenate([mask, mask], axis=0), scores * LOG2E, NEG_BIG)


def side_by_side(stacked):
    return jnp.where(low_half(), stacked[:ROWS], stacked[ROWS:])


def column(block, index):
    return block[:, index : index + 1]


def with_columns(block, columns):
    lane = lax.broadcasted_iota(jnp.int32, (ROWS, LANES), 1)
    for index, values in columns:
        block = jnp.where(lane == index, values, block)
    return block


def first_absorb(queries, keys, values, mask, tops_ref, sums_ref, acc_ref):
    tops = jnp.zeros((ROWS, LANES), F32)
    sums = jnp.zeros((ROWS, LANES), F32)
    for pair in range(2):
        at = slice(pair * LANES, (pair + 1) * LANES)
        scores = pair_scores(queries[:, at], keys[:, at], mask)
        top = jnp.max(scores, axis=1, keepdims=True)
        weights = jnp.exp2(scores - top)
        total = jnp.sum(weights, axis=1, keepdims=True)
        mixed = jnp.dot(weights.astype(BF16), values[:, at], preferred_element_type=F32)
        tops = with_columns(tops, ((2 * pair, top[:ROWS]), (2 * pair + 1, top[ROWS:])))
        sums = with_columns(sums, ((2 * pair, total[:ROWS]), (2 * pair + 1, total[ROWS:])))
        acc_ref[:, at] = side_by_side(mixed)
    tops_ref[...] = tops
    sums_ref[...] = sums


def next_absorb(queries, keys, values, mask, tops_ref, sums_ref, acc_ref):
    tops = tops_ref[...]
    sums = sums_ref[...]
    for pair in range(2):
        at = slice(pair * LANES, (pair + 1) * LANES)
        one, two = 2 * pair, 2 * pair + 1
        scores = pair_scores(queries[:, at], keys[:, at], mask)
        old_top = jnp.concatenate([column(tops, one), column(tops, two)], axis=0)
        old_sum = jnp.concatenate([column(sums, one), column(sums, two)], axis=0)
        top = jnp.maximum(old_top, jnp.max(scores, axis=1, keepdims=True))
        rescale = jnp.exp2(old_top - top)
        weights = jnp.exp2(scores - top)
        total = old_sum * rescale + jnp.sum(weights, axis=1, keepdims=True)
        mixed = jnp.dot(weights.astype(BF16), values[:, at], preferred_element_type=F32)
        tops = with_columns(tops, ((one, top[:ROWS]), (two, top[ROWS:])))
        sums = with_columns(sums, ((one, total[:ROWS]), (two, total[ROWS:])))
        scale = jnp.where(low_half(), rescale[:ROWS], rescale[ROWS:])
        acc_ref[:, at] = acc_ref[:, at] * scale + side_by_side(mixed)
    tops_ref[...] = tops
    sums_ref[...] = sums


def projected(frames, weight_ref):
    return jnp.dot(frames, weight_ref[...], preferred_element_type=F32).astype(BF16)


def own_kernel(own_ref, wq_ref, wk_ref, wv_ref, queries_ref, tops_ref, sums_ref, acc_ref):
    frames = unpacked(own_ref)
    row = id_row(own_ref)
    mask = id_column(row) == row
    queries = projected(frames, wq_ref) * jnp.asarray(0.125, BF16)
    queries_ref[...] = queries
    keys = projected(frames, wk_ref)
    values = projected(frames, wv_ref)
    first_absorb(queries, keys, values, mask, tops_ref, sums_ref, acc_ref)


def weight_spec(section):
    return pl.BlockSpec((WIDTH, QUAD), lambda j: (0, section * QUADS + j))


PACKED_SPEC = pl.BlockSpec((PACKED, LANES), lambda j: (0, 0))
COLUMN_SPEC = pl.BlockSpec((ROWS, QUAD), lambda j: (0, j))
STAT_SPEC = pl.BlockSpec((None, ROWS, LANES), lambda j: (j, 0, 0))
STATE_SHAPES = (
    jax.ShapeDtypeStruct((QUADS, ROWS, LANES), F32),
    jax.ShapeDtypeStruct((QUADS, ROWS, LANES), F32),
    jax.ShapeDtypeStruct((ROWS, WIDTH), F32),
)


def own_block(own, w_qkv):
    return pl.pallas_call(
        own_kernel,
        grid=(QUADS,),
        in_specs=[PACKED_SPEC, weight_spec(0), weight_spec(1), weight_spec(2)],
        out_specs=[COLUMN_SPEC, STAT_SPEC, STAT_SPEC, COLUMN_SPEC],
        out_shape=[jax.ShapeDtypeStruct((ROWS, WIDTH), BF16), *STATE_SHAPES],
        compiler_params=vmem_limit(24),
        cost_estimate=pl.CostEstimate(
            flops=2 * ROWS * WIDTH * 3 * WIDTH, bytes_accessed=7 << 20, transcendentals=0
        ),
        name="own_block",
    )(own, w_qkv, w_qkv, w_qkv)


def absorb_group(near_ref, far_ref, own_row, queries, wk_ref, wv_ref, state):
    frames = jnp.concatenate([unpacked(near_ref), unpacked(far_ref)], axis=0)
    keys = projected(frames, wk_ref)
    values = projected(frames, wv_ref)
    rows = jnp.concatenate([id_row(near_ref), id_row(far_ref)], axis=1)
    mask = id_column(own_row) == rows
    next_absorb(queries, keys, values, mask, *state)


def absorb_both(own_ref, left_near, left_far, right_near, right_far, queries_ref, wk_ref, wv_ref, state):
    own_row = id_row(own_ref)
    left_needed = jnp.max(id_row(left_near)) == jnp.min(own_row)
    right_needed = jnp.min(id_row(right_near)) == jnp.max(own_row)

    @pl.when(left_needed)
    def _():
        absorb_group(left_near, left_far, own_row, queries_ref[...], wk_ref, wv_ref, state)

    @pl.when(right_needed)
    def _():
        absorb_group(right_near, right_far, own_row, queries_ref[...], wk_ref, wv_ref, state)


def stage_kernel(
    own_ref, left_near, left_far, right_near, right_far, queries_ref, wk_ref, wv_ref,
    old_tops, old_sums, old_acc, tops_ref, sums_ref, acc_ref,
):
    tops_ref[...] = old_tops[...]
    sums_ref[...] = old_sums[...]
    acc_ref[...] = old_acc[...]
    state = (tops_ref, sums_ref, acc_ref)
    absorb_both(own_ref, left_near, left_far, right_near, right_far, queries_ref, wk_ref, wv_ref, state)


STAGE_COST = pl.CostEstimate(
    flops=2 * 4 * ROWS * WIDTH * 2 * WIDTH, bytes_accessed=8 << 20, transcendentals=0
)


def absorb_stage(own, near_far, queries, w_qkv, state):
    return pl.pallas_call(
        stage_kernel,
        grid=(QUADS,),
        in_specs=[PACKED_SPEC] * 5
        + [COLUMN_SPEC, weight_spec(1), weight_spec(2), STAT_SPEC, STAT_SPEC, COLUMN_SPEC],
        out_specs=[STAT_SPEC, STAT_SPEC, COLUMN_SPEC],
        out_shape=list(STATE_SHAPES),
        compiler_params=vmem_limit(32),
        cost_estimate=STAGE_COST,
        name="absorb_stage",
    )(own, *near_far, queries, w_qkv, w_qkv, *state)


def last_kernel(
    own_ref, left_near, left_far, right_near, right_far, queries_ref, wk_ref, wv_ref,
    old_tops, old_sums, old_acc, frames_ref, wout_ref, attended_ref, out_ref,
    tops_ref, sums_ref, acc_ref, total_ref,
):
    quad = pl.program_id(0)
    tops_ref[...] = old_tops[...]
    sums_ref[...] = old_sums[...]
    acc_ref[...] = old_acc[...]
    state = (tops_ref, sums_ref, acc_ref)
    absorb_both(own_ref, left_near, left_far, right_near, right_far, queries_ref, wk_ref, wv_ref, state)
    sums = sums_ref[...]
    parts = []
    for pair in range(2):
        at = slice(pair * LANES, (pair + 1) * LANES)
        divisor = jnp.where(low_half(), column(sums, 2 * pair), column(sums, 2 * pair + 1))
        part = (acc_ref[:, at] / divisor).astype(BF16)
        attended_ref[pair] = part
        parts.append(part)
    term = jnp.dot(jnp.concatenate(parts, axis=1), wout_ref[...], preferred_element_type=F32)

    @pl.when(quad == 0)
    def _():
        total_ref[...] = frames_ref[...].astype(F32) + term

    @pl.when(quad > 0)
    def _():
        total_ref[...] += term

    @pl.when(quad == QUADS - 1)
    def _():
        out_ref[...] = total_ref[...].astype(BF16)


def last_stage(own, near_far, queries, w_qkv, state, frames, w_out):
    return pl.pallas_call(
        last_kernel,
        grid=(QUADS,),
        in_specs=[PACKED_SPEC] * 5
        + [COLUMN_SPEC, weight_spec(1), weight_spec(2), STAT_SPEC, STAT_SPEC, COLUMN_SPEC]
        + [
            pl.BlockSpec((ROWS, WIDTH), lambda j: (0, 0)),
            pl.BlockSpec((QUAD, WIDTH), lambda j: (j, 0)),
        ],
        out_specs=[
            pl.BlockSpec((2, ROWS, LANES), lambda j: (j, 0, 0)),
            pl.BlockSpec((ROWS, WIDTH), lambda j: (0, 0)),
        ],
        out_shape=[
            jax.ShapeDtypeStruct((CHUNKS, ROWS, LANES), BF16),
            jax.ShapeDtypeStruct((ROWS, WIDTH), BF16),
        ],
        scratch_shapes=[
            pltpu.VMEM((ROWS, LANES), F32),
            pltpu.VMEM((ROWS, LANES), F32),
            pltpu.VMEM((ROWS, QUAD), F32),
            pltpu.VMEM((ROWS, WIDTH), F32),
        ],
        compiler_params=vmem_limit(32),
        cost_estimate=STAGE_COST,
        name="last_stage",
    )(own, *near_far, queries, w_qkv, w_qkv, *state, frames, w_out)


def grad_kernel(attended_ref, cotangent_ref, out_ref):
    product = lax.dot_general(
        attended_ref[...], cotangent_ref[...], (((0,), (0,)), ((), ())), preferred_element_type=F32
    ).astype(BF16)
    for half in range(2):
        out_ref[half] = product[:, half * LANES : (half + 1) * LANES]


def grad_product(attended, cotangent):
    frames = attended.shape[0]
    return pl.pallas_call(
        grad_kernel,
        grid=(QUADS,),
        in_specs=[
            pl.BlockSpec((frames, LANES), lambda j: (0, 0)),
            pl.BlockSpec((frames, QUAD), lambda j: (0, j)),
        ],
        out_specs=pl.BlockSpec((2, LANES, LANES), lambda j: (j, 0, 0)),
        out_shape=jax.ShapeDtypeStruct((CHUNKS, LANES, LANES), BF16),
        compiler_params=vmem_limit(16),
        name="grad_product",
    )(attended, cotangent)


def local(frames, segment_ids, norm_gain, w_qkv, w_out, cotangent):
    n_dp = lax.axis_size("dp")
    n_seq = lax.axis_size("seq")
    frames = frames[0]
    own = normalize(frames, segment_ids, norm_gain[None, :])
    all_grads = lax.all_gather(cotangent[0], "dp", axis=0, tiled=True)

    left1, right1 = shifted(own, 1), shifted(own, -1)
    left4, right4 = shifted(own, 4), shifted(own, -4)
    queries, *state = own_block(own, w_qkv)

    left2, right2 = shifted(left1, 1), shifted(right1, -1)
    left5, right5 = shifted(left1, 4), shifted(right1, -4)
    state = absorb_stage(own, (left1, left4, right1, right4), queries, w_qkv, state)

    left3, right3 = shifted(left2, 1), shifted(right2, -1)
    left6, right6 = shifted(left2, 4), shifted(right2, -4)
    state = absorb_stage(own, (left2, left5, right2, right5), queries, w_qkv, state)

    attended, block_out = last_stage(
        own, (left3, left6, right3, right6), queries, w_qkv, state, frames, w_out
    )

    swapped = lax.all_to_all(attended, "dp", 0, 0, tiled=True)
    share = grad_product(swapped.reshape(n_dp * ROWS, LANES), all_grads)
    pieces = lax.all_to_all(share.reshape(n_seq, LANES * CHUNKS // n_seq, LANES), "seq", 0, 0, tiled=True)
    grad_scale = (n_dp * n_seq * ROWS) ** (-0.5)
    block = jnp.sum(pieces.astype(F32), axis=0) * grad_scale
    inner = n_seq // n_dp
    route = [
        (p * n_seq + q * inner + r, q * n_seq + p * inner + r)
        for p in range(n_dp)
        for q in range(n_dp)
        for r in range(inner)
    ]
    return (block_out[None], lax.ppermute(block, ("dp", "seq"), route))


def solution(mesh):
    placed = (P("dp", "seq", None), P("dp", "seq"), P(), P(), P(), P("dp", "seq", None))
    return jax.shard_map(
        local,
        mesh=mesh,
        in_specs=placed,
        out_specs=(P("dp", "seq", None), P("seq", "dp")),
        check_vma=False,
    )
```

profile of v0, /device:TPU:4, one launch (start us, length us, event | category | flops | bytes accessed | tf_op | source)
XLA Modules:
  0.0 170.6 jit_solution(15421007025698830759)
XLA Ops:
  7.9 1.9 %layer_norm.1.own_ref = bf16[1040,128]{1,0:T(8,128)(2,1)} custom-call(bf16[128,1024]{1,0:T(8,128)(2,1)} %bitcast.7, s32[1,128]{1,0:T(1,128)} %ids_ref.1, f32[1,1024]{1,0:T(1,128)} %bitcast.11), custom_call_target="tpu_custom_call" | custom-call | tf_op jit(solution)/shard_map/layer_norm/pallas_call | solution.py:48
  9.8 3.5 %collective-permute-start = (bf16[1040,128]{1,0:T(8,128)(2,1)}, bf16[1040,128]{1,0:T(8,128)(2,1)S(1)}, u32[]{:S(2)}, u32[]{:S(2)}) collective-permute-start(bf16[1040,128]{1,0:T(8,128)(2,1)} %layer_norm.1.own_ref), channel_id=1, source_target_pairs={{0,1},{1,2},{2,3},{3,4},{4,5},{5,6},{6,7},{7,8},{8,9},{9,10},{10,1... | collective-permute-start | bytes 798728 | tf_op jit(solution)/shard_map/ppermute | solution.py:32
  13.3 1.3 collective-permute-start.4
  14.6 7.0 %collective-permute-start.10 = (bf16[1040,128]{1,0:T(8,128)(2,1)}, bf16[1040,128]{1,0:T(8,128)(2,1)S(1)}, u32[]{:S(2)}, u32[]{:S(2)}) collective-permute-start(bf16[1040,128]{1,0:T(8,128)(2,1)} %layer_norm.1.own_ref), channel_id=1, source_target_pairs={{0,4},{1,5},{2,6},{3,7},{4,8},{5,9},{6,10},{7,11},{8,12},{9,13},{1... | collective-permute-start | bytes 798728 | tf_op jit(solution)/shard_map/ppermute | solution.py:32
  21.6 1.9 %collective-permute-start.1 = (bf16[1040,128]{1,0:T(8,128)(2,1)S(1)}, bf16[1040,128]{1,0:T(8,128)(2,1)S(1)}, u32[]{:S(2)}, u32[]{:S(2)}) collective-permute-start(bf16[1040,128]{1,0:T(8,128)(2,1)S(1)} %collective-permute-done.left_near), channel_id=1, source_target_pairs={{0,1},{1,2},{2,3},{3,4},{4,5},{5,6},{6,7},{7,8},{8,9},{9,10},{10,1... | collective-permute-start | bytes 798728 | tf_op jit(solution)/shard_map/ppermute | solution.py:32
  23.5 1.3 collective-permute-start.11
  24.9 1.3 collective-permute-start.5
  26.1 9.1 %collective-permute-start.8 = (bf16[1040,128]{1,0:T(8,128)(2,1)S(1)}, bf16[1040,128]{1,0:T(8,128)(2,1)S(1)}, u32[]{:S(2)}, u32[]{:S(2)}) collective-permute-start(bf16[1040,128]{1,0:T(8,128)(2,1)S(1)} %collective-permute-done.left_near), channel_id=1, source_target_pairs={{0,4},{1,5},{2,6},{3,7},{4,8},{5,9},{6,10},{7,11},{8,12},{9,13},{1... | collective-permute-start | bytes 798728 | tf_op jit(solution)/shard_map/ppermute | solution.py:32
  35.3 1.3 collective-permute-start.9
  36.6 2.9 %copy-done = bf16[1024,3072]{1,0:T(8,128)(2,1)S(1)} copy-done((bf16[1024,3072]{1,0:T(8,128)(2,1)S(1)}, bf16[1024,3072]{1,0:T(8,128)(2,1)}, u32[]{:S(2)}) %copy-start) | copy-done | bytes 6291480
  40.4 4.6 %own_block.1 = (bf16[128,1024]{1,0:T(8,128)(2,1)S(1)}, f32[4,128,128]{2,1,0:T(8,128)S(1)}, f32[4,128,128]{2,1,0:T(8,128)S(1)}, f32[128,1024]{1,0:T(8,128)S(1)}) custom-call(bf16[1040,128]{1,0:T(8,128)(2,1)S(1)} %copy-done.2, bf16[1024,3072]{1,0:T(8,128)(2,1)S(1)} %copy-done, bf16[1024,3072]{1,0:T(8,128)(2,1)S(1)} %copy-done, bf16[1024,3072]{1,0:T(8,128)(2,1)S(1)} %copy-done), custom_call_target="tpu_custom_call" | custom-call | flops 805306368 | bytes 7340032 | tf_op jit(solution)/shard_map/own_block/pallas_call | solution.py:170
  45.0 1.3 collective-permute-start.2
  46.3 5.7 %collective-permute-start.3 = (bf16[1040,128]{1,0:T(8,128)(2,1)S(1)}, bf16[1040,128]{1,0:T(8,128)(2,1)S(1)}, u32[]{:S(2)}, u32[]{:S(2)}) collective-permute-start(bf16[1040,128]{1,0:T(8,128)(2,1)S(1)} %collective-permute-done.1.left_near), channel_id=1, source_target_pairs={{0,4},{1,5},{2,6},{3,7},{4,8},{5,9},{6,10},{7,11},{8,12},{9,13},{1... | collective-permute-start | bytes 798728 | tf_op jit(solution)/shard_map/ppermute | solution.py:32
  53.4 1.3 collective-permute-start.7
  54.7 9.4 %absorb_stage.2 = (f32[4,128,128]{2,1,0:T(8,128)S(1)}, f32[4,128,128]{2,1,0:T(8,128)S(1)}, f32[128,1024]{1,0:T(8,128)S(1)}) custom-call(bf16[1040,128]{1,0:T(8,128)(2,1)S(1)} %copy-done.3, bf16[1040,128]{1,0:T(8,128)(2,1)S(1)} %collective-permute-done.left_near, bf16[1040,128]{1,0:T(8,128)(2,1)S(1)} %collective-permute-done.10.left_far, ...), custom_call_target="tpu_custom_call" | custom-call | flops 2147483648 | bytes 8388608 | tf_op jit(solution)/shard_map/absorb_stage/pallas_call | solution.py:224
  64.2 1.4 absorb_stage.3
  65.6 5.8 %collective-permute-done.7.right_far = bf16[1040,128]{1,0:T(8,128)(2,1)S(1)} collective-permute-done((bf16[1040,128]{1,0:T(8,128)(2,1)S(1)}, bf16[1040,128]{1,0:T(8,128)(2,1)S(1)}, u32[]{:S(2)}, u32[]{:S(2)}) %collective-permute-start.7) | collective-permute-done | bytes 266272 | tf_op jit(solution)/shard_map/ppermute | solution.py:32
  71.4 3.6 %last_stage.1 = (bf16[8,128,128]{2,1,0:T(8,128)(2,1)S(1)}, bf16[128,1024]{1,0:T(8,128)(2,1)}) custom-call(bf16[1040,128]{1,0:T(8,128)(2,1)S(1)} %copy-done.3, bf16[1040,128]{1,0:T(8,128)(2,1)S(1)} %collective-permute-done.2.left_near, bf16[1040,128]{1,0:T(8,128)(2,1)S(1)} %collective-permute-done.3.left_far, ...), custom_call_target="tpu_custom_call" | custom-call | flops 2147483648 | bytes 8388608 | tf_op jit(solution)/shard_map/last_stage/pallas_call | solution.py:272
  75.0 17.8 %all_to_all.10 = bf16[8,128,128]{2,1,0:T(8,128)(2,1)S(1)} all-to-all(bf16[8,128,128]{2,1,0:T(8,128)(2,1)S(1)} %get-tuple-element.25), channel_id=1, replica_groups=mesh['dp'=8,'seq'=32] {'dp'}, dimensions={0} | all-to-all | bytes 524288 | tf_op jit(solution)/shard_map/all_to_all | solution.py:348
  92.8 1.6 copy-done.4
  94.4 1.4 grad_product.1
  95.8 55.3 %all_to_all.11 = bf16[32,32,128]{2,1,0:T(8,128)(2,1)S(1)} all-to-all(bf16[32,32,128]{2,1,0:T(8,128)(2,1)S(1)} %bitcast.10), channel_id=1, replica_groups=mesh['dp'=8,'seq'=32] {'seq'}, dimensions={0} | all-to-all | bytes 524288 | tf_op jit(solution)/shard_map/all_to_all | solution.py:350
  151.2 5.6 %collective-permute-start.12 = (f32[32,128]{1,0:T(8,128)S(1)}, f32[32,128]{1,0:T(8,128)S(1)}, u32[]{:S(2)}, u32[]{:S(2)}) collective-permute-start(f32[32,128]{1,0:T(8,128)S(1)} %broadcast_multiply_fusion), channel_id=1, source_target_pairs={{0,0},{1,1},{2,2},{3,3},{4,32},{5,33},{6,34},{7,35},{8,64},{9,65},... | collective-permute-start | bytes 49160 | tf_op jit(solution)/shard_map/ppermute | solution.py:360
  156.9 6.3 %collective-permute-done.12 = f32[32,128]{1,0:T(8,128)S(1)} collective-permute-done((f32[32,128]{1,0:T(8,128)S(1)}, f32[32,128]{1,0:T(8,128)S(1)}, u32[]{:S(2)}, u32[]{:S(2)}) %collective-permute-start.12) | collective-permute-done | bytes 16416 | tf_op jit(solution)/shard_map/ppermute | solution.py:360
  (30 shorter events, 3.7 us)
Async XLA Ops:
  7.2 85.6 %all-gather.3.cloned.1.call-start = ((), (), s32[]{:S(2)}) async-start(), calls=%async_computation.2 | async-start | bytes 2359296 | tf_op jit(solution)/shard_map/all_gather | solution.py:330
  9.8 11.8 %collective-permute-start = (bf16[1040,128]{1,0:T(8,128)(2,1)}, bf16[1040,128]{1,0:T(8,128)(2,1)S(1)}, u32[]{:S(2)}, u32[]{:S(2)}) collective-permute-start(bf16[1040,128]{1,0:T(8,128)(2,1)} %layer_norm.1.own_ref), channel_id=1, source_target_pairs={{0,1},{1,2},{2,3},{3,4},{4,5},{5,6},{6,7},{7,8},{8,9},{9,10},{10,1... | collective-permute-start | bytes 798728 | tf_op jit(solution)/shard_map/ppermute | solution.py:32
  13.3 11.5 %collective-permute-start.4 = (bf16[1040,128]{1,0:T(8,128)(2,1)}, bf16[1040,128]{1,0:T(8,128)(2,1)S(1)}, u32[]{:S(2)}, u32[]{:S(2)}) collective-permute-start(bf16[1040,128]{1,0:T(8,128)(2,1)} %layer_norm.1.own_ref), channel_id=1, source_target_pairs={{1,0},{2,1},{3,2},{4,3},{5,4},{6,5},{7,6},{8,7},{9,8},{10,9},{11,1... | collective-permute-start | bytes 798728 | tf_op jit(solution)/shard_map/ppermute | solution.py:32
  14.6 20.7 %collective-permute-start.10 = (bf16[1040,128]{1,0:T(8,128)(2,1)}, bf16[1040,128]{1,0:T(8,128)(2,1)S(1)}, u32[]{:S(2)}, u32[]{:S(2)}) collective-permute-start(bf16[1040,128]{1,0:T(8,128)(2,1)} %layer_norm.1.own_ref), channel_id=1, source_target_pairs={{0,4},{1,5},{2,6},{3,7},{4,8},{5,9},{6,10},{7,11},{8,12},{9,13},{1... | collective-permute-start | bytes 798728 | tf_op jit(solution)/shard_map/ppermute | solution.py:32
  21.6 23.4 %collective-permute-start.1 = (bf16[1040,128]{1,0:T(8,128)(2,1)S(1)}, bf16[1040,128]{1,0:T(8,128)(2,1)S(1)}, u32[]{:S(2)}, u32[]{:S(2)}) collective-permute-start(bf16[1040,128]{1,0:T(8,128)(2,1)S(1)} %collective-permute-done.left_near), channel_id=1, source_target_pairs={{0,1},{1,2},{2,3},{3,4},{4,5},{5,6},{6,7},{7,8},{8,9},{9,10},{10,1... | collective-permute-start | bytes 798728 | tf_op jit(solution)/shard_map/ppermute | solution.py:32
  23.5 22.8 %collective-permute-start.11 = (bf16[1040,128]{1,0:T(8,128)(2,1)}, bf16[1040,128]{1,0:T(8,128)(2,1)S(1)}, u32[]{:S(2)}, u32[]{:S(2)}) collective-permute-start(bf16[1040,128]{1,0:T(8,128)(2,1)} %layer_norm.1.own_ref), channel_id=1, source_target_pairs={{4,0},{5,1},{6,2},{7,3},{8,4},{9,5},{10,6},{11,7},{12,8},{13,9},{1... | collective-permute-start | bytes 798728 | tf_op jit(solution)/shard_map/ppermute | solution.py:32
  24.9 27.2 %collective-permute-start.5 = (bf16[1040,128]{1,0:T(8,128)(2,1)S(1)}, bf16[1040,128]{1,0:T(8,128)(2,1)S(1)}, u32[]{:S(2)}, u32[]{:S(2)}) collective-permute-start(bf16[1040,128]{1,0:T(8,128)(2,1)S(1)} %collective-permute-done.4.right_near), channel_id=1, source_target_pairs={{1,0},{2,1},{3,2},{4,3},{5,4},{6,5},{7,6},{8,7},{9,8},{10,9},{11,1... | collective-permute-start | bytes 798728 | tf_op jit(solution)/shard_map/ppermute | solution.py:32
  26.1 27.2 %collective-permute-start.8 = (bf16[1040,128]{1,0:T(8,128)(2,1)S(1)}, bf16[1040,128]{1,0:T(8,128)(2,1)S(1)}, u32[]{:S(2)}, u32[]{:S(2)}) collective-permute-start(bf16[1040,128]{1,0:T(8,128)(2,1)S(1)} %collective-permute-done.left_near), channel_id=1, source_target_pairs={{0,4},{1,5},{2,6},{3,7},{4,8},{5,9},{6,10},{7,11},{8,12},{9,13},{1... | collective-permute-start | bytes 798728 | tf_op jit(solution)/shard_map/ppermute | solution.py:32
  35.3 28.9 %collective-permute-start.9 = (bf16[1040,128]{1,0:T(8,128)(2,1)S(1)}, bf16[1040,128]{1,0:T(8,128)(2,1)S(1)}, u32[]{:S(2)}, u32[]{:S(2)}) collective-permute-start(bf16[1040,128]{1,0:T(8,128)(2,1)S(1)} %collective-permute-done.4.right_near), channel_id=1, source_target_pairs={{4,0},{5,1},{6,2},{7,3},{8,4},{9,5},{10,6},{11,7},{12,8},{13,9},{1... | collective-permute-start | bytes 798728 | tf_op jit(solution)/shard_map/ppermute | solution.py:32
  36.6 2.9 %copy-start = (bf16[1024,3072]{1,0:T(8,128)(2,1)S(1)}, bf16[1024,3072]{1,0:T(8,128)(2,1)}, u32[]{:S(2)}) copy-start(bf16[1024,3072]{1,0:T(8,128)(2,1)} %wv_ref.7) | copy-start | bytes 18874372
  39.4 1.0 copy-start.2
  40.4 14.3 %copy-start.1 = (bf16[1024,3072]{1,0:T(8,128)(2,1)S(1)}, bf16[1024,3072]{1,0:T(8,128)(2,1)}, u32[]{:S(2)}) copy-start(bf16[1024,3072]{1,0:T(8,128)(2,1)} %wv_ref.7) | copy-start | bytes 18874372
  40.4 14.3 %copy-start.3 = (bf16[1040,128]{1,0:T(8,128)(2,1)S(1)}, bf16[1040,128]{1,0:T(8,128)(2,1)}, u32[]{:S(2)}) copy-start(bf16[1040,128]{1,0:T(8,128)(2,1)} %layer_norm.1.own_ref) | copy-start | bytes 798724
  45.0 20.6 %collective-permute-start.2 = (bf16[1040,128]{1,0:T(8,128)(2,1)S(1)}, bf16[1040,128]{1,0:T(8,128)(2,1)S(1)}, u32[]{:S(2)}, u32[]{:S(2)}) collective-permute-start(bf16[1040,128]{1,0:T(8,128)(2,1)S(1)} %collective-permute-done.1.left_near), channel_id=1, source_target_pairs={{0,1},{1,2},{2,3},{3,4},{4,5},{5,6},{6,7},{7,8},{8,9},{9,10},{10,1... | collective-permute-start | bytes 798728 | tf_op jit(solution)/shard_map/ppermute | solution.py:32
  46.3 19.3 %collective-permute-start.3 = (bf16[1040,128]{1,0:T(8,128)(2,1)S(1)}, bf16[1040,128]{1,0:T(8,128)(2,1)S(1)}, u32[]{:S(2)}, u32[]{:S(2)}) collective-permute-start(bf16[1040,128]{1,0:T(8,128)(2,1)S(1)} %collective-permute-done.1.left_near), channel_id=1, source_target_pairs={{0,4},{1,5},{2,6},{3,7},{4,8},{5,9},{6,10},{7,11},{8,12},{9,13},{1... | collective-permute-start | bytes 798728 | tf_op jit(solution)/shard_map/ppermute | solution.py:32
  52.1 13.5 %collective-permute-start.6 = (bf16[1040,128]{1,0:T(8,128)(2,1)S(1)}, bf16[1040,128]{1,0:T(8,128)(2,1)S(1)}, u32[]{:S(2)}, u32[]{:S(2)}) collective-permute-start(bf16[1040,128]{1,0:T(8,128)(2,1)S(1)} %collective-permute-done.5.right_near), channel_id=1, source_target_pairs={{1,0},{2,1},{3,2},{4,3},{5,4},{6,5},{7,6},{8,7},{9,8},{10,9},{11,1... | collective-permute-start | bytes 798728 | tf_op jit(solution)/shard_map/ppermute | solution.py:32
  53.4 18.0 %collective-permute-start.7 = (bf16[1040,128]{1,0:T(8,128)(2,1)S(1)}, bf16[1040,128]{1,0:T(8,128)(2,1)S(1)}, u32[]{:S(2)}, u32[]{:S(2)}) collective-permute-start(bf16[1040,128]{1,0:T(8,128)(2,1)S(1)} %collective-permute-done.5.right_near), channel_id=1, source_target_pairs={{4,0},{5,1},{6,2},{7,3},{8,4},{9,5},{10,6},{11,7},{12,8},{13,9},{1... | collective-permute-start | bytes 798728 | tf_op jit(solution)/shard_map/ppermute | solution.py:32
  64.2 7.2 %copy-start.5 = (bf16[1024,1024]{1,0:T(8,128)(2,1)S(1)}, bf16[1024,1024]{1,0:T(8,128)(2,1)}, u32[]{:S(2)}) copy-start(bf16[1024,1024]{1,0:T(8,128)(2,1)} %wout_ref.1) | copy-start | bytes 6291460
  64.2 7.2 %copy-start.6 = (bf16[1,128,1024]{2,1,0:T(8,128)(2,1)S(1)}, bf16[1,128,1024]{2,1,0:T(8,128)(2,1)}, u32[]{:S(2)}) copy-start(bf16[1,128,1024]{2,1,0:T(8,128)(2,1)} %param.6) | copy-start | bytes 786436
  92.8 1.6 copy-start.4
  151.2 11.9 %collective-permute-start.12 = (f32[32,128]{1,0:T(8,128)S(1)}, f32[32,128]{1,0:T(8,128)S(1)}, u32[]{:S(2)}, u32[]{:S(2)}) collective-permute-start(f32[32,128]{1,0:T(8,128)S(1)} %broadcast_multiply_fusion), channel_id=1, source_target_pairs={{0,0},{1,1},{2,2},{3,3},{4,32},{5,33},{6,34},{7,35},{8,64},{9,65},... | collective-permute-start | bytes 49160 | tf_op jit(solution)/shard_map/ppermute | solution.py:360
Sparse Core Ops, SparseCore 0:
  9.9 29.6 all-gather.2
where the time goes:
time: 172 us; the launch traced here: 171 us
  blocking collectives  73.1 us (42%)
  starting transfers between devices  42 us (24%)
  Pallas kernels  22.3 us (13%)
  between operations  14.3 us (8%)
  waiting for transfers between devices  12.8 us (7%)
  local copies, waits for them, and re-layouts  6.03 us (4%)
    all_to_all x1, blocking collectives, local(): lax.all_to_all(share.reshape(n_seq, LANES * CHUNKS // n_seq, LANES), 'seq...  55.3 us
    ppermute x12, starting transfers between devices, shifted(): return lax.ppermute(block, 'seq', route)  36.3 us
    all_to_all x1, blocking collectives, local(): swapped = lax.all_to_all(attended, 'dp', 0, 0, tiled=True)  17.8 us
    pallas_call x2, Pallas kernels, absorb_stage(): pl.pallas_call(stage_kernel, grid=(QUADS,), in_specs=[PACKED_SPEC] * 5 +...  10.8 us
    ppermute x1, waiting for transfers between devices, local(): return (block_out[None], lax.ppermute(block, ('dp', 'seq'), route))  6.3 us
    unnamed x15, local copies, waits for them, and re-layouts  6.03 us
    ppermute x12, waiting for transfers between devices, shifted(): return lax.ppermute(block, 'seq', route)  5.79 us
    ppermute x1, starting transfers between devices, local(): return (block_out[None], lax.ppermute(block, ('dp', 'seq'), route))  5.64 us
  transfers between devices with their start and end apart: 14, of which 2 were waited for; matrix products, arithmetic and copies ran while one was open for 0% of the time, Pallas kernels for 12%

commit v1 on v0

v1 whole, which is shorter than its diff:
```python
import jax
import jax.numpy as jnp
from jax import lax
from jax.experimental import pallas as pl
from jax.experimental.pallas import tpu as pltpu
from jax.sharding import PartitionSpec as P

ROWS = 128
LANES = 128
HALF = 64
WIDTH = 1024
CHUNKS = WIDTH // LANES
PACKED = WIDTH + 16
QUAD = 256
QUADS = WIDTH // QUAD
NEG_BIG = -1e30
EPSILON = 1e-05
LOG2E = 1.4426950408889634
F32 = jnp.float32
BF16 = jnp.bfloat16
LIMIT = pltpu.CompilerParams(vmem_limit_bytes=24 * 1024 * 1024)


def shifted(block, distance):
    n_seq = lax.axis_size("seq")
    route = [(i, (i + distance) % n_seq) for i in range(n_seq)]
    return lax.ppermute(block, "seq", route)


def norm_kernel(frames_ref, ids_ref, gain_ref, packed_ref):
    float_frames = frames_ref[...].astype(F32)
    average = jnp.mean(float_frames, axis=-1, keepdims=True)
    centered = float_frames - average
    variance = jnp.mean(centered * centered, axis=-1, keepdims=True)
    normed = (centered * lax.rsqrt(variance + EPSILON) * gain_ref[...]).astype(BF16)
    for c in range(CHUNKS):
        packed_ref[c * ROWS : (c + 1) * ROWS, :] = normed[:, c * LANES : (c + 1) * LANES]
    ids = (ids_ref[...] + 1).astype(F32)
    packed_ref[WIDTH:PACKED, :] = jnp.broadcast_to(ids, (16, LANES)).astype(BF16)


def normalize(frames, ids, gain):
    return pl.pallas_call(
        norm_kernel,
        out_shape=jax.ShapeDtypeStruct((PACKED, LANES), BF16),
        compiler_params=LIMIT,
        name="layer_norm",
    )(frames, ids, gain)


def unpacked(block):
    ref, slot = block
    base = slot * PACKED
    chunks = [ref[base + c * ROWS : base + (c + 1) * ROWS, :] for c in range(CHUNKS)]
    return jnp.concatenate(chunks, axis=1)


def id_row(block):
    ref, slot = block
    base = slot * PACKED + WIDTH
    return ref[base : base + 16, :].astype(F32)[0:1, :]


def id_column(row):
    across = lax.broadcasted_iota(jnp.int32, (ROWS, LANES), 1)
    down = lax.broadcasted_iota(jnp.int32, (ROWS, LANES), 0)
    return jnp.sum(jnp.where(across == down, row, 0.0), axis=1, keepdims=True)


def projected(frames, weight_ref):
    return jnp.dot(frames, weight_ref[...], preferred_element_type=F32).astype(BF16)


def absorb(queries_ref, keys, values, mask, tops_ref, sums_ref, acc_ref, first):
    flipped = jnp.transpose(values)
    both = jnp.concatenate([mask, mask], axis=1)
    for pair in range(2):
        at = slice(pair * LANES, (pair + 1) * LANES)
        heads = (2 * pair, 2 * pair + 1)
        scores = lax.dot_general(
            keys[:, at], queries_ref[pair], (((1,), (1,)), ((), ())), preferred_element_type=F32
        )
        scores = jnp.where(both, scores * LOG2E, NEG_BIG)
        top = jnp.max(scores, axis=0, keepdims=True)
        if not first:
            old_top = jnp.concatenate([tops_ref[h : h + 1, :] for h in heads], axis=1)
            old_sum = jnp.concatenate([sums_ref[h : h + 1, :] for h in heads], axis=1)
            top = jnp.maximum(old_top, top)
            rescale = jnp.exp2(old_top - top)
        weights = jnp.exp2(scores - top)
        total = jnp.sum(weights, axis=0, keepdims=True)
        mixed = jnp.dot(flipped[at, :], weights.astype(BF16), preferred_element_type=F32)
        if not first:
            total = old_sum * rescale + total
        for k, h in enumerate(heads):
            lanes = slice(k * LANES, (k + 1) * LANES)
            rows = slice(h * HALF, (h + 1) * HALF)
            term = mixed[k * HALF : (k + 1) * HALF, lanes]
            if not first:
                term = acc_ref[rows, :] * rescale[:, lanes] + term
            acc_ref[rows, :] = term
            tops_ref[h : h + 1, :] = top[:, lanes]
            sums_ref[h : h + 1, :] = total[:, lanes]


def own_kernel(own_ref, wq_ref, wk_ref, wv_ref, queries_ref, tops_ref, sums_ref, acc_ref):
    frames = unpacked((own_ref, 0))
    row = id_row((own_ref, 0))
    queries = projected(frames, wq_ref) * jnp.asarray(0.125, BF16)
    low = lax.broadcasted_iota(jnp.int32, (ROWS, LANES), 1) < HALF
    for pair in range(2):
        block = queries[:, pair * LANES : (pair + 1) * LANES]
        zeros = jnp.zeros_like(block)
        queries_ref[pair, 0:ROWS, :] = jnp.where(low, block, zeros)
        queries_ref[pair, ROWS:, :] = jnp.where(low, zeros, block)
    keys = projected(frames, wk_ref)
    values = projected(frames, wv_ref)
    absorb(queries_ref, keys, values, id_column(row) == row, tops_ref, sums_ref, acc_ref, True)


def weight_spec(section):
    return pl.BlockSpec((WIDTH, QUAD), lambda j: (0, section * QUADS + j))


def packed_spec(block):
    return pl.BlockSpec(block.shape, lambda j: (0, 0))


QUERY_SPEC = pl.BlockSpec((2, 2 * ROWS, LANES), lambda j: (j, 0, 0))
STATE_SPECS = (
    pl.BlockSpec((None, 8, LANES), lambda j: (j, 0, 0)),
    pl.BlockSpec((None, 8, LANES), lambda j: (j, 0, 0)),
    pl.BlockSpec((QUAD, LANES), lambda j: (j, 0)),
)
STATE_SHAPES = (
    jax.ShapeDtypeStruct((QUADS, 8, LANES), F32),
    jax.ShapeDtypeStruct((QUADS, 8, LANES), F32),
    jax.ShapeDtypeStruct((WIDTH, LANES), F32),
)


def cost(blocks, mib):
    return pl.CostEstimate(
        flops=2 * blocks * ROWS * WIDTH * 2 * WIDTH, bytes_accessed=mib << 20, transcendentals=0
    )


def own_block(own, w_qkv):
    return pl.pallas_call(
        own_kernel,
        grid=(QUADS,),
        in_specs=[packed_spec(own), weight_spec(0), weight_spec(1), weight_spec(2)],
        out_specs=[QUERY_SPEC, *STATE_SPECS],
        out_shape=[jax.ShapeDtypeStruct((CHUNKS, 2 * ROWS, LANES), BF16), *STATE_SHAPES],
        compiler_params=LIMIT,
        cost_estimate=cost(3, 8),
        name="own_block",
    )(own, w_qkv, w_qkv, w_qkv)


def absorb_side(blocks, own_row, queries_ref, wk_ref, wv_ref, state):
    frames = jnp.concatenate([unpacked(block) for block in blocks], axis=0)
    keys = projected(frames, wk_ref)
    values = projected(frames, wv_ref)
    columns = jnp.concatenate([id_column(id_row(block)) for block in blocks], axis=0)
    absorb(queries_ref, keys, values, columns == own_row, *state, False)


def absorb_both(own_ref, left, right, queries_ref, wk_ref, wv_ref, state):
    own_row = id_row((own_ref, 0))
    left_needed = jnp.max(id_row(left[0])) == jnp.min(own_row)
    right_needed = jnp.min(id_row(right[0])) == jnp.max(own_row)

    @pl.when(left_needed)
    def _():
        absorb_side(left, own_row, queries_ref, wk_ref, wv_ref, state)

    @pl.when(right_needed)
    def _():
        absorb_side(right, own_row, queries_ref, wk_ref, wv_ref, state)


def located(refs, places):
    return [(refs[i], slot) for i, slot in places]


def absorb_stage(own, blocks, left, right, queries, w_qkv, state):
    count = len(blocks)

    def kernel(own_ref, *refs):
        block_refs, refs = refs[:count], refs[count:]
        queries_ref, wk_ref, wv_ref, old_tops, old_sums, old_acc, tops_ref, sums_ref, acc_ref = refs
        tops_ref[...] = old_tops[...]
        sums_ref[...] = old_sums[...]
        acc_ref[...] = old_acc[...]
        state_refs = (tops_ref, sums_ref, acc_ref)
        absorb_both(
            own_ref, located(block_refs, left), located(block_refs, right),
            queries_ref, wk_ref, wv_ref, state_refs,
        )

    return pl.pallas_call(
        kernel,
        grid=(QUADS,),
        in_specs=[packed_spec(own)]
        + [packed_spec(block) for block in blocks]
        + [QUERY_SPEC, weight_spec(1), weight_spec(2), *STATE_SPECS],
        out_specs=list(STATE_SPECS),
        out_shape=list(STATE_SHAPES),
        compiler_params=LIMIT,
        cost_estimate=cost(len(left) + len(right), 8),
        name="absorb_stage",
    )(own, *blocks, queries, w_qkv, w_qkv, *state)


def last_stage(own, blocks, left, right, queries, w_qkv, state, frames, w_out):
    count = len(blocks)

    def kernel(own_ref, *refs):
        block_refs, refs = refs[:count], refs[count:]
        queries_ref, wk_ref, wv_ref, old_tops, old_sums, old_acc = refs[:6]
        frames_ref, wout_ref, attended_ref, out_ref, tops_ref, sums_ref, acc_ref, total_ref = refs[6:]
        quad = pl.program_id(0)
        tops_ref[...] = old_tops[...]
        sums_ref[...] = old_sums[...]
        acc_ref[...] = old_acc[...]
        state_refs = (tops_ref, sums_ref, acc_ref)
        absorb_both(
            own_ref, located(block_refs, left), located(block_refs, right),
            queries_ref, wk_ref, wv_ref, state_refs,
        )
        for h in range(4):
            rows = slice(h * HALF, (h + 1) * HALF)
            attended_ref[rows, :] = (acc_ref[rows, :] / sums_ref[h : h + 1, :]).astype(BF16)
        term = jnp.dot(jnp.transpose(attended_ref[...]), wout_ref[...], preferred_element_type=F32)

        @pl.when(quad == 0)
        def _():
            total_ref[...] = frames_ref[...].astype(F32) + term

        @pl.when(quad > 0)
        def _():
            total_ref[...] += term

        @pl.when(quad == QUADS - 1)
        def _():
            out_ref[...] = total_ref[...].astype(BF16)

    return pl.pallas_call(
        kernel,
        grid=(QUADS,),
        in_specs=[packed_spec(own)]
        + [packed_spec(block) for block in blocks]
        + [QUERY_SPEC, weight_spec(1), weight_spec(2), *STATE_SPECS]
        + [
            pl.BlockSpec((ROWS, WIDTH), lambda j: (0, 0)),
            pl.BlockSpec((QUAD, WIDTH), lambda j: (j, 0)),
        ],
        out_specs=[
            pl.BlockSpec((QUAD, LANES), lambda j: (j, 0)),
            pl.BlockSpec((ROWS, WIDTH), lambda j: (0, 0)),
        ],
        out_shape=[
            jax.ShapeDtypeStruct((WIDTH, LANES), BF16),
            jax.ShapeDtypeStruct((ROWS, WIDTH), BF16),
        ],
        scratch_shapes=[
            pltpu.VMEM((8, LANES), F32),
            pltpu.VMEM((8, LANES), F32),
            pltpu.VMEM((QUAD, LANES), F32),
            pltpu.VMEM((ROWS, WIDTH), F32),
        ],
        compiler_params=LIMIT,
        cost_estimate=cost(len(left) + len(right) + 1, 10),
        name="last_stage",
    )(own, *blocks, queries, w_qkv, w_qkv, *state, frames, w_out)


def grad_kernel(attended_ref, cotangent_ref, out_ref):
    attended = jnp.concatenate([attended_ref[p] for p in range(CHUNKS)], axis=1)
    product = jnp.dot(attended, cotangent_ref[...], preferred_element_type=F32).astype(BF16)
    for half in range(2):
        out_ref[half] = product[:, half * LANES : (half + 1) * LANES]


def grad_product(attended, cotangent):
    return pl.pallas_call(
        grad_kernel,
        grid=(QUADS,),
        in_specs=[
            pl.BlockSpec((CHUNKS, LANES, ROWS), lambda j: (0, 0, 0)),
            pl.BlockSpec((CHUNKS * ROWS, QUAD), lambda j: (0, j)),
        ],
        out_specs=pl.BlockSpec((2, LANES, LANES), lambda j: (j, 0, 0)),
        out_shape=jax.ShapeDtypeStruct((CHUNKS, LANES, LANES), BF16),
        compiler_params=LIMIT,
        name="grad_product",
    )(attended, cotangent)


def gathered_over_dp(block):
    n_dp = lax.axis_size("dp")
    chips = n_dp // 2

    def turned(distance):
        route = [((2 * x + c), 2 * ((x + distance) % chips) + c) for x in range(chips) for c in range(2)]
        return lax.ppermute(block, "dp", route)

    ring = [block, turned(1), turned(2), turned(3)]
    mine = jnp.concatenate(ring, axis=0)
    theirs = lax.ppermute(mine, "dp", [(i, i ^ 1) for i in range(n_dp)])
    return mine, theirs


def local(frames, segment_ids, norm_gain, w_qkv, w_out, cotangent):
    n_dp = lax.axis_size("dp")
    n_seq = lax.axis_size("seq")
    frames = frames[0]
    own = normalize(frames, segment_ids, norm_gain[None, :])

    left1, right1 = shifted(own, 1), shifted(own, -1)
    queries, *state = own_block(own, w_qkv)
    trio = jnp.concatenate([left1, own, right1], axis=0)
    left_trio, right_trio = shifted(trio, 4), shifted(trio, -4)
    left2, right2 = shifted(left1, 1), shifted(right1, -1)
    state = absorb_stage(
        own, (left1, left2, right1, right2), ((0, 0), (1, 0)), ((2, 0), (3, 0)), queries, w_qkv, state
    )
    mine, theirs = gathered_over_dp(cotangent[0])

    left2, right2, left_trio, right_trio = lax.optimization_barrier(
        (left2, right2, left_trio, right_trio)
    )
    left6, right6 = shifted(left2, 4), shifted(right2, -4)
    state = absorb_stage(
        own, (left_trio, right_trio), ((0, 2), (0, 1), (0, 0)), ((1, 0), (1, 1), (1, 2)),
        queries, w_qkv, state,
    )
    attended, block_out = last_stage(
        own, (left6, right6), ((0, 0),), ((1, 0),), queries, w_qkv, state, frames, w_out
    )

    pieces = lax.all_to_all(attended, "dp", 0, 0, tiled=True).reshape(n_dp, LANES, ROWS)
    chip = lax.axis_index("dp") // 2
    core = lax.axis_index("dp") % 2
    chips = n_dp // 2
    order = [2 * ((chip - d) % chips) + core for d in range(chips)]
    order += [2 * ((chip - d) % chips) + 1 - core for d in range(chips)]
    pieces = jnp.take(pieces, jnp.stack(order), axis=0)
    share = grad_product(pieces, jnp.concatenate([mine, theirs], axis=0))
    rows = LANES * CHUNKS // n_seq
    parts = lax.all_to_all(share.reshape(n_seq, rows, LANES), "seq", 0, 0, tiled=True)
    grad_scale = (n_dp * n_seq * ROWS) ** (-0.5)
    block = jnp.sum(parts.astype(F32), axis=0) * grad_scale
    inner = n_seq // n_dp
    route = [
        (p * n_seq + q * inner + r, q * n_seq + p * inner + r)
        for p in range(n_dp)
        for q in range(n_dp)
        for r in range(inner)
    ]
    return (block_out[None], lax.ppermute(block, ("dp", "seq"), route))


def solution(mesh):
    placed = (P("dp", "seq", None), P("dp", "seq"), P(), P(), P(), P("dp", "seq", None))
    return jax.shard_map(
        local,
        mesh=mesh,
        in_specs=placed,
        out_specs=(P("dp", "seq", None), P("seq", "dp")),
        check_vma=False,
    )
```

time: 172 us -> 117 us (0.68)
  blocking collectives: 73.1 us -> 23.5 us
  between operations: 14.3 us -> 0.87 us
  waiting for transfers between devices: 12.8 us -> 20.2 us
  starting transfers between devices: 42 us -> 37.3 us
  local copies, waits for them, and re-layouts: 6.03 us -> 9.75 us
  other arithmetic: 0.05 us -> 2.26 us
    all_to_all x2 -> x1, blocking collectives: 73.1 us -> 23.5 us  [local(): lax.all_to_all(share.reshape(n_seq, rows, LANES), 'seq', 0, 0, tiled=True)]
    ppermute x12 -> x8, starting transfers between devices: 36.3 us -> 23.7 us  [shifted(): return lax.ppermute(block, 'seq', route)]
    ppermute x12 -> x8, waiting for transfers between devices: 5.79 us -> 10.8 us  [shifted(): return lax.ppermute(block, 'seq', route)]
    all_to_all x0 -> x1, starting transfers between devices: none -> 4.8 us  [local(): lax.all_to_all(attended, 'dp', 0, 0, tiled=True).reshape(n_dp, LANES, ROWS)]
    ppermute x0 -> x4, starting transfers between devices: none -> 3.14 us  [the longest x3 3.14 us: turned(): return lax.ppermute(block, 'dp', route)]
    all_to_all x0 -> x1, waiting for transfers between devices: none -> 3.05 us  [local(): lax.all_to_all(attended, 'dp', 0, 0, tiled=True).reshape(n_dp, LANES, ROWS)]
    concatenate x0 -> x2, other arithmetic: none -> 2.09 us  [the longest x1 2.03 us: gathered_over_dp(): mine = jnp.concatenate(ring, axis=0)]
    unnamed x15 -> x23, local copies, waits for them, and re-layouts: 6.03 us -> 7.67 us
  transfers between devices with their start and end apart: 14 -> 14, of which waited for: 2 -> 4; matrix products, arithmetic and copies ran while one was open for 0% -> 5% of each run, Pallas kernels for 12% -> 17%
where the time goes in v1:
time: 117 us; the launch traced here: 115 us
  starting transfers between devices  37.3 us (32%)
  blocking collectives  23.5 us (20%)
  Pallas kernels  21.7 us (19%)
  waiting for transfers between devices  20.2 us (17%)
  local copies, waits for them, and re-layouts  9.75 us (8%)
  other arithmetic  2.26 us (2%)
    ppermute x8, starting transfers between devices, shifted(): return lax.ppermute(block, 'seq', route)  23.7 us
    all_to_all x1, blocking collectives, local(): lax.all_to_all(share.reshape(n_seq, rows, LANES), 'seq', 0, 0, tiled=True)  23.5 us
    pallas_call x2, Pallas kernels, absorb_stage(): pl.pallas_call(kernel, grid=(QUADS,), in_specs=[packed_spec(own)] + [pack...  12.3 us
    ppermute x8, waiting for transfers between devices, shifted(): return lax.ppermute(block, 'seq', route)  10.8 us
    unnamed x23, local copies, waits for them, and re-layouts  7.67 us
    ppermute x1, waiting for transfers between devices, local(): return (block_out[None], lax.ppermute(block, ('dp', 'seq'), route))  6.3 us
    ppermute x1, starting transfers between devices, local(): return (block_out[None], lax.ppermute(block, ('dp', 'seq'), route))  5.64 us
    all_to_all x1, starting transfers between devices, local(): lax.all_to_all(attended, 'dp', 0, 0, tiled=True).reshape(n_dp, LANES, ROWS)  4.8 us
  transfers between devices with their start and end apart: 14, of which 4 were waited for; matrix products, arithmetic and copies ran while one was open for 5% of the time, Pallas kernels for 17%

profile of v1, /device:TPU:4, one launch (start us, length us, event | category | flops | bytes accessed | tf_op | source)
XLA Modules:
  0.0 115.5 jit_solution(479666943551474506)
XLA Ops:
  3.2 1.7 %collective-permute-start = (bf16[1040,128]{1,0:T(8,128)(2,1)S(1)}, bf16[1040,128]{1,0:T(8,128)(2,1)S(1)}, u32[]{:S(2)}, u32[]{:S(2)}) collective-permute-start(bf16[1040,128]{1,0:T(8,128)(2,1)S(1)} %layer_norm.1.own_ref), channel_id=1, source_target_pairs={{0,1},{1,2},{2,3},{3,4},{4,5},{5,6},{6,7},{7,8},{8,9},{9,10},{10,1... | collective-permute-start | bytes 798728 | tf_op jit(solution)/shard_map/ppermute | solution.py:27
  4.8 6.8 %collective-permute-start.2 = (bf16[1040,128]{1,0:T(8,128)(2,1)S(1)}, bf16[1040,128]{1,0:T(8,128)(2,1)S(1)}, u32[]{:S(2)}, u32[]{:S(2)}) collective-permute-start(bf16[1040,128]{1,0:T(8,128)(2,1)S(1)} %layer_norm.1.own_ref), channel_id=1, source_target_pairs={{0,31},{1,0},{2,1},{3,2},{4,3},{5,4},{6,5},{7,6},{8,7},{9,8},{10,9... | collective-permute-start | bytes 798728 | tf_op jit(solution)/shard_map/ppermute | solution.py:27
  11.7 1.2 %collective-permute-start.8 = (bf16[128,1024]{1,0:T(8,128)(2,1)}, bf16[128,1024]{1,0:T(8,128)(2,1)S(1)}, u32[]{:S(2)}, u32[]{:S(2)}) collective-permute-start(bf16[128,1024]{1,0:T(8,128)(2,1)} %bitcast.31), channel_id=1, source_target_pairs={{0,64},{32,96},{64,128},{96,160},{128,192},{160,224},{192,0},{224,... | collective-permute-start | bytes 786440 | tf_op jit(solution)/shard_map/ppermute | solution.py:307
  13.7 1.1 collective-permute-start.10
  15.0 1.0 constant_dynamic-update-slice_fusion.4
  16.0 2.0 %collective-permute-done.refs_0_ = bf16[1040,128]{1,0:T(8,128)(2,1)S(1)} collective-permute-done((bf16[1040,128]{1,0:T(8,128)(2,1)S(1)}, bf16[1040,128]{1,0:T(8,128)(2,1)S(1)}, u32[]{:S(2)}, u32[]{:S(2)}) %collective-permute-start) | collective-permute-done | bytes 266272 | tf_op jit(solution)/shard_map/ppermute | solution.py:27
  18.1 3.2 %collective-permute-start.5 = (bf16[3120,128]{1,0:T(8,128)(2,1)S(1)}, bf16[3120,128]{1,0:T(8,128)(2,1)S(1)}, u32[]{:S(2)}, u32[]{:S(2)}) collective-permute-start(bf16[3120,128]{1,0:T(8,128)(2,1)S(1)} %pad_maximum_fusion.1), channel_id=1, source_target_pairs={{0,28},{1,29},{2,30},{3,31},{4,0},{5,1},{6,2},{7,3},{8,4},{9,5},{1... | collective-permute-start | bytes 2396168 | tf_op jit(solution)/shard_map/ppermute | solution.py:27
  21.3 2.8 %copy-done = bf16[1024,3072]{1,0:T(8,128)(2,1)S(1)} copy-done((bf16[1024,3072]{1,0:T(8,128)(2,1)S(1)}, bf16[1024,3072]{1,0:T(8,128)(2,1)}, u32[]{:S(2)}) %copy-start) | copy-done | bytes 6291480
  24.1 4.5 %own_block.1 = (bf16[8,256,128]{2,1,0:T(8,128)(2,1)S(1)}, f32[4,8,128]{2,1,0:T(8,128)S(1)}, f32[4,8,128]{2,1,0:T(8,128)S(1)}, f32[1024,128]{1,0:T(8,128)S(1)}) custom-call(bf16[1040,128]{1,0:T(8,128)(2,1)S(1)} %layer_norm.1.own_ref, bf16[1024,3072]{1,0:T(8,128)(2,1)S(1)} %copy-done, bf16[1024,3072]{1,0:T(8,128)(2,1)S(1)} %copy-done, ...), custom_call_target="tpu_custom_call" | custom-call | flops 1610612736 | bytes 8388608 | tf_op jit(solution)/shard_map/own_block/pallas_call | solution.py:149
  28.7 2.0 %pad_maximum_fusion = bf16[512,1024]{1,0:T(8,128)(2,1)} fusion(bf16[128,1024]{1,0:T(8,128)(2,1)S(1)} %collective-permute-done.10, bf16[128,1024]{1,0:T(8,128)(2,1)} %collective-permute-done.9, bf16[128,1024]{1,0:T(8,128)(2,1)S(1)} %collective-permute-done.8, bf16[128,1024]{1,0:T(8,128)(2,1)S(1)} %bitcast.34), kind=kLoop, calls=%fused_computation.1 | loop fusion | flops 4194304 | bytes 2097152 | tf_op jit(solution)/shard_map/concatenate | solution.py:310
  30.7 5.3 %collective-permute-start.3 = (bf16[1040,128]{1,0:T(8,128)(2,1)S(1)}, bf16[1040,128]{1,0:T(8,128)(2,1)S(1)}, u32[]{:S(2)}, u32[]{:S(2)}) collective-permute-start(bf16[1040,128]{1,0:T(8,128)(2,1)S(1)} %collective-permute-done.2.refs_2_), channel_id=1, source_target_pairs={{0,31},{1,0},{2,1},{3,2},{4,3},{5,4},{6,5},{7,6},{8,7},{9,8},{10,9... | collective-permute-start | bytes 798728 | tf_op jit(solution)/shard_map/ppermute | solution.py:27
  37.1 8.8 %collective-permute-done.1.refs_1_ = bf16[1040,128]{1,0:T(8,128)(2,1)S(1)} collective-permute-done((bf16[1040,128]{1,0:T(8,128)(2,1)S(1)}, bf16[1040,128]{1,0:T(8,128)(2,1)S(1)}, u32[]{:S(2)}, u32[]{:S(2)}) %collective-permute-start.1) | collective-permute-done | bytes 266272 | tf_op jit(solution)/shard_map/ppermute | solution.py:27
  45.9 5.7 %absorb_stage.2 = (f32[4,8,128]{2,1,0:T(8,128)S(1)}, f32[4,8,128]{2,1,0:T(8,128)S(1)}, f32[1024,128]{1,0:T(8,128)S(1)}) custom-call(bf16[1040,128]{1,0:T(8,128)(2,1)S(1)} %layer_norm.1.own_ref, bf16[1040,128]{1,0:T(8,128)(2,1)S(1)} %collective-permute-done.refs_0_, bf16[1040,128]{1,0:T(8,128)(2,1)S(1)} %collective-permute-done.1.refs_1_, ...), custom_call_target="tpu_custom_call" | custom-call | flops 2147483648 | bytes 8388608 | tf_op jit(solution)/shard_map/absorb_stage/pallas_call | solution.py:202
  51.6 2.0 %collective-permute-start.6 = (bf16[1040,128]{1,0:T(8,128)(2,1)S(1)}, bf16[1040,128]{1,0:T(8,128)(2,1)S(1)}, u32[]{:S(2)}, u32[]{:S(2)}) collective-permute-start(bf16[1040,128]{1,0:T(8,128)(2,1)S(1)} %collective-permute-done.1.refs_1_), channel_id=1, source_target_pairs={{0,4},{1,5},{2,6},{3,7},{4,8},{5,9},{6,10},{7,11},{8,12},{9,13},{1... | collective-permute-start | bytes 798728 | tf_op jit(solution)/shard_map/ppermute | solution.py:27
  53.6 4.5 %collective-permute-start.7 = (bf16[1040,128]{1,0:T(8,128)(2,1)S(1)}, bf16[1040,128]{1,0:T(8,128)(2,1)S(1)}, u32[]{:S(2)}, u32[]{:S(2)}) collective-permute-start(bf16[1040,128]{1,0:T(8,128)(2,1)S(1)} %collective-permute-done.3.refs_3_), channel_id=1, source_target_pairs={{0,28},{1,29},{2,30},{3,31},{4,0},{5,1},{6,2},{7,3},{8,4},{9,5},{1... | collective-permute-start | bytes 798728 | tf_op jit(solution)/shard_map/ppermute | solution.py:27
  58.1 6.7 %absorb_stage.3 = (f32[4,8,128]{2,1,0:T(8,128)S(1)}, f32[4,8,128]{2,1,0:T(8,128)S(1)}, f32[1024,128]{1,0:T(8,128)S(1)}) custom-call(bf16[1040,128]{1,0:T(8,128)(2,1)S(1)} %layer_norm.1.own_ref, bf16[3120,128]{1,0:T(8,128)(2,1)S(1)} %collective-permute-done.4.refs_0_, bf16[3120,128]{1,0:T(8,128)(2,1)S(1)} %collective-permute-done.5.refs_1_, ...), custom_call_target="tpu_custom_call" | custom-call | flops 3221225472 | bytes 8388608 | tf_op jit(solution)/shard_map/absorb_stage/pallas_call | solution.py:202
  64.9 3.3 %last_stage.1 = (bf16[1024,128]{1,0:T(8,128)(2,1)}, bf16[128,1024]{1,0:T(8,128)(2,1)}) custom-call(bf16[1040,128]{1,0:T(8,128)(2,1)S(1)} %layer_norm.1.own_ref, bf16[1040,128]{1,0:T(8,128)(2,1)S(1)} %collective-permute-done.6.refs_0_, bf16[1040,128]{1,0:T(8,128)(2,1)S(1)} %collective-permute-done.7.refs_1_, ...), custom_call_target="tpu_custom_call" | custom-call | flops 1610612736 | bytes 10485760 | tf_op jit(solution)/shard_map/last_stage/pallas_call | solution.py:249
  68.2 4.8 %all-to-all-start = ((bf16[8,128,128]{2,1,0:T(8,128)(2,1)}), bf16[8,128,128]{2,1,0:T(8,128)(2,1)S(1)}, u32[]{:S(2)}, u32[]{:S(2)}) async-start(bf16[8,128,128]{2,1,0:T(8,128)(2,1)} %bitcast.11), calls=%async_computation | async-start | bytes 524288 | tf_op jit(solution)/shard_map/all_to_all | solution.py:343
  73.0 1.3 %constant_dynamic-update-slice_fusion.cotangent_ref = bf16[1024,1024]{1,0:T(8,128)(2,1)S(1)} fusion(bf16[1024,1024]{1,0:T(8,128)(2,1)S(1)} %constant_dynamic-update-slice_fusion.1, bf16[512,1024]{1,0:T(8,128)(2,1)} %collective-permute-done.11), kind=kLoop, calls=%fused_computation.5 | loop fusion | bytes 2097152 | tf_op jit(solution)/shard_map/concatenate | solution.py:350
  74.3 3.1 %all-to-all-done = bf16[8,128,128]{2,1,0:T(8,128)(2,1)S(1)} async-done(((bf16[8,128,128]{2,1,0:T(8,128)(2,1)}), bf16[8,128,128]{2,1,0:T(8,128)(2,1)S(1)}, u32[]{:S(2)}, u32[]{:S(2)}) %all-to-all-start) | async-done | bytes 262176 | tf_op jit(solution)/shard_map/all_to_all | solution.py:343
  78.1 1.3 %grad_product.1 = bf16[8,128,128]{2,1,0:T(8,128)(2,1)S(1)} custom-call(bf16[8,128,128]{2,1,0:T(8,128)(2,1)S(1)} %broadcast_select_fusion.attended_ref, bf16[1024,1024]{1,0:T(8,128)(2,1)S(1)} %constant_dynamic-update-slice_fusion.cotangent_ref), custom_call_target="tpu_custom_call" | custom-call | tf_op jit(solution)/shard_map/grad_product/pallas_call | solution.py:287
  79.4 23.5 %all_to_all.14 = bf16[32,32,128]{2,1,0:T(8,128)(2,1)S(1)} all-to-all(bf16[32,32,128]{2,1,0:T(8,128)(2,1)S(1)} %bitcast.29), channel_id=1, replica_groups=mesh['dp'=8,'seq'=32] {'seq'}, dimensions={0} | all-to-all | bytes 524288 | tf_op jit(solution)/shard_map/all_to_all | solution.py:352
  102.9 5.6 %collective-permute-start.12 = (f32[32,128]{1,0:T(8,128)S(1)}, f32[32,128]{1,0:T(8,128)S(1)}, u32[]{:S(2)}, u32[]{:S(2)}) collective-permute-start(f32[32,128]{1,0:T(8,128)S(1)} %broadcast_multiply_fusion), channel_id=1, source_target_pairs={{0,0},{1,1},{2,2},{3,3},{4,32},{5,33},{6,34},{7,35},{8,64},{9,65},... | collective-permute-start | bytes 49160 | tf_op jit(solution)/shard_map/ppermute | solution.py:362
  108.6 6.3 %collective-permute-done.12 = f32[32,128]{1,0:T(8,128)S(1)} collective-permute-done((f32[32,128]{1,0:T(8,128)S(1)}, f32[32,128]{1,0:T(8,128)S(1)}, u32[]{:S(2)}, u32[]{:S(2)}) %collective-permute-start.12) | collective-permute-done | bytes 16416 | tf_op jit(solution)/shard_map/ppermute | solution.py:362
  (47 shorter events, 6.1 us)
Async XLA Ops:
  0.6 1.0 copy-start.2
  1.6 0.7 copy-start.4
  2.3 0.7 copy-start.5
  3.2 14.8 %collective-permute-start = (bf16[1040,128]{1,0:T(8,128)(2,1)S(1)}, bf16[1040,128]{1,0:T(8,128)(2,1)S(1)}, u32[]{:S(2)}, u32[]{:S(2)}) collective-permute-start(bf16[1040,128]{1,0:T(8,128)(2,1)S(1)} %layer_norm.1.own_ref), channel_id=1, source_target_pairs={{0,1},{1,2},{2,3},{3,4},{4,5},{5,6},{6,7},{7,8},{8,9},{9,10},{10,1... | collective-permute-start | bytes 798728 | tf_op jit(solution)/shard_map/ppermute | solution.py:27
  4.8 13.1 %collective-permute-start.2 = (bf16[1040,128]{1,0:T(8,128)(2,1)S(1)}, bf16[1040,128]{1,0:T(8,128)(2,1)S(1)}, u32[]{:S(2)}, u32[]{:S(2)}) collective-permute-start(bf16[1040,128]{1,0:T(8,128)(2,1)S(1)} %layer_norm.1.own_ref), channel_id=1, source_target_pairs={{0,31},{1,0},{2,1},{3,2},{4,3},{5,4},{6,5},{7,6},{8,7},{9,8},{10,9... | collective-permute-start | bytes 798728 | tf_op jit(solution)/shard_map/ppermute | solution.py:27
  11.7 17.0 %collective-permute-start.8 = (bf16[128,1024]{1,0:T(8,128)(2,1)}, bf16[128,1024]{1,0:T(8,128)(2,1)S(1)}, u32[]{:S(2)}, u32[]{:S(2)}) collective-permute-start(bf16[128,1024]{1,0:T(8,128)(2,1)} %bitcast.31), channel_id=1, source_target_pairs={{0,64},{32,96},{64,128},{96,160},{128,192},{160,224},{192,0},{224,... | collective-permute-start | bytes 786440 | tf_op jit(solution)/shard_map/ppermute | solution.py:307
  12.9 15.8 %collective-permute-start.9 = (bf16[128,1024]{1,0:T(8,128)(2,1)}, bf16[128,1024]{1,0:T(8,128)(2,1)}, u32[]{:S(2)}, u32[]{:S(2)}) collective-permute-start(bf16[128,1024]{1,0:T(8,128)(2,1)} %bitcast.32), channel_id=1, source_target_pairs={{0,128},{32,160},{64,192},{96,224},{128,0},{160,32},{192,64},{224,... | collective-permute-start | bytes 786440 | tf_op jit(solution)/shard_map/ppermute | solution.py:307
  13.7 15.0 %collective-permute-start.10 = (bf16[128,1024]{1,0:T(8,128)(2,1)}, bf16[128,1024]{1,0:T(8,128)(2,1)S(1)}, u32[]{:S(2)}, u32[]{:S(2)}) collective-permute-start(bf16[128,1024]{1,0:T(8,128)(2,1)} %bitcast.33), channel_id=1, source_target_pairs={{0,192},{32,224},{64,0},{96,32},{128,64},{160,96},{192,128},{224,1... | collective-permute-start | bytes 786440 | tf_op jit(solution)/shard_map/ppermute | solution.py:307
  18.0 10.7 %copy-start.6 = (bf16[1,128,1024]{2,1,0:T(8,128)(2,1)S(1)}, bf16[1,128,1024]{2,1,0:T(8,128)(2,1)}, u32[]{:S(2)}) copy-start(bf16[1,128,1024]{2,1,0:T(8,128)(2,1)} %param.11) | copy-start | bytes 786436
  18.0 33.5 %collective-permute-start.4 = (bf16[3120,128]{1,0:T(8,128)(2,1)S(1)}, bf16[3120,128]{1,0:T(8,128)(2,1)S(1)}, u32[]{:S(2)}, u32[]{:S(2)}) collective-permute-start(bf16[3120,128]{1,0:T(8,128)(2,1)S(1)} %pad_maximum_fusion.1), channel_id=1, source_target_pairs={{0,4},{1,5},{2,6},{3,7},{4,8},{5,9},{6,10},{7,11},{8,12},{9,13},{1... | collective-permute-start | bytes 2396168 | tf_op jit(solution)/shard_map/ppermute | solution.py:27
  18.1 33.4 %collective-permute-start.5 = (bf16[3120,128]{1,0:T(8,128)(2,1)S(1)}, bf16[3120,128]{1,0:T(8,128)(2,1)S(1)}, u32[]{:S(2)}, u32[]{:S(2)}) collective-permute-start(bf16[3120,128]{1,0:T(8,128)(2,1)S(1)} %pad_maximum_fusion.1), channel_id=1, source_target_pairs={{0,28},{1,29},{2,30},{3,31},{4,0},{5,1},{6,2},{7,3},{8,4},{9,5},{1... | collective-permute-start | bytes 2396168 | tf_op jit(solution)/shard_map/ppermute | solution.py:27
  21.3 2.8 %copy-start = (bf16[1024,3072]{1,0:T(8,128)(2,1)S(1)}, bf16[1024,3072]{1,0:T(8,128)(2,1)}, u32[]{:S(2)}) copy-start(bf16[1024,3072]{1,0:T(8,128)(2,1)} %refs_4_.3) | copy-start | bytes 18874372
  30.7 42.3 %collective-permute-start.11 = (bf16[512,1024]{1,0:T(8,128)(2,1)}, bf16[512,1024]{1,0:T(8,128)(2,1)}, u32[]{:S(2)}, u32[]{:S(2)}) collective-permute-start(bf16[512,1024]{1,0:T(8,128)(2,1)} %pad_maximum_fusion), channel_id=1, source_target_pairs={{0,32},{32,0},{64,96},{96,64},{128,160},{160,128},{192,224},{224,1... | collective-permute-start | bytes 3145736 | tf_op jit(solution)/shard_map/ppermute | solution.py:311
  30.7 15.2 %collective-permute-start.1 = (bf16[1040,128]{1,0:T(8,128)(2,1)S(1)}, bf16[1040,128]{1,0:T(8,128)(2,1)S(1)}, u32[]{:S(2)}, u32[]{:S(2)}) collective-permute-start(bf16[1040,128]{1,0:T(8,128)(2,1)S(1)} %collective-permute-done.refs_0_), channel_id=1, source_target_pairs={{0,1},{1,2},{2,3},{3,4},{4,5},{5,6},{6,7},{7,8},{8,9},{9,10},{10,1... | collective-permute-start | bytes 798728 | tf_op jit(solution)/shard_map/ppermute | solution.py:27
  30.7 15.2 %collective-permute-start.3 = (bf16[1040,128]{1,0:T(8,128)(2,1)S(1)}, bf16[1040,128]{1,0:T(8,128)(2,1)S(1)}, u32[]{:S(2)}, u32[]{:S(2)}) collective-permute-start(bf16[1040,128]{1,0:T(8,128)(2,1)S(1)} %collective-permute-done.2.refs_2_), channel_id=1, source_target_pairs={{0,31},{1,0},{2,1},{3,2},{4,3},{5,4},{6,5},{7,6},{8,7},{9,8},{10,9... | collective-permute-start | bytes 798728 | tf_op jit(solution)/shard_map/ppermute | solution.py:27
  51.6 13.3 %collective-permute-start.6 = (bf16[1040,128]{1,0:T(8,128)(2,1)S(1)}, bf16[1040,128]{1,0:T(8,128)(2,1)S(1)}, u32[]{:S(2)}, u32[]{:S(2)}) collective-permute-start(bf16[1040,128]{1,0:T(8,128)(2,1)S(1)} %collective-permute-done.1.refs_1_), channel_id=1, source_target_pairs={{0,4},{1,5},{2,6},{3,7},{4,8},{5,9},{6,10},{7,11},{8,12},{9,13},{1... | collective-permute-start | bytes 798728 | tf_op jit(solution)/shard_map/ppermute | solution.py:27
  53.6 11.2 %collective-permute-start.7 = (bf16[1040,128]{1,0:T(8,128)(2,1)S(1)}, bf16[1040,128]{1,0:T(8,128)(2,1)S(1)}, u32[]{:S(2)}, u32[]{:S(2)}) collective-permute-start(bf16[1040,128]{1,0:T(8,128)(2,1)S(1)} %collective-permute-done.3.refs_3_), channel_id=1, source_target_pairs={{0,28},{1,29},{2,30},{3,31},{4,0},{5,1},{6,2},{7,3},{8,4},{9,5},{1... | collective-permute-start | bytes 798728 | tf_op jit(solution)/shard_map/ppermute | solution.py:27
  58.1 6.7 %slice-start = ((s8[6291456]{0:T(1024)(128)(4,1)}), s8[4194304]{0:T(1024)(128)(4,1)S(1)}, s32[]{:S(2)}) async-start(s8[6291456]{0:T(1024)(128)(4,1)} %bitcast.25), calls=%async_computation.2 | async-start | bytes 8388608
  58.1 6.7 %slice-start.1 = ((s8[6291456]{0:T(1024)(128)(4,1)}), s8[2097152]{0:T(1024)(128)(4,1)S(1)}, s32[]{:S(2)}) async-start(s8[6291456]{0:T(1024)(128)(4,1)} %bitcast.25), calls=%async_computation.3 | async-start | bytes 4194304
  58.1 6.7 %copy-start.1 = (bf16[1024,1024]{1,0:T(8,128)(2,1)S(1)}, bf16[1024,1024]{1,0:T(8,128)(2,1)}, u32[]{:S(2)}) copy-start(bf16[1024,1024]{1,0:T(8,128)(2,1)} %refs_9_.1) | copy-start | bytes 6291460
  58.1 6.7 %copy-start.3 = (bf16[1,128,1024]{2,1,0:T(8,128)(2,1)S(1)}, bf16[1,128,1024]{2,1,0:T(8,128)(2,1)}, u32[]{:S(2)}) copy-start(bf16[1,128,1024]{2,1,0:T(8,128)(2,1)} %param.6) | copy-start | bytes 786436
  68.2 9.2 %all-to-all-start = ((bf16[8,128,128]{2,1,0:T(8,128)(2,1)}), bf16[8,128,128]{2,1,0:T(8,128)(2,1)S(1)}, u32[]{:S(2)}, u32[]{:S(2)}) async-start(bf16[8,128,128]{2,1,0:T(8,128)(2,1)} %bitcast.11), calls=%async_computation | async-start | bytes 524288 | tf_op jit(solution)/shard_map/all_to_all | solution.py:343
  102.9 11.9 %collective-permute-start.12 = (f32[32,128]{1,0:T(8,128)S(1)}, f32[32,128]{1,0:T(8,128)S(1)}, u32[]{:S(2)}, u32[]{:S(2)}) collective-permute-start(f32[32,128]{1,0:T(8,128)S(1)} %broadcast_multiply_fusion), channel_id=1, source_target_pairs={{0,0},{1,1},{2,2},{3,3},{4,32},{5,33},{6,34},{7,35},{8,64},{9,65},... | collective-permute-start | bytes 49160 | tf_op jit(solution)/shard_map/ppermute | solution.py:362

commit v2 on v1

v2 whole, which is shorter than its diff:
```python
import jax
import jax.numpy as jnp
from jax import lax
from jax.experimental import pallas as pl
from jax.experimental.pallas import tpu as pltpu
from jax.sharding import PartitionSpec as P

ROWS = 128
LANES = 128
HALF = 64
WIDTH = 1024
CHUNKS = WIDTH // LANES
PACKED = WIDTH + 16
QUAD = 256
QUADS = WIDTH // QUAD
NEG_BIG = -1e30
EPSILON = 1e-05
LOG2E = 1.4426950408889634
AHEAD = 2
F32 = jnp.float32
BF16 = jnp.bfloat16
LIMIT = pltpu.CompilerParams(vmem_limit_bytes=40 * 1024 * 1024)


def shifted(block, distance):
    n_seq = lax.axis_size("seq")
    route = [(i, (i + distance) % n_seq) for i in range(n_seq)]
    return lax.ppermute(block, "seq", route)


def norm_kernel(frames_ref, ids_ref, gain_ref, packed_ref):
    float_frames = frames_ref[...].astype(F32)
    average = jnp.mean(float_frames, axis=-1, keepdims=True)
    centered = float_frames - average
    variance = jnp.mean(centered * centered, axis=-1, keepdims=True)
    normed = (centered * lax.rsqrt(variance + EPSILON) * gain_ref[...]).astype(BF16)
    for c in range(CHUNKS):
        packed_ref[c * ROWS : (c + 1) * ROWS, :] = normed[:, c * LANES : (c + 1) * LANES]
    ids = (ids_ref[...] + 1).astype(F32)
    packed_ref[WIDTH:PACKED, :] = jnp.broadcast_to(ids, (16, LANES)).astype(BF16)


def normalize(frames, ids, gain):
    return pl.pallas_call(
        norm_kernel,
        out_shape=jax.ShapeDtypeStruct((PACKED, LANES), BF16),
        compiler_params=pltpu.CompilerParams(vmem_limit_bytes=60 * 1024 * 1024),
        name="layer_norm",
    )(frames, ids, gain)


def unpacked(block):
    ref, slot = block
    base = slot * PACKED
    chunks = [ref[base + c * ROWS : base + (c + 1) * ROWS, :] for c in range(CHUNKS)]
    return jnp.concatenate(chunks, axis=1)


def id_row(block):
    ref, slot = block
    base = slot * PACKED + WIDTH
    return ref[base : base + 16, :].astype(F32)[0:1, :]


def id_column(row):
    across = lax.broadcasted_iota(jnp.int32, (ROWS, LANES), 1)
    down = lax.broadcasted_iota(jnp.int32, (ROWS, LANES), 0)
    return jnp.sum(jnp.where(across == down, row, 0.0), axis=1, keepdims=True)


def projected(frames, weight_ref, section, quad):
    at = section * WIDTH + quad * QUAD
    block = weight_ref[:, at : at + QUAD]
    return jnp.dot(frames, block, preferred_element_type=F32).astype(BF16)


def absorb(frames, bias, queries_ref, weight_ref, state, first):
    tops_ref, sums_ref, acc_ref = state
    both = jnp.concatenate([bias, bias], axis=1)
    pairs = 2 * QUADS
    keys, flipped, waiting = {}, {}, []

    def score(index):
        quad, at = index // 2, (index % 2) * LANES
        if quad not in keys:
            keys[quad] = projected(frames, weight_ref, 1, quad)
            flipped[quad] = jnp.transpose(projected(frames, weight_ref, 2, quad))
        part = keys[quad][:, at : at + LANES]
        return jnp.dot(part, queries_ref[index], preferred_element_type=F32) + both

    for index in range(pairs + AHEAD):
        if index < pairs:
            waiting.append(score(index))
        if index < AHEAD:
            continue
        pair = index - AHEAD
        heads = (2 * pair, 2 * pair + 1)
        scores = waiting[pair]
        waiting[pair] = None
        top = jnp.max(scores, axis=0, keepdims=True)
        if not first:
            old_top = jnp.concatenate([tops_ref[h : h + 1, :] for h in heads], axis=1)
            old_sum = jnp.concatenate([sums_ref[h : h + 1, :] for h in heads], axis=1)
            top = jnp.maximum(old_top, top)
            rescale = jnp.exp2((old_top - top) * LOG2E)
        weights = jnp.exp2((scores - top) * LOG2E)
        total = jnp.sum(weights, axis=0, keepdims=True)
        at = (pair % 2) * LANES
        values = flipped[pair // 2][at : at + LANES, :]
        mixed = jnp.dot(values, weights.astype(BF16), preferred_element_type=F32)
        if not first:
            total = old_sum * rescale + total
        for k, h in enumerate(heads):
            lanes = slice(k * LANES, (k + 1) * LANES)
            rows = slice(h * HALF, (h + 1) * HALF)
            term = mixed[k * HALF : (k + 1) * HALF, lanes]
            if not first:
                term = acc_ref[rows, :] * rescale[:, lanes] + term
            acc_ref[rows, :] = term
            tops_ref[h : h + 1, :] = top[:, lanes]
            sums_ref[h : h + 1, :] = total[:, lanes]


def bias_of(blocks, own_row):
    columns = jnp.concatenate([id_column(id_row(block)) for block in blocks], axis=0)
    return jnp.where(columns == own_row, 0.0, NEG_BIG)


def own_kernel(own_ref, weight_ref, queries_ref, *state):
    frames = unpacked((own_ref, 0))
    row = id_row((own_ref, 0))
    for quad in range(QUADS):
        queries = projected(frames, weight_ref, 0, quad) * jnp.asarray(0.125, BF16)
        flipped = jnp.transpose(queries)
        zeros = jnp.zeros((HALF, ROWS), BF16)
        for pair in range(2):
            index = 2 * quad + pair
            at = pair * LANES
            queries_ref[index, 0:HALF, 0:ROWS] = flipped[at : at + HALF, :]
            queries_ref[index, 0:HALF, ROWS:] = zeros
            queries_ref[index, HALF:, 0:ROWS] = zeros
            queries_ref[index, HALF:, ROWS:] = flipped[at + HALF : at + LANES, :]
    absorb(frames, bias_of(((own_ref, 0),), row), queries_ref, weight_ref, state, True)


STATE_SHAPES = (
    jax.ShapeDtypeStruct((2 * CHUNKS, LANES), F32),
    jax.ShapeDtypeStruct((2 * CHUNKS, LANES), F32),
    jax.ShapeDtypeStruct((WIDTH, LANES), F32),
)


def cost(blocks, mib):
    return pl.CostEstimate(
        flops=2 * blocks * ROWS * WIDTH * 2 * WIDTH, bytes_accessed=mib << 20, transcendentals=0
    )


def own_block(own, w_qkv):
    return pl.pallas_call(
        own_kernel,
        out_shape=[jax.ShapeDtypeStruct((CHUNKS, LANES, 2 * ROWS), BF16), *STATE_SHAPES],
        compiler_params=LIMIT,
        cost_estimate=cost(3, 8),
        name="own_block",
    )(own, w_qkv)


def absorb_both(own_ref, left, right, queries_ref, weight_ref, state):
    own_row = id_row((own_ref, 0))
    left_needed = jnp.max(id_row(left[0])) == jnp.min(own_row)
    right_needed = jnp.min(id_row(right[0])) == jnp.max(own_row)

    @pl.when(left_needed | right_needed)
    def _():
        blocks = (*left, *right)
        frames = jnp.concatenate([unpacked(block) for block in blocks], axis=0)
        absorb(frames, bias_of(blocks, own_row), queries_ref, weight_ref, state, False)


def located(refs, places):
    return [(refs[i], slot) for i, slot in places]


def copied(old_state, state):
    for old, new in zip(old_state, state):
        new[...] = old[...]


def absorb_stage(own, blocks, left, right, queries, w_qkv, state):
    count = len(blocks)

    def kernel(own_ref, *refs):
        block_refs, refs = refs[:count], refs[count:]
        queries_ref, weight_ref = refs[:2]
        copied(refs[2:5], refs[5:8])
        absorb_both(
            own_ref, located(block_refs, left), located(block_refs, right), queries_ref, weight_ref, refs[5:8]
        )

    return pl.pallas_call(
        kernel,
        out_shape=list(STATE_SHAPES),
        compiler_params=LIMIT,
        cost_estimate=cost(len(left) + len(right), 8),
        name="absorb_stage",
    )(own, *blocks, queries, w_qkv, *state)


def last_stage(own, blocks, left, right, queries, w_qkv, state, frames, w_out):
    count = len(blocks)

    def kernel(own_ref, *refs):
        block_refs, refs = refs[:count], refs[count:]
        queries_ref, weight_ref = refs[:2]
        frames_ref, wout_ref, attended_ref, out_ref = refs[5:9]
        state_refs = refs[9:12]
        copied(refs[2:5], state_refs)
        absorb_both(
            own_ref, located(block_refs, left), located(block_refs, right), queries_ref, weight_ref, state_refs
        )
        _, sums_ref, acc_ref = state_refs
        for h in range(2 * CHUNKS):
            rows = slice(h * HALF, (h + 1) * HALF)
            attended_ref[rows, :] = (acc_ref[rows, :] / sums_ref[h : h + 1, :]).astype(BF16)
        attended = jnp.concatenate(
            [jnp.transpose(attended_ref[c * LANES : (c + 1) * LANES, :]) for c in range(CHUNKS)], axis=1
        )
        product = jnp.dot(attended, wout_ref[...], preferred_element_type=F32)
        out_ref[...] = (frames_ref[...].astype(F32) + product).astype(BF16)

    return pl.pallas_call(
        kernel,
        out_shape=[
            jax.ShapeDtypeStruct((WIDTH, LANES), BF16),
            jax.ShapeDtypeStruct((ROWS, WIDTH), BF16),
        ],
        scratch_shapes=[pltpu.VMEM(shape.shape, F32) for shape in STATE_SHAPES],
        compiler_params=LIMIT,
        cost_estimate=cost(len(left) + len(right) + 1, 10),
        name="last_stage",
    )(own, *blocks, queries, w_qkv, *state, frames, w_out)


def grad_kernel(attended_ref, cotangent_ref, out_ref):
    attended = jnp.concatenate([attended_ref[p] for p in range(CHUNKS)], axis=1)
    product = jnp.dot(attended, cotangent_ref[...], preferred_element_type=F32).astype(BF16)
    for half in range(2):
        out_ref[half] = product[:, half * LANES : (half + 1) * LANES]


def grad_product(attended, cotangent):
    return pl.pallas_call(
        grad_kernel,
        grid=(QUADS,),
        in_specs=[
            pl.BlockSpec((CHUNKS, LANES, ROWS), lambda j: (0, 0, 0)),
            pl.BlockSpec((CHUNKS * ROWS, QUAD), lambda j: (0, j)),
        ],
        out_specs=pl.BlockSpec((2, LANES, LANES), lambda j: (j, 0, 0)),
        out_shape=jax.ShapeDtypeStruct((CHUNKS, LANES, LANES), BF16),
        compiler_params=LIMIT,
        name="grad_product",
    )(attended, cotangent)


def local(frames, segment_ids, norm_gain, w_qkv, w_out, cotangent):
    n_dp = lax.axis_size("dp")
    n_seq = lax.axis_size("seq")
    frames = frames[0]
    own = normalize(frames, segment_ids, norm_gain[None, :])

    left1, right1 = shifted(own, 1), shifted(own, -1)
    left4, right4 = shifted(own, 4), shifted(own, -4)
    queries, *state = own_block(own, w_qkv)
    left1, right1, left4, right4, queries = lax.optimization_barrier(
        (left1, right1, left4, right4, queries)
    )
    near = jnp.concatenate([left1, right1], axis=0)
    left_two, right_two = shifted(near, 4), shifted(near, -4)
    left2, right2 = shifted(left1, 1), shifted(right1, -1)
    cotangent, near = lax.optimization_barrier((cotangent, near))
    copies = jnp.broadcast_to(cotangent, (n_dp, *cotangent.shape[1:]))
    all_grads = lax.all_to_all(copies, "dp", 0, 0, tiled=True).reshape(n_dp * ROWS, WIDTH)

    state = absorb_stage(
        own, (left1, left4, right1, right4), ((0, 0), (1, 0)), ((2, 0), (3, 0)), queries, w_qkv, state
    )
    state = absorb_stage(own, (left2, right2), ((0, 0),), ((1, 0),), queries, w_qkv, state)
    left2, right2, left_two, right_two = lax.optimization_barrier((left2, right2, left_two, right_two))
    left6, right6 = shifted(left2, 4), shifted(right2, -4)
    state = absorb_stage(
        own, (left_two, right_two), ((0, 1), (0, 0)), ((1, 0), (1, 1)), queries, w_qkv, state
    )
    attended, block_out = last_stage(
        own, (left6, right6), ((0, 0),), ((1, 0),), queries, w_qkv, state, frames, w_out
    )

    pieces = lax.all_to_all(attended, "dp", 0, 0, tiled=True).reshape(n_dp, LANES, ROWS)
    share = grad_product(pieces, all_grads)
    rows = LANES * CHUNKS // n_seq
    parts = lax.all_to_all(share.reshape(n_seq, rows, LANES), "seq", 0, 0, tiled=True)
    grad_scale = (n_dp * n_seq * ROWS) ** (-0.5)
    block = jnp.sum(parts.astype(F32), axis=0) * grad_scale
    inner = n_seq // n_dp
    route = [
        (p * n_seq + q * inner + r, q * n_seq + p * inner + r)
        for p in range(n_dp)
        for q in range(n_dp)
        for r in range(inner)
    ]
    return (block_out[None], lax.ppermute(block, ("dp", "seq"), route))


def solution(mesh):
    placed = (P("dp", "seq", None), P("dp", "seq"), P(), P(), P(), P("dp", "seq", None))
    return jax.shard_map(
        local,
        mesh=mesh,
        in_specs=placed,
        out_specs=(P("dp", "seq", None), P("seq", "dp")),
        check_vma=False,
    )
```

time: 117 us -> 129 us (1.10); the launches traced: 115 us -> 130 us
  blocking collectives: 23.5 us -> 47.1 us
  Pallas kernels: 21.7 us -> 13.2 us
  waiting for transfers between devices: 20.2 us -> 26.4 us
  local copies, waits for them, and re-layouts: 9.75 us -> 5.06 us
  other arithmetic: 2.26 us -> 0.05 us
    all_to_all x0 -> x1, blocking collectives: none -> 29.9 us  [local(): lax.all_to_all(copies, 'dp', 0, 0, tiled=True).reshape(n_dp * ROWS, WIDTH)]
    pallas_call x4 -> x5, Pallas kernels: 20.1 us -> 10 us  [the longest x3 6.82 us: absorb_stage(): pl.pallas_call(kernel, out_shape=list(STATE_SHAPES), compiler_params=LIMI...]
    all_to_all x1, blocking collectives: 23.5 us -> 17.2 us  [local(): lax.all_to_all(share.reshape(n_seq, rows, LANES), 'seq', 0, 0, tiled=True)]
    ppermute x8 -> x10, waiting for transfers between devices: 10.8 us -> 15.8 us  [shifted(): return lax.ppermute(block, 'seq', route)]
    all_to_all x1, starting transfers between devices: 4.8 us -> 9.01 us  [local(): lax.all_to_all(attended, 'dp', 0, 0, tiled=True).reshape(n_dp, LANES, ROWS)]
    ppermute x4 -> x0, starting transfers between devices: 3.14 us -> none  [the longest x3 3.14 us: turned(): return lax.ppermute(block, 'dp', route)]
    unnamed x23 -> x18, local copies, waits for them, and re-layouts: 7.67 us -> 4.77 us
    concatenate x2 -> x0, other arithmetic: 2.09 us -> none  [the longest x1 2.03 us: gathered_over_dp(): mine = jnp.concatenate(ring, axis=0)]
  transfers between devices with their start and end apart: 14 -> 12, of which waited for: 4 -> 6; matrix products, arithmetic and copies ran while one was open for 5% -> 0% of each run, Pallas kernels for 17% -> 7%
where the time goes in v2:
time: 129 us; the launch traced here: 130 us
  blocking collectives  47.1 us (37%)
  starting transfers between devices  37 us (29%)
  waiting for transfers between devices  26.4 us (20%)
  Pallas kernels  13.2 us (10%)
  local copies, waits for them, and re-layouts  5.06 us (4%)
    all_to_all x1, blocking collectives, local(): lax.all_to_all(copies, 'dp', 0, 0, tiled=True).reshape(n_dp * ROWS, WIDTH)  29.9 us
    ppermute x10, starting transfers between devices, shifted(): return lax.ppermute(block, 'seq', route)  22.3 us
    all_to_all x1, blocking collectives, local(): lax.all_to_all(share.reshape(n_seq, rows, LANES), 'seq', 0, 0, tiled=True)  17.2 us
    ppermute x10, waiting for transfers between devices, shifted(): return lax.ppermute(block, 'seq', route)  15.8 us
    all_to_all x1, starting transfers between devices, local(): lax.all_to_all(attended, 'dp', 0, 0, tiled=True).reshape(n_dp, LANES, ROWS)  9.01 us
    pallas_call x3, Pallas kernels, absorb_stage(): pl.pallas_call(kernel, out_shape=list(STATE_SHAPES), compiler_params=LIMI...  6.82 us
    ppermute x1, waiting for transfers between devices, local(): return (block_out[None], lax.ppermute(block, ('dp', 'seq'), route))  6.24 us
    ppermute x1, starting transfers between devices, local(): return (block_out[None], lax.ppermute(block, ('dp', 'seq'), route))  5.7 us
  transfers between devices with their start and end apart: 12, of which 6 were waited for; matrix products, arithmetic and copies ran while one was open for 0% of the time, Pallas kernels for 7%

profile of v2, /device:TPU:4, one launch (start us, length us, event | category | flops | bytes accessed | tf_op | source)
XLA Modules:
  0.0 129.6 jit_solution(3889886401082796435)
XLA Ops:
  0.6 1.9 %layer_norm.1.own_ref = bf16[1040,128]{1,0:T(8,128)(2,1)} custom-call(bf16[128,1024]{1,0:T(8,128)(2,1)} %bitcast.10, s32[1,128]{1,0:T(1,128)} %ids_ref.1, f32[1,1024]{1,0:T(1,128)} %bitcast.14), custom_call_target="tpu_custom_call" | custom-call | tf_op jit(solution)/shard_map/layer_norm/pallas_call | solution.py:44
  2.6 5.9 %collective-permute-start.3 = (bf16[1040,128]{1,0:T(8,128)(2,1)}, bf16[1040,128]{1,0:T(8,128)(2,1)S(1)}, u32[]{:S(2)}, u32[]{:S(2)}) collective-permute-start(bf16[1040,128]{1,0:T(8,128)(2,1)} %layer_norm.1.own_ref), channel_id=1, source_target_pairs={{0,28},{1,29},{2,30},{3,31},{4,0},{5,1},{6,2},{7,3},{8,4},{9,5},{1... | collective-permute-start | bytes 798728 | tf_op jit(solution)/shard_map/ppermute | solution.py:28
  8.4 5.7 %collective-permute-start.1 = (bf16[1040,128]{1,0:T(8,128)(2,1)}, bf16[1040,128]{1,0:T(8,128)(2,1)S(1)}, u32[]{:S(2)}, u32[]{:S(2)}) collective-permute-start(bf16[1040,128]{1,0:T(8,128)(2,1)} %layer_norm.1.own_ref), channel_id=1, source_target_pairs={{0,31},{1,0},{2,1},{3,2},{4,3},{5,4},{6,5},{7,6},{8,7},{9,8},{10,9... | collective-permute-start | bytes 798728 | tf_op jit(solution)/shard_map/ppermute | solution.py:28
  14.1 2.8 %copy-done = bf16[1024,3072]{1,0:T(8,128)(2,1)S(1)} copy-done((bf16[1024,3072]{1,0:T(8,128)(2,1)S(1)}, bf16[1024,3072]{1,0:T(8,128)(2,1)}, u32[]{:S(2)}) %copy-start) | copy-done | bytes 6291480
  16.9 0.9 copy-done.1
  17.8 1.9 %own_block.1 = (bf16[8,128,256]{2,1,0:T(8,128)(2,1)S(1)}, f32[16,128]{1,0:T(8,128)S(1)}, f32[16,128]{1,0:T(8,128)S(1)}, f32[1024,128]{1,0:T(8,128)S(1)}) custom-call(bf16[1040,128]{1,0:T(8,128)(2,1)S(1)} %copy-done.1, bf16[1024,3072]{1,0:T(8,128)(2,1)S(1)} %copy-done), custom_call_target="tpu_custom_call" | custom-call | flops 1610612736 | bytes 8388608 | tf_op jit(solution)/shard_map/own_block/pallas_call | solution.py:160
  20.1 5.8 %collective-permute-done.refs_0_ = bf16[1040,128]{1,0:T(8,128)(2,1)S(1)} collective-permute-done((bf16[1040,128]{1,0:T(8,128)(2,1)}, bf16[1040,128]{1,0:T(8,128)(2,1)S(1)}, u32[]{:S(2)}, u32[]{:S(2)}) %collective-permute-start) | collective-permute-done | bytes 266272 | tf_op jit(solution)/shard_map/ppermute | solution.py:28
  26.0 2.0 %collective-permute-start.6 = (bf16[2080,128]{1,0:T(8,128)(2,1)S(1)}, bf16[2080,128]{1,0:T(8,128)(2,1)S(1)}, u32[]{:S(2)}, u32[]{:S(2)}) collective-permute-start(bf16[2080,128]{1,0:T(8,128)(2,1)S(1)} %constant_dynamic-update-slice_fusion), channel_id=1, source_target_pairs={{0,4},{1,5},{2,6},{3,7},{4,8},{5,9},{6,10},{7,11},{8,12},{9,13},{1... | collective-permute-start | bytes 1597448 | tf_op jit(solution)/shard_map/ppermute | solution.py:28
  28.0 5.3 %collective-permute-start.5 = (bf16[1040,128]{1,0:T(8,128)(2,1)S(1)}, bf16[1040,128]{1,0:T(8,128)(2,1)S(1)}, u32[]{:S(2)}, u32[]{:S(2)}) collective-permute-start(bf16[1040,128]{1,0:T(8,128)(2,1)S(1)} %collective-permute-done.1.refs_2_), channel_id=1, source_target_pairs={{0,31},{1,0},{2,1},{3,2},{4,3},{5,4},{6,5},{7,6},{8,7},{9,8},{10,9... | collective-permute-start | bytes 798728 | tf_op jit(solution)/shard_map/ppermute | solution.py:28
  33.4 4.1 %absorb_stage.3 = (f32[16,128]{1,0:T(8,128)S(1)}, f32[16,128]{1,0:T(8,128)S(1)}, f32[1024,128]{1,0:T(8,128)S(1)}) custom-call(bf16[1040,128]{1,0:T(8,128)(2,1)S(1)} %copy-done.2, bf16[1040,128]{1,0:T(8,128)(2,1)S(1)} %collective-permute-done.refs_0_, bf16[1040,128]{1,0:T(8,128)(2,1)S(1)} %collective-permute-done.2.refs_1_, ...), custom_call_target="tpu_custom_call" | custom-call | flops 2147483648 | bytes 8388608 | tf_op jit(solution)/shard_map/absorb_stage/pallas_call | solution.py:201
  37.5 8.0 %collective-permute-done.4.refs_0_ = bf16[1040,128]{1,0:T(8,128)(2,1)S(1)} collective-permute-done((bf16[1040,128]{1,0:T(8,128)(2,1)S(1)}, bf16[1040,128]{1,0:T(8,128)(2,1)S(1)}, u32[]{:S(2)}, u32[]{:S(2)}) %collective-permute-start.4) | collective-permute-done | bytes 266272 | tf_op jit(solution)/shard_map/ppermute | solution.py:28
  45.6 3.2 %collective-permute-start.9 = (bf16[1040,128]{1,0:T(8,128)(2,1)S(1)}, bf16[1040,128]{1,0:T(8,128)(2,1)S(1)}, u32[]{:S(2)}, u32[]{:S(2)}) collective-permute-start(bf16[1040,128]{1,0:T(8,128)(2,1)S(1)} %collective-permute-done.5.refs_1_), channel_id=1, source_target_pairs={{0,28},{1,29},{2,30},{3,31},{4,0},{5,1},{6,2},{7,3},{8,4},{9,5},{1... | collective-permute-start | bytes 798728 | tf_op jit(solution)/shard_map/ppermute | solution.py:28
  48.8 2.5 %absorb_stage.4 = (f32[16,128]{1,0:T(8,128)S(1)}, f32[16,128]{1,0:T(8,128)S(1)}, f32[1024,128]{1,0:T(8,128)S(1)}) custom-call(bf16[1040,128]{1,0:T(8,128)(2,1)S(1)} %copy-done.2, bf16[1040,128]{1,0:T(8,128)(2,1)S(1)} %collective-permute-done.4.refs_0_, bf16[1040,128]{1,0:T(8,128)(2,1)S(1)} %collective-permute-done.5.refs_1_, ...), custom_call_target="tpu_custom_call" | custom-call | flops 1073741824 | bytes 8388608 | tf_op jit(solution)/shard_map/absorb_stage/pallas_call | solution.py:201
  51.6 1.7 %collective-permute-done.8.refs_0_ = bf16[1040,128]{1,0:T(8,128)(2,1)S(1)} collective-permute-done((bf16[1040,128]{1,0:T(8,128)(2,1)S(1)}, bf16[1040,128]{1,0:T(8,128)(2,1)S(1)}, u32[]{:S(2)}, u32[]{:S(2)}) %collective-permute-start.8) | collective-permute-done | bytes 266272 | tf_op jit(solution)/shard_map/ppermute | solution.py:28
  53.2 0.4 copy-done.3
  53.6 1.3 %last_stage.1 = (bf16[1024,128]{1,0:T(8,128)(2,1)}, bf16[128,1024]{1,0:T(8,128)(2,1)}) custom-call(bf16[1040,128]{1,0:T(8,128)(2,1)S(1)} %copy-done.2, bf16[1040,128]{1,0:T(8,128)(2,1)S(1)} %collective-permute-done.8.refs_0_, bf16[1040,128]{1,0:T(8,128)(2,1)S(1)} %collective-permute-done.9.refs_1_, ...), custom_call_target="tpu_custom_call" | custom-call | flops 1610612736 | bytes 10485760 | tf_op jit(solution)/shard_map/last_stage/pallas_call | solution.py:232
  55.0 9.0 %all-to-all-start = ((bf16[8,128,128]{2,1,0:T(8,128)(2,1)}), bf16[8,128,128]{2,1,0:T(8,128)(2,1)S(1)}, u32[]{:S(2)}, u32[]{:S(2)}) async-start(bf16[8,128,128]{2,1,0:T(8,128)(2,1)} %bitcast.3), calls=%async_computation | async-start | bytes 524288 | tf_op jit(solution)/shard_map/all_to_all | solution.py:299
  64.0 4.4 %all-to-all-done.attended_ref = bf16[8,128,128]{2,1,0:T(8,128)(2,1)S(1)} async-done(((bf16[8,128,128]{2,1,0:T(8,128)(2,1)}), bf16[8,128,128]{2,1,0:T(8,128)(2,1)S(1)}, u32[]{:S(2)}, u32[]{:S(2)}) %all-to-all-start) | async-done | bytes 262176 | tf_op jit(solution)/shard_map/all_to_all | solution.py:299
  68.6 29.9 %all_to_all.19 = bf16[8,128,1024]{2,1,0:T(8,128)(2,1)S(1)} all-to-all(bf16[8,128,1024]{2,1,0:T(8,128)(2,1)S(1)} %broadcast_in_dim.16), channel_id=1, replica_groups=mesh['dp'=8,'seq'=32] {'dp'}, dimensions={0} | all-to-all | bytes 4194304 | tf_op jit(solution)/shard_map/all_to_all | solution.py:284
  98.6 1.3 grad_product.1
  99.8 17.2 %all_to_all.20 = bf16[32,32,128]{2,1,0:T(8,128)(2,1)S(1)} all-to-all(bf16[32,32,128]{2,1,0:T(8,128)(2,1)S(1)} %bitcast.12), channel_id=1, replica_groups=mesh['dp'=8,'seq'=32] {'seq'}, dimensions={0} | all-to-all | bytes 524288 | tf_op jit(solution)/shard_map/all_to_all | solution.py:302
  117.1 5.7 %collective-permute-start.10 = (f32[32,128]{1,0:T(8,128)S(1)}, f32[32,128]{1,0:T(8,128)S(1)}, u32[]{:S(2)}, u32[]{:S(2)}) collective-permute-start(f32[32,128]{1,0:T(8,128)S(1)} %broadcast_multiply_fusion), channel_id=1, source_target_pairs={{0,0},{1,1},{2,2},{3,3},{4,32},{5,33},{6,34},{7,35},{8,64},{9,65},... | collective-permute-start | bytes 49160 | tf_op jit(solution)/shard_map/ppermute | solution.py:312
  122.8 6.2 %collective-permute-done.10 = f32[32,128]{1,0:T(8,128)S(1)} collective-permute-done((f32[32,128]{1,0:T(8,128)S(1)}, f32[32,128]{1,0:T(8,128)S(1)}, u32[]{:S(2)}, u32[]{:S(2)}) %collective-permute-start.10) | collective-permute-done | bytes 16416 | tf_op jit(solution)/shard_map/ppermute | solution.py:312
  129.0 0.6 copy.10
  (32 shorter events, 1.1 us)
Async XLA Ops:
  2.6 17.2 %collective-permute-start.3 = (bf16[1040,128]{1,0:T(8,128)(2,1)}, bf16[1040,128]{1,0:T(8,128)(2,1)S(1)}, u32[]{:S(2)}, u32[]{:S(2)}) collective-permute-start(bf16[1040,128]{1,0:T(8,128)(2,1)} %layer_norm.1.own_ref), channel_id=1, source_target_pairs={{0,28},{1,29},{2,30},{3,31},{4,0},{5,1},{6,2},{7,3},{8,4},{9,5},{1... | collective-permute-start | bytes 798728 | tf_op jit(solution)/shard_map/ppermute | solution.py:28
  8.4 11.3 %collective-permute-start.2 = (bf16[1040,128]{1,0:T(8,128)(2,1)}, bf16[1040,128]{1,0:T(8,128)(2,1)S(1)}, u32[]{:S(2)}, u32[]{:S(2)}) collective-permute-start(bf16[1040,128]{1,0:T(8,128)(2,1)} %layer_norm.1.own_ref), channel_id=1, source_target_pairs={{0,4},{1,5},{2,6},{3,7},{4,8},{5,9},{6,10},{7,11},{8,12},{9,13},{1... | collective-permute-start | bytes 798728 | tf_op jit(solution)/shard_map/ppermute | solution.py:28
  8.4 11.7 %collective-permute-start.1 = (bf16[1040,128]{1,0:T(8,128)(2,1)}, bf16[1040,128]{1,0:T(8,128)(2,1)S(1)}, u32[]{:S(2)}, u32[]{:S(2)}) collective-permute-start(bf16[1040,128]{1,0:T(8,128)(2,1)} %layer_norm.1.own_ref), channel_id=1, source_target_pairs={{0,31},{1,0},{2,1},{3,2},{4,3},{5,4},{6,5},{7,6},{8,7},{9,8},{10,9... | collective-permute-start | bytes 798728 | tf_op jit(solution)/shard_map/ppermute | solution.py:28
  14.1 11.7 %collective-permute-start = (bf16[1040,128]{1,0:T(8,128)(2,1)}, bf16[1040,128]{1,0:T(8,128)(2,1)S(1)}, u32[]{:S(2)}, u32[]{:S(2)}) collective-permute-start(bf16[1040,128]{1,0:T(8,128)(2,1)} %layer_norm.1.own_ref), channel_id=1, source_target_pairs={{0,1},{1,2},{2,3},{3,4},{4,5},{5,6},{6,7},{7,8},{8,9},{9,10},{10,1... | collective-permute-start | bytes 798728 | tf_op jit(solution)/shard_map/ppermute | solution.py:28
  14.1 2.8 %copy-start = (bf16[1024,3072]{1,0:T(8,128)(2,1)S(1)}, bf16[1024,3072]{1,0:T(8,128)(2,1)}, u32[]{:S(2)}) copy-start(bf16[1024,3072]{1,0:T(8,128)(2,1)} %refs_3_.5) | copy-start | bytes 18874372
  16.9 1.0 copy-start.1
  17.8 15.5 %copy-start.2 = (bf16[1040,128]{1,0:T(8,128)(2,1)S(1)}, bf16[1040,128]{1,0:T(8,128)(2,1)}, u32[]{:S(2)}) copy-start(bf16[1040,128]{1,0:T(8,128)(2,1)} %layer_norm.1.own_ref) | copy-start | bytes 798724
  25.9 19.6 %collective-permute-start.7 = (bf16[2080,128]{1,0:T(8,128)(2,1)S(1)}, bf16[2080,128]{1,0:T(8,128)(2,1)S(1)}, u32[]{:S(2)}, u32[]{:S(2)}) collective-permute-start(bf16[2080,128]{1,0:T(8,128)(2,1)S(1)} %constant_dynamic-update-slice_fusion), channel_id=1, source_target_pairs={{0,28},{1,29},{2,30},{3,31},{4,0},{5,1},{6,2},{7,3},{8,4},{9,5},{1... | collective-permute-start | bytes 1597448 | tf_op jit(solution)/shard_map/ppermute | solution.py:28
  26.0 19.5 %collective-permute-start.6 = (bf16[2080,128]{1,0:T(8,128)(2,1)S(1)}, bf16[2080,128]{1,0:T(8,128)(2,1)S(1)}, u32[]{:S(2)}, u32[]{:S(2)}) collective-permute-start(bf16[2080,128]{1,0:T(8,128)(2,1)S(1)} %constant_dynamic-update-slice_fusion), channel_id=1, source_target_pairs={{0,4},{1,5},{2,6},{3,7},{4,8},{5,9},{6,10},{7,11},{8,12},{9,13},{1... | collective-permute-start | bytes 1597448 | tf_op jit(solution)/shard_map/ppermute | solution.py:28
  28.0 17.5 %collective-permute-start.4 = (bf16[1040,128]{1,0:T(8,128)(2,1)S(1)}, bf16[1040,128]{1,0:T(8,128)(2,1)S(1)}, u32[]{:S(2)}, u32[]{:S(2)}) collective-permute-start(bf16[1040,128]{1,0:T(8,128)(2,1)S(1)} %collective-permute-done.refs_0_), channel_id=1, source_target_pairs={{0,1},{1,2},{2,3},{3,4},{4,5},{5,6},{6,7},{7,8},{8,9},{9,10},{10,1... | collective-permute-start | bytes 798728 | tf_op jit(solution)/shard_map/ppermute | solution.py:28
  28.0 17.5 %collective-permute-start.5 = (bf16[1040,128]{1,0:T(8,128)(2,1)S(1)}, bf16[1040,128]{1,0:T(8,128)(2,1)S(1)}, u32[]{:S(2)}, u32[]{:S(2)}) collective-permute-start(bf16[1040,128]{1,0:T(8,128)(2,1)S(1)} %collective-permute-done.1.refs_2_), channel_id=1, source_target_pairs={{0,31},{1,0},{2,1},{3,2},{4,3},{5,4},{6,5},{7,6},{8,7},{9,8},{10,9... | collective-permute-start | bytes 798728 | tf_op jit(solution)/shard_map/ppermute | solution.py:28
  45.5 7.7 %collective-permute-start.8 = (bf16[1040,128]{1,0:T(8,128)(2,1)S(1)}, bf16[1040,128]{1,0:T(8,128)(2,1)S(1)}, u32[]{:S(2)}, u32[]{:S(2)}) collective-permute-start(bf16[1040,128]{1,0:T(8,128)(2,1)S(1)} %collective-permute-done.4.refs_0_), channel_id=1, source_target_pairs={{0,4},{1,5},{2,6},{3,7},{4,8},{5,9},{6,10},{7,11},{8,12},{9,13},{1... | collective-permute-start | bytes 798728 | tf_op jit(solution)/shard_map/ppermute | solution.py:28
  45.6 7.6 %collective-permute-start.9 = (bf16[1040,128]{1,0:T(8,128)(2,1)S(1)}, bf16[1040,128]{1,0:T(8,128)(2,1)S(1)}, u32[]{:S(2)}, u32[]{:S(2)}) collective-permute-start(bf16[1040,128]{1,0:T(8,128)(2,1)S(1)} %collective-permute-done.5.refs_1_), channel_id=1, source_target_pairs={{0,28},{1,29},{2,30},{3,31},{4,0},{5,1},{6,2},{7,3},{8,4},{9,5},{1... | collective-permute-start | bytes 798728 | tf_op jit(solution)/shard_map/ppermute | solution.py:28
  48.8 4.4 %slice-start = ((s8[6291456]{0:T(1024)(128)(4,1)}), s8[4194304]{0:T(1024)(128)(4,1)S(1)}, s32[]{:S(2)}) async-start(s8[6291456]{0:T(1024)(128)(4,1)} %bitcast.7), calls=%async_computation.3 | async-start | bytes 8388608
  51.4 1.8 %slice-start.1 = ((s8[6291456]{0:T(1024)(128)(4,1)}), s8[2097152]{0:T(1024)(128)(4,1)S(1)}, s32[]{:S(2)}) async-start(s8[6291456]{0:T(1024)(128)(4,1)} %bitcast.7), calls=%async_computation.4 | async-start | bytes 4194304
  51.4 2.2 %copy-start.3 = (bf16[1024,1024]{1,0:T(8,128)(2,1)S(1)}, bf16[1024,1024]{1,0:T(8,128)(2,1)}, u32[]{:S(2)}) copy-start(bf16[1024,1024]{1,0:T(8,128)(2,1)} %refs_8_.1) | copy-start | bytes 6291460
  51.4 2.2 %copy-start.4 = (bf16[1,128,1024]{2,1,0:T(8,128)(2,1)S(1)}, bf16[1,128,1024]{2,1,0:T(8,128)(2,1)}, u32[]{:S(2)}) copy-start(bf16[1,128,1024]{2,1,0:T(8,128)(2,1)} %param.6) | copy-start | bytes 786436
  53.6 14.7 %copy-start.5 = (bf16[1,128,1024]{2,1,0:T(8,128)(2,1)S(1)}, bf16[1,128,1024]{2,1,0:T(8,128)(2,1)}, u32[]{:S(2)}) copy-start(bf16[1,128,1024]{2,1,0:T(8,128)(2,1)} %param.11) | copy-start | bytes 786436
  55.0 13.4 %all-to-all-start = ((bf16[8,128,128]{2,1,0:T(8,128)(2,1)}), bf16[8,128,128]{2,1,0:T(8,128)(2,1)S(1)}, u32[]{:S(2)}, u32[]{:S(2)}) async-start(bf16[8,128,128]{2,1,0:T(8,128)(2,1)} %bitcast.3), calls=%async_computation | async-start | bytes 524288 | tf_op jit(solution)/shard_map/all_to_all | solution.py:299
  117.1 11.9 %collective-permute-start.10 = (f32[32,128]{1,0:T(8,128)S(1)}, f32[32,128]{1,0:T(8,128)S(1)}, u32[]{:S(2)}, u32[]{:S(2)}) collective-permute-start(f32[32,128]{1,0:T(8,128)S(1)} %broadcast_multiply_fusion), channel_id=1, source_target_pairs={{0,0},{1,1},{2,2},{3,3},{4,32},{5,33},{6,34},{7,35},{8,64},{9,65},... | collective-permute-start | bytes 49160 | tf_op jit(solution)/shard_map/ppermute | solution.py:312

commit v3 on v2

--- a/solution.py
+++ b/solution.py
@@ -242,26 +242,45 @@
     )(own, *blocks, queries, w_qkv, *state, frames, w_out)
 
 
-def grad_kernel(attended_ref, cotangent_ref, out_ref):
-    attended = jnp.concatenate([attended_ref[p] for p in range(CHUNKS)], axis=1)
-    product = jnp.dot(attended, cotangent_ref[...], preferred_element_type=F32).astype(BF16)
-    for half in range(2):
-        out_ref[half] = product[:, half * LANES : (half + 1) * LANES]
-
-
-def grad_product(attended, cotangent):
+def grad_kernel(order_ref, attended_ref, *refs):
+    grads, out_ref = refs[:-1], refs[-1]
+    attended = jnp.concatenate([attended_ref[order_ref[i]] for i in range(len(grads))], axis=1)
+    for quad in range(QUADS):
+        at = slice(quad * QUAD, (quad + 1) * QUAD)
+        block = jnp.concatenate([ref[:, at] for ref in grads], axis=0)
+        product = jnp.dot(attended, block, preferred_element_type=F32).astype(BF16)
+        for half in range(2):
+            out_ref[2 * quad + half] = product[:, half * LANES : (half + 1) * LANES]
+
+
+def grad_product(order, attended, grads):
+    vmem = pl.BlockSpec(memory_space=pltpu.VMEM)
     return pl.pallas_call(
         grad_kernel,
-        grid=(QUADS,),
-        in_specs=[
-            pl.BlockSpec((CHUNKS, LANES, ROWS), lambda j: (0, 0, 0)),
-            pl.BlockSpec((CHUNKS * ROWS, QUAD), lambda j: (0, j)),
-        ],
-        out_specs=pl.BlockSpec((2, LANES, LANES), lambda j: (j, 0, 0)),
+        in_specs=[pl.BlockSpec(memory_space=pltpu.SMEM)] + [vmem] * (1 + len(grads)),
         out_shape=jax.ShapeDtypeStruct((CHUNKS, LANES, LANES), BF16),
         compiler_params=LIMIT,
         name="grad_product",
-    )(attended, cotangent)
+    )(order, attended, *grads)
+
+
+def chip_turned(block, distance):
+    n_dp = lax.axis_size("dp")
+    route = [(i, (i + 2 * distance) % n_dp) for i in range(n_dp)]
+    return lax.ppermute(block, "dp", route)
+
+
+def core_swapped(block):
+    return lax.ppermute(block, "dp", [(i, i ^ 1) for i in range(lax.axis_size("dp"))])
+
+
+def gathered_order():
+    n_dp = lax.axis_size("dp")
+    table = []
+    for place in range(n_dp):
+        ring = [(place + n_dp - 2 * d) % n_dp for d in range(n_dp // 2)]
+        table.append(ring + [i ^ 1 for i in ring])
+    return lax.dynamic_index_in_dim(jnp.asarray(table, jnp.int32), lax.axis_index("dp"), 0, False)
 
 
 def local(frames, segment_ids, norm_gain, w_qkv, w_out, cotangent):
@@ -272,6 +291,8 @@
 
     left1, right1 = shifted(own, 1), shifted(own, -1)
     left4, right4 = shifted(own, 4), shifted(own, -4)
+    cotangent = cotangent[0]
+    ring = [chip_turned(cotangent, d) for d in range(1, n_dp // 2)]
     queries, *state = own_block(own, w_qkv)
     left1, right1, left4, right4, queries = lax.optimization_barrier(
         (left1, right1, left4, right4, queries)
@@ -279,9 +300,8 @@
     near = jnp.concatenate([left1, right1], axis=0)
     left_two, right_two = shifted(near, 4), shifted(near, -4)
     left2, right2 = shifted(left1, 1), shifted(right1, -1)
-    cotangent, near = lax.optimization_barrier((cotangent, near))
-    copies = jnp.broadcast_to(cotangent, (n_dp, *cotangent.shape[1:]))
-    all_grads = lax.all_to_all(copies, "dp", 0, 0, tiled=True).reshape(n_dp * ROWS, WIDTH)
+    near, *ring = lax.optimization_barrier((near, *ring))
+    grads = [cotangent, *ring, core_swapped(cotangent), *[core_swapped(block) for block in ring]]
 
     state = absorb_stage(
         own, (left1, left4, right1, right4), ((0, 0), (1, 0)), ((2, 0), (3, 0)), queries, w_qkv, state
@@ -297,7 +317,7 @@
     )
 
     pieces = lax.all_to_all(attended, "dp", 0, 0, tiled=True).reshape(n_dp, LANES, ROWS)
-    share = grad_product(pieces, all_grads)
+    share = grad_product(gathered_order(), pieces, grads)
     rows = LANES * CHUNKS // n_seq
     parts = lax.all_to_all(share.reshape(n_seq, rows, LANES), "seq", 0, 0, tiled=True)
     grad_scale = (n_dp * n_seq * ROWS) ** (-0.5)

time: 129 us -> 103 us (0.80)
  blocking collectives: 47.1 us -> 21.8 us
  starting transfers between devices: 37 us -> 35.6 us
    all_to_all x1 -> x0, blocking collectives: 29.9 us -> none  [local(): lax.all_to_all(copies, 'dp', 0, 0, tiled=True).reshape(n_dp * ROWS, WIDTH)]
    ppermute x0 -> x7, waiting for transfers between devices: none -> 9.38 us  [the longest x3 9.37 us: chip_turned(): return lax.ppermute(block, 'dp', route)]
    ppermute x10, waiting for transfers between devices: 15.8 us -> 6.82 us  [shifted(): return lax.ppermute(block, 'seq', route)]
    all_to_all x1, blocking collectives: 17.2 us -> 21.8 us  [local(): lax.all_to_all(share.reshape(n_seq, rows, LANES), 'seq', 0, 0, tiled=True)]
    ppermute x0 -> x7, starting transfers between devices: none -> 3.79 us  [the longest x3 3.14 us: chip_turned(): return lax.ppermute(block, 'dp', route)]
    all_to_all x1, starting transfers between devices: 9.01 us -> 5.56 us  [local(): lax.all_to_all(attended, 'dp', 0, 0, tiled=True).reshape(n_dp, LANES, ROWS)]
    ppermute x10, starting transfers between devices: 22.3 us -> 20.6 us  [shifted(): return lax.ppermute(block, 'seq', route)]
  transfers between devices with their start and end apart: 12 -> 19, of which waited for: 6 -> 8; matrix products, arithmetic and copies ran while one was open for 0% -> 1% of each run, Pallas kernels for 7% -> 10%
where the time goes in v3:
time: 103 us
  starting transfers between devices  35.6 us (35%)
  waiting for transfers between devices  26.1 us (25%)
  blocking collectives  21.8 us (21%)
  Pallas kernels  13.4 us (13%)
  local copies, waits for them, and re-layouts  5.12 us (5%)
    all_to_all x1, blocking collectives, local(): lax.all_to_all(share.reshape(n_seq, rows, LANES), 'seq', 0, 0, tiled=True)  21.8 us
    ppermute x10, starting transfers between devices, shifted(): return lax.ppermute(block, 'seq', route)  20.6 us
    ppermute x3, waiting for transfers between devices, chip_turned(): return lax.ppermute(block, 'dp', route)  9.37 us
    pallas_call x3, Pallas kernels, absorb_stage(): pl.pallas_call(kernel, out_shape=list(STATE_SHAPES), compiler_params=LIMI...  7.03 us
    ppermute x10, waiting for transfers between devices, shifted(): return lax.ppermute(block, 'seq', route)  6.82 us
    ppermute x1, waiting for transfers between devices, local(): return (block_out[None], lax.ppermute(block, ('dp', 'seq'), route))  6.29 us
    ppermute x1, starting transfers between devices, local(): return (block_out[None], lax.ppermute(block, ('dp', 'seq'), route))  5.64 us
    all_to_all x1, starting transfers between devices, local(): lax.all_to_all(attended, 'dp', 0, 0, tiled=True).reshape(n_dp, LANES, ROWS)  5.56 us
  transfers between devices with their start and end apart: 19, of which 8 were waited for; matrix products, arithmetic and copies ran while one was open for 1% of the time, Pallas kernels for 10%

profile of v3, /device:TPU:4, one launch (start us, length us, event | category | flops | bytes accessed | tf_op | source)
XLA Modules:
  0.0 103.0 jit_solution(8552110833209633382)
XLA Ops:
  0.6 2.0 %layer_norm.1.own_ref = bf16[1040,128]{1,0:T(8,128)(2,1)} custom-call(bf16[128,1024]{1,0:T(8,128)(2,1)} %bitcast.10, s32[1,128]{1,0:T(1,128)} %ids_ref.1, f32[1,1024]{1,0:T(1,128)} %bitcast.18), custom_call_target="tpu_custom_call" | custom-call | tf_op jit(solution)/shard_map/layer_norm/pallas_call | solution.py:44
  2.6 1.6 %collective-permute-start = (bf16[1040,128]{1,0:T(8,128)(2,1)}, bf16[1040,128]{1,0:T(8,128)(2,1)S(1)}, u32[]{:S(2)}, u32[]{:S(2)}) collective-permute-start(bf16[1040,128]{1,0:T(8,128)(2,1)} %layer_norm.1.own_ref), channel_id=1, source_target_pairs={{0,1},{1,2},{2,3},{3,4},{4,5},{5,6},{6,7},{7,8},{8,9},{9,10},{10,1... | collective-permute-start | bytes 798728 | tf_op jit(solution)/shard_map/ppermute | solution.py:28
  4.2 6.7 %collective-permute-start.1 = (bf16[1040,128]{1,0:T(8,128)(2,1)}, bf16[1040,128]{1,0:T(8,128)(2,1)S(1)}, u32[]{:S(2)}, u32[]{:S(2)}) collective-permute-start(bf16[1040,128]{1,0:T(8,128)(2,1)} %layer_norm.1.own_ref), channel_id=1, source_target_pairs={{0,31},{1,0},{2,1},{3,2},{4,3},{5,4},{6,5},{7,6},{8,7},{9,8},{10,9... | collective-permute-start | bytes 798728 | tf_op jit(solution)/shard_map/ppermute | solution.py:28
  10.9 3.2 %collective-permute-start.3 = (bf16[1040,128]{1,0:T(8,128)(2,1)}, bf16[1040,128]{1,0:T(8,128)(2,1)S(1)}, u32[]{:S(2)}, u32[]{:S(2)}) collective-permute-start(bf16[1040,128]{1,0:T(8,128)(2,1)} %layer_norm.1.own_ref), channel_id=1, source_target_pairs={{0,28},{1,29},{2,30},{3,31},{4,0},{5,1},{6,2},{7,3},{8,4},{9,5},{1... | collective-permute-start | bytes 798728 | tf_op jit(solution)/shard_map/ppermute | solution.py:28
  14.1 2.8 %copy-done = bf16[1024,3072]{1,0:T(8,128)(2,1)S(1)} copy-done((bf16[1024,3072]{1,0:T(8,128)(2,1)S(1)}, bf16[1024,3072]{1,0:T(8,128)(2,1)}, u32[]{:S(2)}) %copy-start) | copy-done | bytes 6291480
  17.9 1.9 %own_block.1 = (bf16[8,128,256]{2,1,0:T(8,128)(2,1)S(1)}, f32[16,128]{1,0:T(8,128)S(1)}, f32[16,128]{1,0:T(8,128)S(1)}, f32[1024,128]{1,0:T(8,128)S(1)}) custom-call(bf16[1040,128]{1,0:T(8,128)(2,1)S(1)} %copy-done.1, bf16[1024,3072]{1,0:T(8,128)(2,1)S(1)} %copy-done), custom_call_target="tpu_custom_call" | custom-call | flops 1610612736 | bytes 8388608 | tf_op jit(solution)/shard_map/own_block/pallas_call | solution.py:160
  20.2 2.4 %collective-permute-done.3.refs_3_ = bf16[1040,128]{1,0:T(8,128)(2,1)S(1)} collective-permute-done((bf16[1040,128]{1,0:T(8,128)(2,1)}, bf16[1040,128]{1,0:T(8,128)(2,1)S(1)}, u32[]{:S(2)}, u32[]{:S(2)}) %collective-permute-start.3) | collective-permute-done | bytes 266272 | tf_op jit(solution)/shard_map/ppermute | solution.py:28
  22.7 3.7 %collective-permute-start.7 = (bf16[2080,128]{1,0:T(8,128)(2,1)S(1)}, bf16[2080,128]{1,0:T(8,128)(2,1)S(1)}, u32[]{:S(2)}, u32[]{:S(2)}) collective-permute-start(bf16[2080,128]{1,0:T(8,128)(2,1)S(1)} %constant_dynamic-update-slice_fusion), channel_id=1, source_target_pairs={{0,28},{1,29},{2,30},{3,31},{4,0},{5,1},{6,2},{7,3},{8,4},{9,5},{1... | collective-permute-start | bytes 1597448 | tf_op jit(solution)/shard_map/ppermute | solution.py:28
  26.4 1.2 %collective-permute-start.10 = (bf16[128,1024]{1,0:T(8,128)(2,1)S(1)}, bf16[128,1024]{1,0:T(8,128)(2,1)S(1)}, u32[]{:S(2)}, u32[]{:S(2)}) collective-permute-start(bf16[128,1024]{1,0:T(8,128)(2,1)S(1)} %bitcast.13), channel_id=1, source_target_pairs={{0,64},{32,96},{64,128},{96,160},{128,192},{160,224},{192,0},{224,... | collective-permute-start | bytes 786440 | tf_op jit(solution)/shard_map/ppermute | solution.py:270
  28.4 1.1 %collective-permute-start.12 = (bf16[128,1024]{1,0:T(8,128)(2,1)S(1)}, bf16[128,1024]{1,0:T(8,128)(2,1)S(1)}, u32[]{:S(2)}, u32[]{:S(2)}) collective-permute-start(bf16[128,1024]{1,0:T(8,128)(2,1)S(1)} %bitcast.15), channel_id=1, source_target_pairs={{0,192},{32,224},{64,0},{96,32},{128,64},{160,96},{192,128},{224,1... | collective-permute-start | bytes 786440 | tf_op jit(solution)/shard_map/ppermute | solution.py:270
  29.5 6.1 %collective-permute-done.10.refs_1_ = bf16[128,1024]{1,0:T(8,128)(2,1)S(1)} collective-permute-done((bf16[128,1024]{1,0:T(8,128)(2,1)S(1)}, bf16[128,1024]{1,0:T(8,128)(2,1)S(1)}, u32[]{:S(2)}, u32[]{:S(2)}) %collective-permute-start.10) | collective-permute-done | bytes 262176 | tf_op jit(solution)/shard_map/ppermute | solution.py:270
  35.7 3.3 %collective-permute-done.11.refs_2_ = bf16[128,1024]{1,0:T(8,128)(2,1)S(1)} collective-permute-done((bf16[128,1024]{1,0:T(8,128)(2,1)S(1)}, bf16[128,1024]{1,0:T(8,128)(2,1)S(1)}, u32[]{:S(2)}, u32[]{:S(2)}) %collective-permute-start.11) | collective-permute-done | bytes 262176 | tf_op jit(solution)/shard_map/ppermute | solution.py:270
  38.9 2.1 %collective-permute-start.5 = (bf16[1040,128]{1,0:T(8,128)(2,1)S(1)}, bf16[1040,128]{1,0:T(8,128)(2,1)S(1)}, u32[]{:S(2)}, u32[]{:S(2)}) collective-permute-start(bf16[1040,128]{1,0:T(8,128)(2,1)S(1)} %collective-permute-done.1.refs_2_), channel_id=1, source_target_pairs={{0,31},{1,0},{2,1},{3,2},{4,3},{5,4},{6,5},{7,6},{8,7},{9,8},{10,9... | collective-permute-start | bytes 798728 | tf_op jit(solution)/shard_map/ppermute | solution.py:28
  41.0 4.3 %absorb_stage.3 = (f32[16,128]{1,0:T(8,128)S(1)}, f32[16,128]{1,0:T(8,128)S(1)}, f32[1024,128]{1,0:T(8,128)S(1)}) custom-call(bf16[1040,128]{1,0:T(8,128)(2,1)S(1)} %copy-done.2, bf16[1040,128]{1,0:T(8,128)(2,1)S(1)} %collective-permute-done.refs_0_, bf16[1040,128]{1,0:T(8,128)(2,1)S(1)} %collective-permute-done.2.refs_1_, ...), custom_call_target="tpu_custom_call" | custom-call | flops 2147483648 | bytes 8388608 | tf_op jit(solution)/shard_map/absorb_stage/pallas_call | solution.py:201
  46.2 3.1 %collective-permute-start.9 = (bf16[1040,128]{1,0:T(8,128)(2,1)S(1)}, bf16[1040,128]{1,0:T(8,128)(2,1)S(1)}, u32[]{:S(2)}, u32[]{:S(2)}) collective-permute-start(bf16[1040,128]{1,0:T(8,128)(2,1)S(1)} %collective-permute-done.5.refs_1_), channel_id=1, source_target_pairs={{0,28},{1,29},{2,30},{3,31},{4,0},{5,1},{6,2},{7,3},{8,4},{9,5},{1... | collective-permute-start | bytes 798728 | tf_op jit(solution)/shard_map/ppermute | solution.py:28
  49.3 2.6 %absorb_stage.4 = (f32[16,128]{1,0:T(8,128)S(1)}, f32[16,128]{1,0:T(8,128)S(1)}, f32[1024,128]{1,0:T(8,128)S(1)}) custom-call(bf16[1040,128]{1,0:T(8,128)(2,1)S(1)} %copy-done.2, bf16[1040,128]{1,0:T(8,128)(2,1)S(1)} %collective-permute-done.4.refs_0_, bf16[1040,128]{1,0:T(8,128)(2,1)S(1)} %collective-permute-done.5.refs_1_, ...), custom_call_target="tpu_custom_call" | custom-call | flops 1073741824 | bytes 8388608 | tf_op jit(solution)/shard_map/absorb_stage/pallas_call | solution.py:201
  52.1 3.9 %collective-permute-done.8.refs_0_ = bf16[1040,128]{1,0:T(8,128)(2,1)S(1)} collective-permute-done((bf16[1040,128]{1,0:T(8,128)(2,1)S(1)}, bf16[1040,128]{1,0:T(8,128)(2,1)S(1)}, u32[]{:S(2)}, u32[]{:S(2)}) %collective-permute-start.8) | collective-permute-done | bytes 266272 | tf_op jit(solution)/shard_map/ppermute | solution.py:28
  56.1 1.6 %last_stage.1 = (bf16[1024,128]{1,0:T(8,128)(2,1)}, bf16[128,1024]{1,0:T(8,128)(2,1)}) custom-call(bf16[1040,128]{1,0:T(8,128)(2,1)S(1)} %copy-done.2, bf16[1040,128]{1,0:T(8,128)(2,1)S(1)} %collective-permute-done.8.refs_0_, bf16[1040,128]{1,0:T(8,128)(2,1)S(1)} %collective-permute-done.9.refs_1_, ...), custom_call_target="tpu_custom_call" | custom-call | flops 1610612736 | bytes 10485760 | tf_op jit(solution)/shard_map/last_stage/pallas_call | solution.py:232
  57.6 5.6 %all-to-all-start = ((bf16[8,128,128]{2,1,0:T(8,128)(2,1)}), bf16[8,128,128]{2,1,0:T(8,128)(2,1)S(1)}, u32[]{:S(2)}, u32[]{:S(2)}) async-start(bf16[8,128,128]{2,1,0:T(8,128)(2,1)} %bitcast.4), calls=%async_computation | async-start | bytes 524288 | tf_op jit(solution)/shard_map/all_to_all | solution.py:319
  63.9 3.6 %all-to-all-done.attended_ref = bf16[8,128,128]{2,1,0:T(8,128)(2,1)S(1)} async-done(((bf16[8,128,128]{2,1,0:T(8,128)(2,1)}), bf16[8,128,128]{2,1,0:T(8,128)(2,1)S(1)}, u32[]{:S(2)}, u32[]{:S(2)}) %all-to-all-start) | async-done | bytes 262176 | tf_op jit(solution)/shard_map/all_to_all | solution.py:319
  67.5 1.0 grad_product.1
  68.5 21.8 %all_to_all.14 = bf16[32,32,128]{2,1,0:T(8,128)(2,1)S(1)} all-to-all(bf16[32,32,128]{2,1,0:T(8,128)(2,1)S(1)} %bitcast.12), channel_id=1, replica_groups=mesh['dp'=8,'seq'=32] {'seq'}, dimensions={0} | all-to-all | bytes 524288 | tf_op jit(solution)/shard_map/all_to_all | solution.py:322
  90.4 5.6 %collective-permute-start.17 = (f32[32,128]{1,0:T(8,128)S(1)}, f32[32,128]{1,0:T(8,128)S(1)}, u32[]{:S(2)}, u32[]{:S(2)}) collective-permute-start(f32[32,128]{1,0:T(8,128)S(1)} %broadcast_multiply_fusion), channel_id=1, source_target_pairs={{0,0},{1,1},{2,2},{3,3},{4,32},{5,33},{6,34},{7,35},{8,64},{9,65},... | collective-permute-start | bytes 49160 | tf_op jit(solution)/shard_map/ppermute | solution.py:332
  96.1 6.3 %collective-permute-done.17 = f32[32,128]{1,0:T(8,128)S(1)} collective-permute-done((f32[32,128]{1,0:T(8,128)S(1)}, f32[32,128]{1,0:T(8,128)S(1)}, u32[]{:S(2)}, u32[]{:S(2)}) %collective-permute-start.17) | collective-permute-done | bytes 16416 | tf_op jit(solution)/shard_map/ppermute | solution.py:332
  (45 shorter events, 4.7 us)
Async XLA Ops:
  0.6 25.8 %copy-start.5 = (bf16[1,128,1024]{2,1,0:T(8,128)(2,1)S(1)}, bf16[1,128,1024]{2,1,0:T(8,128)(2,1)}, u32[]{:S(2)}) copy-start(bf16[1,128,1024]{2,1,0:T(8,128)(2,1)} %param.12) | copy-start | bytes 786436
  2.6 17.2 %collective-permute-start = (bf16[1040,128]{1,0:T(8,128)(2,1)}, bf16[1040,128]{1,0:T(8,128)(2,1)S(1)}, u32[]{:S(2)}, u32[]{:S(2)}) collective-permute-start(bf16[1040,128]{1,0:T(8,128)(2,1)} %layer_norm.1.own_ref), channel_id=1, source_target_pairs={{0,1},{1,2},{2,3},{3,4},{4,5},{5,6},{6,7},{7,8},{8,9},{9,10},{10,1... | collective-permute-start | bytes 798728 | tf_op jit(solution)/shard_map/ppermute | solution.py:28
  4.2 15.6 %collective-permute-start.1 = (bf16[1040,128]{1,0:T(8,128)(2,1)}, bf16[1040,128]{1,0:T(8,128)(2,1)S(1)}, u32[]{:S(2)}, u32[]{:S(2)}) collective-permute-start(bf16[1040,128]{1,0:T(8,128)(2,1)} %layer_norm.1.own_ref), channel_id=1, source_target_pairs={{0,31},{1,0},{2,1},{3,2},{4,3},{5,4},{6,5},{7,6},{8,7},{9,8},{10,9... | collective-permute-start | bytes 798728 | tf_op jit(solution)/shard_map/ppermute | solution.py:28
  10.9 9.3 %collective-permute-start.2 = (bf16[1040,128]{1,0:T(8,128)(2,1)}, bf16[1040,128]{1,0:T(8,128)(2,1)S(1)}, u32[]{:S(2)}, u32[]{:S(2)}) collective-permute-start(bf16[1040,128]{1,0:T(8,128)(2,1)} %layer_norm.1.own_ref), channel_id=1, source_target_pairs={{0,4},{1,5},{2,6},{3,7},{4,8},{5,9},{6,10},{7,11},{8,12},{9,13},{1... | collective-permute-start | bytes 798728 | tf_op jit(solution)/shard_map/ppermute | solution.py:28
  10.9 11.7 %collective-permute-start.3 = (bf16[1040,128]{1,0:T(8,128)(2,1)}, bf16[1040,128]{1,0:T(8,128)(2,1)S(1)}, u32[]{:S(2)}, u32[]{:S(2)}) collective-permute-start(bf16[1040,128]{1,0:T(8,128)(2,1)} %layer_norm.1.own_ref), channel_id=1, source_target_pairs={{0,28},{1,29},{2,30},{3,31},{4,0},{5,1},{6,2},{7,3},{8,4},{9,5},{1... | collective-permute-start | bytes 798728 | tf_op jit(solution)/shard_map/ppermute | solution.py:28
  17.9 23.1 %copy-start.2 = (bf16[1040,128]{1,0:T(8,128)(2,1)S(1)}, bf16[1040,128]{1,0:T(8,128)(2,1)}, u32[]{:S(2)}) copy-start(bf16[1040,128]{1,0:T(8,128)(2,1)} %layer_norm.1.own_ref) | copy-start | bytes 798724
  22.6 23.4 %collective-permute-start.6 = (bf16[2080,128]{1,0:T(8,128)(2,1)S(1)}, bf16[2080,128]{1,0:T(8,128)(2,1)S(1)}, u32[]{:S(2)}, u32[]{:S(2)}) collective-permute-start(bf16[2080,128]{1,0:T(8,128)(2,1)S(1)} %constant_dynamic-update-slice_fusion), channel_id=1, source_target_pairs={{0,4},{1,5},{2,6},{3,7},{4,8},{5,9},{6,10},{7,11},{8,12},{9,13},{1... | collective-permute-start | bytes 1597448 | tf_op jit(solution)/shard_map/ppermute | solution.py:28
  22.7 23.3 %collective-permute-start.7 = (bf16[2080,128]{1,0:T(8,128)(2,1)S(1)}, bf16[2080,128]{1,0:T(8,128)(2,1)S(1)}, u32[]{:S(2)}, u32[]{:S(2)}) collective-permute-start(bf16[2080,128]{1,0:T(8,128)(2,1)S(1)} %constant_dynamic-update-slice_fusion), channel_id=1, source_target_pairs={{0,28},{1,29},{2,30},{3,31},{4,0},{5,1},{6,2},{7,3},{8,4},{9,5},{1... | collective-permute-start | bytes 1597448 | tf_op jit(solution)/shard_map/ppermute | solution.py:28
  26.4 9.3 %collective-permute-start.10 = (bf16[128,1024]{1,0:T(8,128)(2,1)S(1)}, bf16[128,1024]{1,0:T(8,128)(2,1)S(1)}, u32[]{:S(2)}, u32[]{:S(2)}) collective-permute-start(bf16[128,1024]{1,0:T(8,128)(2,1)S(1)} %bitcast.13), channel_id=1, source_target_pairs={{0,64},{32,96},{64,128},{96,160},{128,192},{160,224},{192,0},{224,... | collective-permute-start | bytes 786440 | tf_op jit(solution)/shard_map/ppermute | solution.py:270
  27.6 11.3 %collective-permute-start.11 = (bf16[128,1024]{1,0:T(8,128)(2,1)S(1)}, bf16[128,1024]{1,0:T(8,128)(2,1)S(1)}, u32[]{:S(2)}, u32[]{:S(2)}) collective-permute-start(bf16[128,1024]{1,0:T(8,128)(2,1)S(1)} %bitcast.14), channel_id=1, source_target_pairs={{0,128},{32,160},{64,192},{96,224},{128,0},{160,32},{192,64},{224,... | collective-permute-start | bytes 786440 | tf_op jit(solution)/shard_map/ppermute | solution.py:270
  28.4 12.6 %collective-permute-start.12 = (bf16[128,1024]{1,0:T(8,128)(2,1)S(1)}, bf16[128,1024]{1,0:T(8,128)(2,1)S(1)}, u32[]{:S(2)}, u32[]{:S(2)}) collective-permute-start(bf16[128,1024]{1,0:T(8,128)(2,1)S(1)} %bitcast.15), channel_id=1, source_target_pairs={{0,192},{32,224},{64,0},{96,32},{128,64},{160,96},{192,128},{224,1... | collective-permute-start | bytes 786440 | tf_op jit(solution)/shard_map/ppermute | solution.py:270
  35.7 9.7 %collective-permute-start.4 = (bf16[1040,128]{1,0:T(8,128)(2,1)S(1)}, bf16[1040,128]{1,0:T(8,128)(2,1)S(1)}, u32[]{:S(2)}, u32[]{:S(2)}) collective-permute-start(bf16[1040,128]{1,0:T(8,128)(2,1)S(1)} %collective-permute-done.refs_0_), channel_id=1, source_target_pairs={{0,1},{1,2},{2,3},{3,4},{4,5},{5,6},{6,7},{7,8},{8,9},{9,10},{10,1... | collective-permute-start | bytes 798728 | tf_op jit(solution)/shard_map/ppermute | solution.py:28
  38.9 7.0 %collective-permute-start.5 = (bf16[1040,128]{1,0:T(8,128)(2,1)S(1)}, bf16[1040,128]{1,0:T(8,128)(2,1)S(1)}, u32[]{:S(2)}, u32[]{:S(2)}) collective-permute-start(bf16[1040,128]{1,0:T(8,128)(2,1)S(1)} %collective-permute-done.1.refs_2_), channel_id=1, source_target_pairs={{0,31},{1,0},{2,1},{3,2},{4,3},{5,4},{6,5},{7,6},{8,7},{9,8},{10,9... | collective-permute-start | bytes 798728 | tf_op jit(solution)/shard_map/ppermute | solution.py:28
  41.0 22.9 %collective-permute-start.13 = (bf16[128,1024]{1,0:T(8,128)(2,1)S(1)}, bf16[128,1024]{1,0:T(8,128)(2,1)S(1)}, u32[]{:S(2)}, u32[]{:S(2)}) collective-permute-start(bf16[128,1024]{1,0:T(8,128)(2,1)S(1)} %bitcast.16), channel_id=1, source_target_pairs={{0,32},{32,0},{64,96},{96,64},{128,160},{160,128},{192,224},{224,1... | collective-permute-start | bytes 786440 | tf_op jit(solution)/shard_map/ppermute | solution.py:274
  45.4 18.5 %collective-permute-start.14 = (bf16[128,1024]{1,0:T(8,128)(2,1)S(1)}, bf16[128,1024]{1,0:T(8,128)(2,1)S(1)}, u32[]{:S(2)}, u32[]{:S(2)}) collective-permute-start(bf16[128,1024]{1,0:T(8,128)(2,1)S(1)} %collective-permute-done.10.refs_1_), channel_id=1, source_target_pairs={{0,32},{32,0},{64,96},{96,64},{128,160},{160,128},{192,224},{224,1... | collective-permute-start | bytes 786440 | tf_op jit(solution)/shard_map/ppermute | solution.py:274
  45.9 17.9 %collective-permute-start.15 = (bf16[128,1024]{1,0:T(8,128)(2,1)S(1)}, bf16[128,1024]{1,0:T(8,128)(2,1)S(1)}, u32[]{:S(2)}, u32[]{:S(2)}) collective-permute-start(bf16[128,1024]{1,0:T(8,128)(2,1)S(1)} %collective-permute-done.11.refs_2_), channel_id=1, source_target_pairs={{0,32},{32,0},{64,96},{96,64},{128,160},{160,128},{192,224},{224,1... | collective-permute-start | bytes 786440 | tf_op jit(solution)/shard_map/ppermute | solution.py:274
  46.1 9.9 %collective-permute-start.8 = (bf16[1040,128]{1,0:T(8,128)(2,1)S(1)}, bf16[1040,128]{1,0:T(8,128)(2,1)S(1)}, u32[]{:S(2)}, u32[]{:S(2)}) collective-permute-start(bf16[1040,128]{1,0:T(8,128)(2,1)S(1)} %collective-permute-done.4.refs_0_), channel_id=1, source_target_pairs={{0,4},{1,5},{2,6},{3,7},{4,8},{5,9},{6,10},{7,11},{8,12},{9,13},{1... | collective-permute-start | bytes 798728 | tf_op jit(solution)/shard_map/ppermute | solution.py:28
  46.2 9.8 %collective-permute-start.9 = (bf16[1040,128]{1,0:T(8,128)(2,1)S(1)}, bf16[1040,128]{1,0:T(8,128)(2,1)S(1)}, u32[]{:S(2)}, u32[]{:S(2)}) collective-permute-start(bf16[1040,128]{1,0:T(8,128)(2,1)S(1)} %collective-permute-done.5.refs_1_), channel_id=1, source_target_pairs={{0,28},{1,29},{2,30},{3,31},{4,0},{5,1},{6,2},{7,3},{8,4},{9,5},{1... | collective-permute-start | bytes 798728 | tf_op jit(solution)/shard_map/ppermute | solution.py:28
  49.3 6.7 %slice-start = ((s8[6291456]{0:T(1024)(128)(4,1)}), s8[4194304]{0:T(1024)(128)(4,1)S(1)}, s32[]{:S(2)}) async-start(s8[6291456]{0:T(1024)(128)(4,1)} %bitcast.8), calls=%async_computation.2 | async-start | bytes 8388608
  51.9 4.1 %copy-start.3 = (bf16[1024,1024]{1,0:T(8,128)(2,1)S(1)}, bf16[1024,1024]{1,0:T(8,128)(2,1)}, u32[]{:S(2)}) copy-start(bf16[1024,1024]{1,0:T(8,128)(2,1)} %refs_8_.1) | copy-start | bytes 6291460
  51.9 4.1 %copy-start.4 = (bf16[1,128,1024]{2,1,0:T(8,128)(2,1)S(1)}, bf16[1,128,1024]{2,1,0:T(8,128)(2,1)}, u32[]{:S(2)}) copy-start(bf16[1,128,1024]{2,1,0:T(8,128)(2,1)} %param.7) | copy-start | bytes 786436
  56.0 7.9 %collective-permute-start.16 = (bf16[128,1024]{1,0:T(8,128)(2,1)S(1)}, bf16[128,1024]{1,0:T(8,128)(2,1)S(1)}, u32[]{:S(2)}, u32[]{:S(2)}) collective-permute-start(bf16[128,1024]{1,0:T(8,128)(2,1)S(1)} %collective-permute-done.12.refs_3_), channel_id=1, source_target_pairs={{0,32},{32,0},{64,96},{96,64},{128,160},{160,128},{192,224},{224,1... | collective-permute-start | bytes 786440 | tf_op jit(solution)/shard_map/ppermute | solution.py:274
  57.6 9.9 %all-to-all-start = ((bf16[8,128,128]{2,1,0:T(8,128)(2,1)}), bf16[8,128,128]{2,1,0:T(8,128)(2,1)S(1)}, u32[]{:S(2)}, u32[]{:S(2)}) async-start(bf16[8,128,128]{2,1,0:T(8,128)(2,1)} %bitcast.4), calls=%async_computation | async-start | bytes 524288 | tf_op jit(solution)/shard_map/all_to_all | solution.py:319
  90.4 11.9 %collective-permute-start.17 = (f32[32,128]{1,0:T(8,128)S(1)}, f32[32,128]{1,0:T(8,128)S(1)}, u32[]{:S(2)}, u32[]{:S(2)}) collective-permute-start(f32[32,128]{1,0:T(8,128)S(1)} %broadcast_multiply_fusion), channel_id=1, source_target_pairs={{0,0},{1,1},{2,2},{3,3},{4,32},{5,33},{6,34},{7,35},{8,64},{9,65},... | collective-permute-start | bytes 49160 | tf_op jit(solution)/shard_map/ppermute | solution.py:332
  (3 other events, 7.9 us)

commit v4 on v2

--- a/solution.py
+++ b/solution.py
@@ -3,7 +3,7 @@
 from jax import lax
 from jax.experimental import pallas as pl
 from jax.experimental.pallas import tpu as pltpu
-from jax.sharding import PartitionSpec as P
+from jax.sharding import Mesh, PartitionSpec as P
 
 ROWS = 128
 LANES = 128
@@ -13,8 +13,12 @@
 PACKED = WIDTH + 16
 QUAD = 256
 QUADS = WIDTH // QUAD
+SEQ = ("z", "y")
 NEG_BIG = -1e30
 EPSILON = 1e-05
+N_SEQ = 32
+N_Y = 4
+N_CORE = 2
 LOG2E = 1.4426950408889634
 AHEAD = 2
 F32 = jnp.float32
@@ -23,12 +27,27 @@
 
 
 def shifted(block, distance):
-    n_seq = lax.axis_size("seq")
+    n_seq = lax.axis_size(SEQ)
     route = [(i, (i + distance) % n_seq) for i in range(n_seq)]
-    return lax.ppermute(block, "seq", route)
-
-
-def norm_kernel(frames_ref, ids_ref, gain_ref, packed_ref):
+    return lax.ppermute(block, SEQ, route)
+
+
+def core_swapped(block):
+    return lax.ppermute(block, "core", [(0, 1), (1, 0)])
+
+
+def turned(block, distance):
+    n = lax.axis_size("y")
+    return lax.ppermute(block, "y", [(i, (i + distance) % n) for i in range(n)])
+
+
+def gathered_order():
+    n = lax.axis_size("y")
+    table = [[(place + n - d) % n for d in range(n)] for place in range(n)]
+    return lax.dynamic_index_in_dim(jnp.asarray(table, jnp.int32), lax.axis_index("y"), 0, False)
+
+
+def norm_kernel(core_ref, frames_ref, ids_ref, gain_ref, cotangent_ref, packed_ref, mine_ref, theirs_ref):
     float_frames = frames_ref[...].astype(F32)
     average = jnp.mean(float_frames, axis=-1, keepdims=True)
     centered = float_frames - average
@@ -38,15 +57,25 @@
         packed_ref[c * ROWS : (c + 1) * ROWS, :] = normed[:, c * LANES : (c + 1) * LANES]
     ids = (ids_ref[...] + 1).astype(F32)
     packed_ref[WIDTH:PACKED, :] = jnp.broadcast_to(ids, (16, LANES)).astype(BF16)
-
-
-def normalize(frames, ids, gain):
+    first = core_ref[0] == 0
+    for c in range(CHUNKS // 2):
+        even = cotangent_ref[:, 2 * c * LANES : (2 * c + 1) * LANES]
+        odd = cotangent_ref[:, (2 * c + 1) * LANES : (2 * c + 2) * LANES]
+        at = slice(c * LANES, (c + 1) * LANES)
+        mine_ref[:, at] = jnp.where(first, even, odd)
+        theirs_ref[:, at] = jnp.where(first, odd, even)
+
+
+def normalize(core, frames, ids, gain, cotangent):
+    vmem = pl.BlockSpec(memory_space=pltpu.VMEM)
+    half = jax.ShapeDtypeStruct((ROWS, WIDTH // 2), BF16)
     return pl.pallas_call(
         norm_kernel,
-        out_shape=jax.ShapeDtypeStruct((PACKED, LANES), BF16),
+        in_specs=[pl.BlockSpec(memory_space=pltpu.SMEM), vmem, vmem, vmem, vmem],
+        out_shape=[jax.ShapeDtypeStruct((PACKED, LANES), BF16), half, half],
         compiler_params=pltpu.CompilerParams(vmem_limit_bytes=60 * 1024 * 1024),
         name="layer_norm",
-    )(frames, ids, gain)
+    )(core, frames, ids, gain, cotangent)
 
 
 def unpacked(block):
@@ -220,19 +249,25 @@
             own_ref, located(block_refs, left), located(block_refs, right), queries_ref, weight_ref, state_refs
         )
         _, sums_ref, acc_ref = state_refs
-        for h in range(2 * CHUNKS):
-            rows = slice(h * HALF, (h + 1) * HALF)
-            attended_ref[rows, :] = (acc_ref[rows, :] / sums_ref[h : h + 1, :]).astype(BF16)
-        attended = jnp.concatenate(
-            [jnp.transpose(attended_ref[c * LANES : (c + 1) * LANES, :]) for c in range(CHUNKS)], axis=1
-        )
+        n_y, rows = attended_ref.shape[0], WIDTH // N_SEQ
+        chunks = []
+        for c in range(CHUNKS):
+            parts = []
+            for h in (2 * c, 2 * c + 1):
+                parts.append((acc_ref[h * HALF : (h + 1) * HALF, :] / sums_ref[h : h + 1, :]).astype(BF16))
+            chunk = jnp.concatenate(parts, axis=0)
+            for k in range(LANES // rows):
+                z, y = divmod(c * (LANES // rows) + k, n_y)
+                attended_ref[y, z * rows : (z + 1) * rows, :] = chunk[k * rows : (k + 1) * rows, :]
+            chunks.append(jnp.transpose(chunk))
+        attended = jnp.concatenate(chunks, axis=1)
         product = jnp.dot(attended, wout_ref[...], preferred_element_type=F32)
         out_ref[...] = (frames_ref[...].astype(F32) + product).astype(BF16)
 
     return pl.pallas_call(
         kernel,
         out_shape=[
-            jax.ShapeDtypeStruct((WIDTH, LANES), BF16),
+            jax.ShapeDtypeStruct((N_Y, WIDTH // N_Y, LANES), BF16),
             jax.ShapeDtypeStruct((ROWS, WIDTH), BF16),
         ],
         scratch_shapes=[pltpu.VMEM(shape.shape, F32) for shape in STATE_SHAPES],
@@ -242,53 +277,53 @@
     )(own, *blocks, queries, w_qkv, *state, frames, w_out)
 
 
-def grad_kernel(attended_ref, cotangent_ref, out_ref):
-    attended = jnp.concatenate([attended_ref[p] for p in range(CHUNKS)], axis=1)
-    product = jnp.dot(attended, cotangent_ref[...], preferred_element_type=F32).astype(BF16)
+def grad_kernel(order_ref, own_ref, other_ref, *refs):
+    grads, out_ref = refs[:-1], refs[-1]
+    count = len(grads)
+    attended = [ref[order_ref[i]] for i in range(count) for ref in (own_ref, other_ref)]
+    attended = jnp.concatenate(attended, axis=1)
     for half in range(2):
-        out_ref[half] = product[:, half * LANES : (half + 1) * LANES]
-
-
-def grad_product(attended, cotangent):
+        at = slice(half * QUAD, (half + 1) * QUAD)
+        block = jnp.concatenate([ref[:, at] for ref in grads], axis=0)
+        product = jnp.dot(attended, block, preferred_element_type=F32).astype(BF16)
+        for k in range(2):
+            out_ref[2 * half + k] = product[:, k * LANES : (k + 1) * LANES]
+
+
+def grad_product(order, own, other, grads):
+    vmem = pl.BlockSpec(memory_space=pltpu.VMEM)
+    rows, columns = own.shape[1], grads[0].shape[1]
     return pl.pallas_call(
         grad_kernel,
-        grid=(QUADS,),
-        in_specs=[
-            pl.BlockSpec((CHUNKS, LANES, ROWS), lambda j: (0, 0, 0)),
-            pl.BlockSpec((CHUNKS * ROWS, QUAD), lambda j: (0, j)),
-        ],
-        out_specs=pl.BlockSpec((2, LANES, LANES), lambda j: (j, 0, 0)),
-        out_shape=jax.ShapeDtypeStruct((CHUNKS, LANES, LANES), BF16),
+        in_specs=[pl.BlockSpec(memory_space=pltpu.SMEM)] + [vmem] * (2 + len(grads)),
+        out_shape=jax.ShapeDtypeStruct((columns // LANES, rows, LANES), BF16),
         compiler_params=LIMIT,
         name="grad_product",
-    )(attended, cotangent)
+    )(order, own, other, *grads)
 
 
 def local(frames, segment_ids, norm_gain, w_qkv, w_out, cotangent):
-    n_dp = lax.axis_size("dp")
-    n_seq = lax.axis_size("seq")
+    n_y = lax.axis_size("y")
     frames = frames[0]
-    own = normalize(frames, segment_ids, norm_gain[None, :])
+    core = lax.axis_index("core").astype(jnp.int32).reshape(1)
+    own, mine, theirs = normalize(core, frames, segment_ids, norm_gain[None, :], cotangent[0])
 
     left1, right1 = shifted(own, 1), shifted(own, -1)
     left4, right4 = shifted(own, 4), shifted(own, -4)
+    received = core_swapped(theirs)
     queries, *state = own_block(own, w_qkv)
-    left1, right1, left4, right4, queries = lax.optimization_barrier(
-        (left1, right1, left4, right4, queries)
-    )
+    left1, right1, queries = lax.optimization_barrier((left1, right1, queries))
     near = jnp.concatenate([left1, right1], axis=0)
+    left2, right2 = shifted(left1, 1), shifted(right1, -1)
     left_two, right_two = shifted(near, 4), shifted(near, -4)
-    left2, right2 = shifted(left1, 1), shifted(right1, -1)
-    cotangent, near = lax.optimization_barrier((cotangent, near))
-    copies = jnp.broadcast_to(cotangent, (n_dp, *cotangent.shape[1:]))
-    all_grads = lax.all_to_all(copies, "dp", 0, 0, tiled=True).reshape(n_dp * ROWS, WIDTH)
-
     state = absorb_stage(
         own, (left1, left4, right1, right4), ((0, 0), (1, 0)), ((2, 0), (3, 0)), queries, w_qkv, state
     )
+    both = jnp.concatenate([mine, received], axis=0)
+    both, left2, right2, *state = lax.optimization_barrier((both, left2, right2, *state))
+    left6, right6 = shifted(left2, 4), shifted(right2, -4)
+    grads = [both, *[turned(both, d) for d in range(1, n_y)]]
     state = absorb_stage(own, (left2, right2), ((0, 0),), ((1, 0),), queries, w_qkv, state)
-    left2, right2, left_two, right_two = lax.optimization_barrier((left2, right2, left_two, right_two))
-    left6, right6 = shifted(left2, 4), shifted(right2, -4)
     state = absorb_stage(
         own, (left_two, right_two), ((0, 1), (0, 0)), ((1, 0), (1, 1)), queries, w_qkv, state
     )
@@ -296,28 +331,22 @@
         own, (left6, right6), ((0, 0),), ((1, 0),), queries, w_qkv, state, frames, w_out
     )
 
-    pieces = lax.all_to_all(attended, "dp", 0, 0, tiled=True).reshape(n_dp, LANES, ROWS)
-    share = grad_product(pieces, all_grads)
-    rows = LANES * CHUNKS // n_seq
-    parts = lax.all_to_all(share.reshape(n_seq, rows, LANES), "seq", 0, 0, tiled=True)
-    grad_scale = (n_dp * n_seq * ROWS) ** (-0.5)
-    block = jnp.sum(parts.astype(F32), axis=0) * grad_scale
-    inner = n_seq // n_dp
-    route = [
-        (p * n_seq + q * inner + r, q * n_seq + p * inner + r)
-        for p in range(n_dp)
-        for q in range(n_dp)
-        for r in range(inner)
-    ]
-    return (block_out[None], lax.ppermute(block, ("dp", "seq"), route))
+    pieces = lax.all_to_all(attended, "y", 0, 0, tiled=True)
+    share = grad_product(gathered_order(), pieces, core_swapped(pieces), grads)
+    parts = lax.all_to_all(share.reshape(-1, WIDTH // N_SEQ, LANES), ("x", "z"), 0, 0, tiled=True)
+    grad_scale = (lax.axis_size(("x", "core")) * N_SEQ * ROWS) ** (-0.5)
+    return (block_out[None], jnp.sum(parts.astype(F32), axis=0) * grad_scale)
 
 
 def solution(mesh):
-    placed = (P("dp", "seq", None), P("dp", "seq"), P(), P(), P(), P("dp", "seq", None))
+    shape = (mesh.shape["dp"] // N_CORE, N_CORE, N_SEQ // N_Y, N_Y)
+    chips = Mesh(mesh.devices.reshape(shape), ("x", "core", "z", "y"))
+    groups = ("x", "core")
+    placed = (P(groups, SEQ, None), P(groups, SEQ), P(), P(), P(), P(groups, SEQ, None))
     return jax.shard_map(
         local,
-        mesh=mesh,
+        mesh=chips,
         in_specs=placed,
-        out_specs=(P("dp", "seq", None), P("seq", "dp")),
+        out_specs=(P(groups, SEQ, None), P(SEQ, groups)),
         check_vma=False,
     )

time: 129 us -> 94.4 us (0.73); the launches traced: 130 us -> 93 us
  blocking collectives: 47.1 us -> 18.3 us
  starting transfers between devices: 37 us -> 31.8 us
  Pallas kernels: 13.2 us -> 10.7 us
    all_to_all x2 -> x1, blocking collectives: 47.1 us -> 18.3 us  [local(): lax.all_to_all(share.reshape(-1, WIDTH // N_SEQ, LANES), ('x', 'z'), 0, 0...]
    all_to_all x1, starting transfers between devices: 9.01 us -> 3.4 us  [local(): pieces = lax.all_to_all(attended, 'y', 0, 0, tiled=True)]
    all_to_all x1, waiting for transfers between devices: 4.38 us -> 1.94 us  [local(): pieces = lax.all_to_all(attended, 'y', 0, 0, tiled=True)]
    pallas_call x3, Pallas kernels: 6.82 us -> 4.43 us  [absorb_stage(): pl.pallas_call(kernel, out_shape=list(STATE_SHAPES), compiler_params=LIMI...]
    ppermute x11 -> x15, waiting for transfers between devices: 22 us -> 24.2 us  [the longest x10 14.8 us: shifted(): return lax.ppermute(block, SEQ, route)]
    unnamed x18 -> x17, local copies, waits for them, and re-layouts: 4.77 us -> 3.79 us
    ppermute x11 -> x15, starting transfers between devices: 28 us -> 28.4 us  [the longest x10 22.2 us: shifted(): return lax.ppermute(block, SEQ, route)]
  transfers between devices with their start and end apart: 12 -> 16, of which waited for: 6 -> 5; matrix products, arithmetic and copies ran while one was open for 0% -> 1% of each run, Pallas kernels for 7% -> 7%
where the time goes in v4:
time: 94.4 us; the launch traced here: 93 us
  starting transfers between devices  31.8 us (34%)
  waiting for transfers between devices  26.1 us (28%)
  blocking collectives  18.3 us (19%)
  Pallas kernels  10.7 us (11%)
  local copies, waits for them, and re-layouts  4.51 us (5%)
    ppermute x10, starting transfers between devices, shifted(): return lax.ppermute(block, SEQ, route)  22.2 us
    all_to_all x1, blocking collectives, local(): lax.all_to_all(share.reshape(-1, WIDTH // N_SEQ, LANES), ('x', 'z'), 0, 0...  18.3 us
    ppermute x10, waiting for transfers between devices, shifted(): return lax.ppermute(block, SEQ, route)  14.8 us
    ppermute x3, waiting for transfers between devices, turned(): return lax.ppermute(block, 'y', [(i, (i + distance) % n) for i in range(n)])  9.35 us
    ppermute x3, starting transfers between devices, turned(): return lax.ppermute(block, 'y', [(i, (i + distance) % n) for i in range(n)])  6.15 us
    pallas_call x3, Pallas kernels, absorb_stage(): pl.pallas_call(kernel, out_shape=list(STATE_SHAPES), compiler_params=LIMI...  4.43 us
    unnamed x17, local copies, waits for them, and re-layouts  3.79 us
    all_to_all x1, starting transfers between devices, local(): pieces = lax.all_to_all(attended, 'y', 0, 0, tiled=True)  3.4 us
  transfers between devices with their start and end apart: 16, of which 5 were waited for; matrix products, arithmetic and copies ran while one was open for 1% of the time, Pallas kernels for 7%

profile of v4, /device:TPU:4, one launch (start us, length us, event | category | flops | bytes accessed | tf_op | source)
XLA Modules:
  0.0 93.0 jit_solution(3137109172647526550)
XLA Ops:
  0.6 2.1 %layer_norm.1 = (bf16[1040,128]{1,0:T(8,128)(2,1)}, bf16[128,512]{1,0:T(8,128)(2,1)}, bf16[128,512]{1,0:T(8,128)(2,1)}) custom-call(s32[1]{0:T(128)} %bitcast.core_ref, bf16[128,1024]{1,0:T(8,128)(2,1)} %bitcast.10, s32[1,128]{1,0:T(1,128)} %ids_ref.1, f32[1,1024]{1,0:T(1,128)} %bitcast.14, bf16[128,1024]{1,0:T(8,128)(2,1)} %bitcast.13), custom_call_target="tpu_custom_call" | custom-call | tf_op jit(solution)/shard_map/layer_norm/pallas_call | solution.py:72
  2.8 1.6 %collective-permute-start.1 = (bf16[1040,128]{1,0:T(8,128)(2,1)}, bf16[1040,128]{1,0:T(8,128)(2,1)S(1)}, u32[]{:S(2)}, u32[]{:S(2)}) collective-permute-start(bf16[1040,128]{1,0:T(8,128)(2,1)} %get-tuple-element.29.own_ref), channel_id=1, source_target_pairs={{0,1},{1,2},{2,3},{3,4},{4,5},{5,6},{6,7},{7,8},{8,9},{9,10},{10,1... | collective-permute-start | bytes 798728 | tf_op jit(solution)/shard_map/ppermute | solution.py:32
  4.3 6.7 %collective-permute-start.2 = (bf16[1040,128]{1,0:T(8,128)(2,1)}, bf16[1040,128]{1,0:T(8,128)(2,1)S(1)}, u32[]{:S(2)}, u32[]{:S(2)}) collective-permute-start(bf16[1040,128]{1,0:T(8,128)(2,1)} %get-tuple-element.29.own_ref), channel_id=1, source_target_pairs={{0,31},{1,0},{2,1},{3,2},{4,3},{5,4},{6,5},{7,6},{8,7},{9,8},{10,9... | collective-permute-start | bytes 798728 | tf_op jit(solution)/shard_map/ppermute | solution.py:32
  11.1 3.2 %collective-permute-start.6 = (bf16[1040,128]{1,0:T(8,128)(2,1)}, bf16[1040,128]{1,0:T(8,128)(2,1)S(1)}, u32[]{:S(2)}, u32[]{:S(2)}) collective-permute-start(bf16[1040,128]{1,0:T(8,128)(2,1)} %get-tuple-element.29.own_ref), channel_id=1, source_target_pairs={{0,28},{1,29},{2,30},{3,31},{4,0},{5,1},{6,2},{7,3},{8,4},{9,5},{1... | collective-permute-start | bytes 798728 | tf_op jit(solution)/shard_map/ppermute | solution.py:32
  14.3 2.8 %copy-done = bf16[1024,3072]{1,0:T(8,128)(2,1)S(1)} copy-done((bf16[1024,3072]{1,0:T(8,128)(2,1)S(1)}, bf16[1024,3072]{1,0:T(8,128)(2,1)}, u32[]{:S(2)}) %copy-start) | copy-done | bytes 6291480
  17.1 0.9 %copy-done.1 = bf16[1040,128]{1,0:T(8,128)(2,1)S(1)} copy-done((bf16[1040,128]{1,0:T(8,128)(2,1)S(1)}, bf16[1040,128]{1,0:T(8,128)(2,1)}, u32[]{:S(2)}) %copy-start.1) | copy-done | bytes 266264
  18.0 1.9 %own_block.1 = (bf16[8,128,256]{2,1,0:T(8,128)(2,1)S(1)}, f32[16,128]{1,0:T(8,128)S(1)}, f32[16,128]{1,0:T(8,128)S(1)}, f32[1024,128]{1,0:T(8,128)S(1)}) custom-call(bf16[1040,128]{1,0:T(8,128)(2,1)S(1)} %copy-done.1, bf16[1024,3072]{1,0:T(8,128)(2,1)S(1)} %copy-done), custom_call_target="tpu_custom_call" | custom-call | flops 1610612736 | bytes 8388608 | tf_op jit(solution)/shard_map/own_block/pallas_call | solution.py:189
  20.6 1.6 %collective-permute-start.9 = (bf16[2080,128]{1,0:T(8,128)(2,1)S(1)}, bf16[2080,128]{1,0:T(8,128)(2,1)S(1)}, u32[]{:S(2)}, u32[]{:S(2)}) collective-permute-start(bf16[2080,128]{1,0:T(8,128)(2,1)S(1)} %constant_dynamic-update-slice_fusion), channel_id=1, source_target_pairs={{0,4},{1,5},{2,6},{3,7},{4,8},{5,9},{6,10},{7,11},{8,12},{9,13},{1... | collective-permute-start | bytes 1597448 | tf_op jit(solution)/shard_map/ppermute | solution.py:32
  22.1 5.3 %collective-permute-start.4 = (bf16[1040,128]{1,0:T(8,128)(2,1)S(1)}, bf16[1040,128]{1,0:T(8,128)(2,1)S(1)}, u32[]{:S(2)}, u32[]{:S(2)}) collective-permute-start(bf16[1040,128]{1,0:T(8,128)(2,1)S(1)} %collective-permute-done.2.refs_2_), channel_id=1, source_target_pairs={{0,31},{1,0},{2,1},{3,2},{4,3},{5,4},{6,5},{7,6},{8,7},{9,8},{10,9... | collective-permute-start | bytes 798728 | tf_op jit(solution)/shard_map/ppermute | solution.py:32
  27.5 4.2 %absorb_stage.3 = (f32[16,128]{1,0:T(8,128)S(1)}, f32[16,128]{1,0:T(8,128)S(1)}, f32[1024,128]{1,0:T(8,128)S(1)}) custom-call(bf16[1040,128]{1,0:T(8,128)(2,1)S(1)} %copy-done.1, bf16[1040,128]{1,0:T(8,128)(2,1)S(1)} %collective-permute-done.1.refs_0_, bf16[1040,128]{1,0:T(8,128)(2,1)S(1)} %collective-permute-done.5.refs_1_, ...), custom_call_target="tpu_custom_call" | custom-call | flops 2147483648 | bytes 8388608 | tf_op jit(solution)/shard_map/absorb_stage/pallas_call | solution.py:230
  31.7 10.8 %collective-permute-done.3.refs_0_ = bf16[1040,128]{1,0:T(8,128)(2,1)S(1)} collective-permute-done((bf16[1040,128]{1,0:T(8,128)(2,1)S(1)}, bf16[1040,128]{1,0:T(8,128)(2,1)S(1)}, u32[]{:S(2)}, u32[]{:S(2)}) %collective-permute-start.3) | collective-permute-done | bytes 266272 | tf_op jit(solution)/shard_map/ppermute | solution.py:32
  42.5 3.2 %collective-permute-start.8 = (bf16[1040,128]{1,0:T(8,128)(2,1)S(1)}, bf16[1040,128]{1,0:T(8,128)(2,1)S(1)}, u32[]{:S(2)}, u32[]{:S(2)}) collective-permute-start(bf16[1040,128]{1,0:T(8,128)(2,1)S(1)} %collective-permute-done.4.refs_1_), channel_id=1, source_target_pairs={{0,28},{1,29},{2,30},{3,31},{4,0},{5,1},{6,2},{7,3},{8,4},{9,5},{1... | collective-permute-start | bytes 798728 | tf_op jit(solution)/shard_map/ppermute | solution.py:32
  46.1 4.0 %collective-permute-done.7.refs_0_ = bf16[1040,128]{1,0:T(8,128)(2,1)S(1)} collective-permute-done((bf16[1040,128]{1,0:T(8,128)(2,1)S(1)}, bf16[1040,128]{1,0:T(8,128)(2,1)S(1)}, u32[]{:S(2)}, u32[]{:S(2)}) %collective-permute-start.7) | collective-permute-done | bytes 266272 | tf_op jit(solution)/shard_map/ppermute | solution.py:32
  50.2 1.3 %last_stage.1 = (bf16[4,256,128]{2,1,0:T(8,128)(2,1)}, bf16[128,1024]{1,0:T(8,128)(2,1)}) custom-call(bf16[1040,128]{1,0:T(8,128)(2,1)S(1)} %copy-done.2, bf16[1040,128]{1,0:T(8,128)(2,1)S(1)} %collective-permute-done.7.refs_0_, bf16[1040,128]{1,0:T(8,128)(2,1)S(1)} %collective-permute-done.8.refs_1_, ...), custom_call_target="tpu_custom_call" | custom-call | flops 1610612736 | bytes 10485760 | tf_op jit(solution)/shard_map/last_stage/pallas_call | solution.py:267
  51.5 3.4 %all-to-all-start = ((bf16[4,256,128]{2,1,0:T(8,128)(2,1)}), bf16[4,256,128]{2,1,0:T(8,128)(2,1)S(1)}, u32[]{:S(2)}, u32[]{:S(2)}) async-start(bf16[4,256,128]{2,1,0:T(8,128)(2,1)} %get-tuple-element.54), calls=%async_computation | async-start | bytes 524288 | tf_op jit(solution)/shard_map/all_to_all | solution.py:334
  54.9 2.0 %collective-permute-start.12 = (bf16[256,512]{1,0:T(8,128)(2,1)S(1)}, bf16[256,512]{1,0:T(8,128)(2,1)S(1)}, u32[]{:S(2)}, u32[]{:S(2)}) collective-permute-start(bf16[256,512]{1,0:T(8,128)(2,1)S(1)} %pad_maximum_fusion.refs_0_), channel_id=1, source_target_pairs={{0,1},{1,2},{2,3},{3,0},{4,5},{5,6},{6,7},{7,4},{8,9},{9,10},{10,1... | collective-permute-start | bytes 786440 | tf_op jit(solution)/shard_map/ppermute | solution.py:41
  56.9 2.7 %collective-permute-start.13 = (bf16[256,512]{1,0:T(8,128)(2,1)S(1)}, bf16[256,512]{1,0:T(8,128)(2,1)S(1)}, u32[]{:S(2)}, u32[]{:S(2)}) collective-permute-start(bf16[256,512]{1,0:T(8,128)(2,1)S(1)} %pad_maximum_fusion.refs_0_), channel_id=1, source_target_pairs={{0,2},{1,3},{2,0},{3,1},{4,6},{5,7},{6,4},{7,5},{8,10},{9,11},{10,... | collective-permute-start | bytes 786440 | tf_op jit(solution)/shard_map/ppermute | solution.py:41
  59.6 1.5 %collective-permute-start.14 = (bf16[256,512]{1,0:T(8,128)(2,1)S(1)}, bf16[256,512]{1,0:T(8,128)(2,1)S(1)}, u32[]{:S(2)}, u32[]{:S(2)}) collective-permute-start(bf16[256,512]{1,0:T(8,128)(2,1)S(1)} %pad_maximum_fusion.refs_0_), channel_id=1, source_target_pairs={{0,3},{1,0},{2,1},{3,2},{4,7},{5,4},{6,5},{7,6},{8,11},{9,8},{10,9... | collective-permute-start | bytes 786440 | tf_op jit(solution)/shard_map/ppermute | solution.py:41
  61.0 1.9 %all-to-all-done.own_ref = bf16[4,256,128]{2,1,0:T(8,128)(2,1)S(1)} async-done(((bf16[4,256,128]{2,1,0:T(8,128)(2,1)}), bf16[4,256,128]{2,1,0:T(8,128)(2,1)S(1)}, u32[]{:S(2)}, u32[]{:S(2)}) %all-to-all-start) | async-done | bytes 262176 | tf_op jit(solution)/shard_map/all_to_all | solution.py:334
  63.0 0.7 dynamic-slice_bitcast_fusion.order_ref
  63.7 4.3 %collective-permute-done.12.refs_1_ = bf16[256,512]{1,0:T(8,128)(2,1)S(1)} collective-permute-done((bf16[256,512]{1,0:T(8,128)(2,1)S(1)}, bf16[256,512]{1,0:T(8,128)(2,1)S(1)}, u32[]{:S(2)}, u32[]{:S(2)}) %collective-permute-start.12) | collective-permute-done | bytes 262176 | tf_op jit(solution)/shard_map/ppermute | solution.py:41
  68.0 5.0 %collective-permute-done.13.refs_2_ = bf16[256,512]{1,0:T(8,128)(2,1)S(1)} collective-permute-done((bf16[256,512]{1,0:T(8,128)(2,1)S(1)}, bf16[256,512]{1,0:T(8,128)(2,1)S(1)}, u32[]{:S(2)}, u32[]{:S(2)}) %collective-permute-start.13) | collective-permute-done | bytes 262176 | tf_op jit(solution)/shard_map/ppermute | solution.py:41
  73.0 1.0 %grad_product.1 = bf16[4,256,128]{2,1,0:T(8,128)(2,1)S(1)} custom-call(s32[4]{0:T(128)S(1)} %dynamic-slice_bitcast_fusion.order_ref, bf16[4,256,128]{2,1,0:T(8,128)(2,1)S(1)} %all-to-all-done.own_ref, bf16[4,256,128]{2,1,0:T(8,128)(2,1)S(1)} %collective-permute-done.11.other_ref, bf16[256,512]{1,0:T(8,128)(2,1)S(1)} %pad_maximum_fusion.refs_0_, ...), custom_call_target="tpu_custom_call" | custom-call | tf_op jit(solution)/shard_map/grad_product/pallas_call | solution.py:296
  74.0 18.3 %all_to_all.10 = bf16[32,32,128]{2,1,0:T(8,128)(2,1)S(1)} all-to-all(bf16[32,32,128]{2,1,0:T(8,128)(2,1)S(1)} %bitcast.12), channel_id=1, replica_groups=mesh['x'=4,'core'=2,'z'=8,'y'=4] {'x','z'}, dimensions={0} | all-to-all | bytes 524288 | tf_op jit(solution)/shard_map/all_to_all | solution.py:336
  (39 shorter events, 1.6 us)
Async XLA Ops:
  2.8 17.2 %collective-permute-start.1 = (bf16[1040,128]{1,0:T(8,128)(2,1)}, bf16[1040,128]{1,0:T(8,128)(2,1)S(1)}, u32[]{:S(2)}, u32[]{:S(2)}) collective-permute-start(bf16[1040,128]{1,0:T(8,128)(2,1)} %get-tuple-element.29.own_ref), channel_id=1, source_target_pairs={{0,1},{1,2},{2,3},{3,4},{4,5},{5,6},{6,7},{7,8},{8,9},{9,10},{10,1... | collective-permute-start | bytes 798728 | tf_op jit(solution)/shard_map/ppermute | solution.py:32
  4.3 15.6 %collective-permute-start.2 = (bf16[1040,128]{1,0:T(8,128)(2,1)}, bf16[1040,128]{1,0:T(8,128)(2,1)S(1)}, u32[]{:S(2)}, u32[]{:S(2)}) collective-permute-start(bf16[1040,128]{1,0:T(8,128)(2,1)} %get-tuple-element.29.own_ref), channel_id=1, source_target_pairs={{0,31},{1,0},{2,1},{3,2},{4,3},{5,4},{6,5},{7,6},{8,7},{9,8},{10,9... | collective-permute-start | bytes 798728 | tf_op jit(solution)/shard_map/ppermute | solution.py:32
  11.1 11.1 %collective-permute-start.5 = (bf16[1040,128]{1,0:T(8,128)(2,1)}, bf16[1040,128]{1,0:T(8,128)(2,1)S(1)}, u32[]{:S(2)}, u32[]{:S(2)}) collective-permute-start(bf16[1040,128]{1,0:T(8,128)(2,1)} %get-tuple-element.29.own_ref), channel_id=1, source_target_pairs={{0,4},{1,5},{2,6},{3,7},{4,8},{5,9},{6,10},{7,11},{8,12},{9,13},{1... | collective-permute-start | bytes 798728 | tf_op jit(solution)/shard_map/ppermute | solution.py:32
  11.1 16.4 %collective-permute-start.6 = (bf16[1040,128]{1,0:T(8,128)(2,1)}, bf16[1040,128]{1,0:T(8,128)(2,1)S(1)}, u32[]{:S(2)}, u32[]{:S(2)}) collective-permute-start(bf16[1040,128]{1,0:T(8,128)(2,1)} %get-tuple-element.29.own_ref), channel_id=1, source_target_pairs={{0,28},{1,29},{2,30},{3,31},{4,0},{5,1},{6,2},{7,3},{8,4},{9,5},{1... | collective-permute-start | bytes 798728 | tf_op jit(solution)/shard_map/ppermute | solution.py:32
  14.3 7.8 %collective-permute-start = (bf16[128,512]{1,0:T(8,128)(2,1)}, bf16[128,512]{1,0:T(8,128)(2,1)S(1)}, u32[]{:S(2)}, u32[]{:S(2)}) collective-permute-start(bf16[128,512]{1,0:T(8,128)(2,1)} %get-tuple-element.31), channel_id=1, source_target_pairs={{0,32},{32,0},{1,33},{33,1},{2,34},{34,2},{3,35},{35,3},{4,36},{36... | collective-permute-start | bytes 393224 | tf_op jit(solution)/shard_map/ppermute | solution.py:36
  14.3 2.8 %copy-start = (bf16[1024,3072]{1,0:T(8,128)(2,1)S(1)}, bf16[1024,3072]{1,0:T(8,128)(2,1)}, u32[]{:S(2)}) copy-start(bf16[1024,3072]{1,0:T(8,128)(2,1)} %refs_3_.5) | copy-start | bytes 18874372
  17.1 1.0 %copy-start.1 = (bf16[1040,128]{1,0:T(8,128)(2,1)S(1)}, bf16[1040,128]{1,0:T(8,128)(2,1)}, u32[]{:S(2)}) copy-start(bf16[1040,128]{1,0:T(8,128)(2,1)} %get-tuple-element.29.own_ref) | copy-start | bytes 798724
  18.0 9.4 %copy-start.5 = (bf16[128,512]{1,0:T(8,128)(2,1)S(1)}, bf16[128,512]{1,0:T(8,128)(2,1)}, u32[]{:S(2)}) copy-start(bf16[128,512]{1,0:T(8,128)(2,1)} %get-tuple-element.30) | copy-start | bytes 393220
  20.0 25.9 %collective-permute-start.10 = (bf16[2080,128]{1,0:T(8,128)(2,1)S(1)}, bf16[2080,128]{1,0:T(8,128)(2,1)S(1)}, u32[]{:S(2)}, u32[]{:S(2)}) collective-permute-start(bf16[2080,128]{1,0:T(8,128)(2,1)S(1)} %constant_dynamic-update-slice_fusion), channel_id=1, source_target_pairs={{0,28},{1,29},{2,30},{3,31},{4,0},{5,1},{6,2},{7,3},{8,4},{9,5},{1... | collective-permute-start | bytes 1597448 | tf_op jit(solution)/shard_map/ppermute | solution.py:32
  20.6 25.3 %collective-permute-start.9 = (bf16[2080,128]{1,0:T(8,128)(2,1)S(1)}, bf16[2080,128]{1,0:T(8,128)(2,1)S(1)}, u32[]{:S(2)}, u32[]{:S(2)}) collective-permute-start(bf16[2080,128]{1,0:T(8,128)(2,1)S(1)} %constant_dynamic-update-slice_fusion), channel_id=1, source_target_pairs={{0,4},{1,5},{2,6},{3,7},{4,8},{5,9},{6,10},{7,11},{8,12},{9,13},{1... | collective-permute-start | bytes 1597448 | tf_op jit(solution)/shard_map/ppermute | solution.py:32
  22.1 20.3 %collective-permute-start.3 = (bf16[1040,128]{1,0:T(8,128)(2,1)S(1)}, bf16[1040,128]{1,0:T(8,128)(2,1)S(1)}, u32[]{:S(2)}, u32[]{:S(2)}) collective-permute-start(bf16[1040,128]{1,0:T(8,128)(2,1)S(1)} %collective-permute-done.1.refs_0_), channel_id=1, source_target_pairs={{0,1},{1,2},{2,3},{3,4},{4,5},{5,6},{6,7},{7,8},{8,9},{9,10},{10,1... | collective-permute-start | bytes 798728 | tf_op jit(solution)/shard_map/ppermute | solution.py:32
  22.1 20.3 %collective-permute-start.4 = (bf16[1040,128]{1,0:T(8,128)(2,1)S(1)}, bf16[1040,128]{1,0:T(8,128)(2,1)S(1)}, u32[]{:S(2)}, u32[]{:S(2)}) collective-permute-start(bf16[1040,128]{1,0:T(8,128)(2,1)S(1)} %collective-permute-done.2.refs_2_), channel_id=1, source_target_pairs={{0,31},{1,0},{2,1},{3,2},{4,3},{5,4},{6,5},{7,6},{8,7},{9,8},{10,9... | collective-permute-start | bytes 798728 | tf_op jit(solution)/shard_map/ppermute | solution.py:32
  42.5 7.6 %collective-permute-start.7 = (bf16[1040,128]{1,0:T(8,128)(2,1)S(1)}, bf16[1040,128]{1,0:T(8,128)(2,1)S(1)}, u32[]{:S(2)}, u32[]{:S(2)}) collective-permute-start(bf16[1040,128]{1,0:T(8,128)(2,1)S(1)} %collective-permute-done.3.refs_0_), channel_id=1, source_target_pairs={{0,4},{1,5},{2,6},{3,7},{4,8},{5,9},{6,10},{7,11},{8,12},{9,13},{1... | collective-permute-start | bytes 798728 | tf_op jit(solution)/shard_map/ppermute | solution.py:32
  42.5 7.6 %collective-permute-start.8 = (bf16[1040,128]{1,0:T(8,128)(2,1)S(1)}, bf16[1040,128]{1,0:T(8,128)(2,1)S(1)}, u32[]{:S(2)}, u32[]{:S(2)}) collective-permute-start(bf16[1040,128]{1,0:T(8,128)(2,1)S(1)} %collective-permute-done.4.refs_1_), channel_id=1, source_target_pairs={{0,28},{1,29},{2,30},{3,31},{4,0},{5,1},{6,2},{7,3},{8,4},{9,5},{1... | collective-permute-start | bytes 798728 | tf_op jit(solution)/shard_map/ppermute | solution.py:32
  45.7 4.4 %slice-start = ((s8[6291456]{0:T(1024)(128)(4,1)}), s8[4194304]{0:T(1024)(128)(4,1)S(1)}, s32[]{:S(2)}) async-start(s8[6291456]{0:T(1024)(128)(4,1)} %bitcast.8), calls=%async_computation.2 | async-start | bytes 8388608
  45.9 4.3 %copy-start.2 = (bf16[1040,128]{1,0:T(8,128)(2,1)S(1)}, bf16[1040,128]{1,0:T(8,128)(2,1)}, u32[]{:S(2)}) copy-start(bf16[1040,128]{1,0:T(8,128)(2,1)} %get-tuple-element.29.own_ref) | copy-start | bytes 798724
  45.9 4.3 %copy-start.3 = (bf16[1024,1024]{1,0:T(8,128)(2,1)S(1)}, bf16[1024,1024]{1,0:T(8,128)(2,1)}, u32[]{:S(2)}) copy-start(bf16[1024,1024]{1,0:T(8,128)(2,1)} %refs_8_.1) | copy-start | bytes 6291460
  45.9 4.3 %copy-start.4 = (bf16[1,128,1024]{2,1,0:T(8,128)(2,1)S(1)}, bf16[1,128,1024]{2,1,0:T(8,128)(2,1)}, u32[]{:S(2)}) copy-start(bf16[1,128,1024]{2,1,0:T(8,128)(2,1)} %param.7) | copy-start | bytes 786436
  45.9 4.2 %slice-start.1 = ((s8[6291456]{0:T(1024)(128)(4,1)}), s8[2097152]{0:T(1024)(128)(4,1)S(1)}, s32[]{:S(2)}) async-start(s8[6291456]{0:T(1024)(128)(4,1)} %bitcast.8), calls=%async_computation.3 | async-start | bytes 4194304
  51.5 11.5 %all-to-all-start = ((bf16[4,256,128]{2,1,0:T(8,128)(2,1)}), bf16[4,256,128]{2,1,0:T(8,128)(2,1)S(1)}, u32[]{:S(2)}, u32[]{:S(2)}) async-start(bf16[4,256,128]{2,1,0:T(8,128)(2,1)} %get-tuple-element.54), calls=%async_computation | async-start | bytes 524288 | tf_op jit(solution)/shard_map/all_to_all | solution.py:334
  54.9 13.1 %collective-permute-start.12 = (bf16[256,512]{1,0:T(8,128)(2,1)S(1)}, bf16[256,512]{1,0:T(8,128)(2,1)S(1)}, u32[]{:S(2)}, u32[]{:S(2)}) collective-permute-start(bf16[256,512]{1,0:T(8,128)(2,1)S(1)} %pad_maximum_fusion.refs_0_), channel_id=1, source_target_pairs={{0,1},{1,2},{2,3},{3,0},{4,5},{5,6},{6,7},{7,4},{8,9},{9,10},{10,1... | collective-permute-start | bytes 786440 | tf_op jit(solution)/shard_map/ppermute | solution.py:41
  56.9 16.1 %collective-permute-start.13 = (bf16[256,512]{1,0:T(8,128)(2,1)S(1)}, bf16[256,512]{1,0:T(8,128)(2,1)S(1)}, u32[]{:S(2)}, u32[]{:S(2)}) collective-permute-start(bf16[256,512]{1,0:T(8,128)(2,1)S(1)} %pad_maximum_fusion.refs_0_), channel_id=1, source_target_pairs={{0,2},{1,3},{2,0},{3,1},{4,6},{5,7},{6,4},{7,5},{8,10},{9,11},{10,... | collective-permute-start | bytes 786440 | tf_op jit(solution)/shard_map/ppermute | solution.py:41
  59.6 13.4 %collective-permute-start.14 = (bf16[256,512]{1,0:T(8,128)(2,1)S(1)}, bf16[256,512]{1,0:T(8,128)(2,1)S(1)}, u32[]{:S(2)}, u32[]{:S(2)}) collective-permute-start(bf16[256,512]{1,0:T(8,128)(2,1)S(1)} %pad_maximum_fusion.refs_0_), channel_id=1, source_target_pairs={{0,3},{1,0},{2,1},{3,2},{4,7},{5,4},{6,5},{7,6},{8,11},{9,8},{10,9... | collective-permute-start | bytes 786440 | tf_op jit(solution)/shard_map/ppermute | solution.py:41
  63.0 10.0 %collective-permute-start.11 = (bf16[4,256,128]{2,1,0:T(8,128)(2,1)S(1)}, bf16[4,256,128]{2,1,0:T(8,128)(2,1)S(1)}, u32[]{:S(2)}, u32[]{:S(2)}) collective-permute-start(bf16[4,256,128]{2,1,0:T(8,128)(2,1)S(1)} %all-to-all-done.own_ref), channel_id=1, source_target_pairs={{0,32},{32,0},{1,33},{33,1},{2,34},{34,2},{3,35},{35,3},{4,36},{36... | collective-permute-start | bytes 786440 | tf_op jit(solution)/shard_map/ppermute | solution.py:36

commit v5 on v4

--- a/solution.py
+++ b/solution.py
@@ -41,13 +41,14 @@
     return lax.ppermute(block, "y", [(i, (i + distance) % n) for i in range(n)])
 
 
-def gathered_order():
-    n = lax.axis_size("y")
-    table = [[(place + n - d) % n for d in range(n)] for place in range(n)]
-    return lax.dynamic_index_in_dim(jnp.asarray(table, jnp.int32), lax.axis_index("y"), 0, False)
-
-
-def norm_kernel(core_ref, frames_ref, ids_ref, gain_ref, cotangent_ref, packed_ref, mine_ref, theirs_ref):
+def norm_kernel(core_ref, frames_hbm, ids_hbm, gain_hbm, cotangent_hbm, packed_ref, mine_ref, theirs_ref, *scratch):
+    frames_ref, ids_ref, gain_ref, cotangent_ref, sems = scratch
+    pairs = zip((frames_hbm, ids_hbm, gain_hbm, cotangent_hbm), scratch)
+    copies = [pltpu.make_async_copy(src, dst, sems.at[i]) for i, (src, dst) in enumerate(pairs)]
+    for copy in copies:
+        copy.start()
+    for copy in copies[:3]:
+        copy.wait()
     float_frames = frames_ref[...].astype(F32)
     average = jnp.mean(float_frames, axis=-1, keepdims=True)
     centered = float_frames - average
@@ -57,6 +58,7 @@
         packed_ref[c * ROWS : (c + 1) * ROWS, :] = normed[:, c * LANES : (c + 1) * LANES]
     ids = (ids_ref[...] + 1).astype(F32)
     packed_ref[WIDTH:PACKED, :] = jnp.broadcast_to(ids, (16, LANES)).astype(BF16)
+    copies[3].wait()
     first = core_ref[0] == 0
     for c in range(CHUNKS // 2):
         even = cotangent_ref[:, 2 * c * LANES : (2 * c + 1) * LANES]
@@ -67,15 +69,18 @@
 
 
 def normalize(core, frames, ids, gain, cotangent):
-    vmem = pl.BlockSpec(memory_space=pltpu.VMEM)
+    hbm = pl.BlockSpec(memory_space=pltpu.HBM)
     half = jax.ShapeDtypeStruct((ROWS, WIDTH // 2), BF16)
+    operands = (frames, ids, gain, cotangent)
     return pl.pallas_call(
         norm_kernel,
-        in_specs=[pl.BlockSpec(memory_space=pltpu.SMEM), vmem, vmem, vmem, vmem],
+        in_specs=[pl.BlockSpec(memory_space=pltpu.SMEM)] + [hbm] * len(operands),
         out_shape=[jax.ShapeDtypeStruct((PACKED, LANES), BF16), half, half],
+        scratch_shapes=[pltpu.VMEM(x.shape, x.dtype) for x in operands]
+        + [pltpu.SemaphoreType.DMA((len(operands),))],
         compiler_params=pltpu.CompilerParams(vmem_limit_bytes=60 * 1024 * 1024),
         name="layer_norm",
-    )(core, frames, ids, gain, cotangent)
+    )(core, *operands)
 
 
 def unpacked(block):
@@ -277,10 +282,11 @@
     )(own, *blocks, queries, w_qkv, *state, frames, w_out)
 
 
-def grad_kernel(order_ref, own_ref, other_ref, *refs):
+def grad_kernel(place_ref, own_ref, other_ref, *refs):
     grads, out_ref = refs[:-1], refs[-1]
     count = len(grads)
-    attended = [ref[order_ref[i]] for i in range(count) for ref in (own_ref, other_ref)]
+    order = [lax.rem(place_ref[0] + count - i, count) for i in range(count)]
+    attended = [ref[i] for i in order for ref in (own_ref, other_ref)]
     attended = jnp.concatenate(attended, axis=1)
     for half in range(2):
         at = slice(half * QUAD, (half + 1) * QUAD)
@@ -290,7 +296,7 @@
             out_ref[2 * half + k] = product[:, k * LANES : (k + 1) * LANES]
 
 
-def grad_product(order, own, other, grads):
+def grad_product(place, own, other, grads):
     vmem = pl.BlockSpec(memory_space=pltpu.VMEM)
     rows, columns = own.shape[1], grads[0].shape[1]
     return pl.pallas_call(
@@ -299,23 +305,25 @@
         out_shape=jax.ShapeDtypeStruct((columns // LANES, rows, LANES), BF16),
         compiler_params=LIMIT,
         name="grad_product",
-    )(order, own, other, *grads)
+    )(place, own, other, *grads)
 
 
 def local(frames, segment_ids, norm_gain, w_qkv, w_out, cotangent):
     n_y = lax.axis_size("y")
     frames = frames[0]
     core = lax.axis_index("core").astype(jnp.int32).reshape(1)
+    place = lax.axis_index("y").astype(jnp.int32).reshape(1)
     own, mine, theirs = normalize(core, frames, segment_ids, norm_gain[None, :], cotangent[0])
 
     left1, right1 = shifted(own, 1), shifted(own, -1)
     left4, right4 = shifted(own, 4), shifted(own, -4)
     received = core_swapped(theirs)
-    queries, *state = own_block(own, w_qkv)
-    left1, right1, queries = lax.optimization_barrier((left1, right1, queries))
-    near = jnp.concatenate([left1, right1], axis=0)
     left2, right2 = shifted(left1, 1), shifted(right1, -1)
+    left4, right4, near1, near2 = lax.optimization_barrier((left4, right4, left1, right1))
+    near = jnp.concatenate([near1, near2], axis=0)
     left_two, right_two = shifted(near, 4), shifted(near, -4)
+    held, near = lax.optimization_barrier((own, near))
+    queries, *state = own_block(held, w_qkv)
     state = absorb_stage(
         own, (left1, left4, right1, right4), ((0, 0), (1, 0)), ((2, 0), (3, 0)), queries, w_qkv, state
     )
@@ -327,12 +335,13 @@
     state = absorb_stage(
         own, (left_two, right_two), ((0, 1), (0, 0)), ((1, 0), (1, 1)), queries, w_qkv, state
     )
+    left6, right6, grads, state = lax.optimization_barrier((left6, right6, grads, state))
     attended, block_out = last_stage(
         own, (left6, right6), ((0, 0),), ((1, 0),), queries, w_qkv, state, frames, w_out
     )
 
     pieces = lax.all_to_all(attended, "y", 0, 0, tiled=True)
-    share = grad_product(gathered_order(), pieces, core_swapped(pieces), grads)
+    share = grad_product(place, pieces, core_swapped(pieces), grads)
     parts = lax.all_to_all(share.reshape(-1, WIDTH // N_SEQ, LANES), ("x", "z"), 0, 0, tiled=True)
     grad_scale = (lax.axis_size(("x", "core")) * N_SEQ * ROWS) ** (-0.5)
     return (block_out[None], jnp.sum(parts.astype(F32), axis=0) * grad_scale)

time: 94.4 us -> 92.9 us (0.984)
  waiting for transfers between devices: 26.1 us -> 11.3 us
  blocking collectives: 18.3 us -> 27.1 us
  Pallas kernels: 10.7 us -> 19.1 us
  starting transfers between devices: 31.8 us -> 27.3 us
    all_to_all x0 -> x1, blocking collectives: none -> 9.05 us  [local(): pieces = lax.all_to_all(attended, 'y', 0, 0, tiled=True)]
    ppermute x3, waiting for transfers between devices: 9.35 us -> 0.42 us  [turned(): return lax.ppermute(block, 'y', [(i, (i + distance) % n) for i in range(n)])]
    pallas_call x3, Pallas kernels: 4.43 us -> 10.9 us  [absorb_stage(): pl.pallas_call(kernel, out_shape=list(STATE_SHAPES), compiler_params=LIMI...]
    ppermute x10, waiting for transfers between devices: 14.8 us -> 9.35 us  [shifted(): return lax.ppermute(block, SEQ, route)]
    ppermute x3, starting transfers between devices: 6.15 us -> 2.03 us  [turned(): return lax.ppermute(block, 'y', [(i, (i + distance) % n) for i in range(n)])]
    all_to_all x1 -> x0, starting transfers between devices: 3.4 us -> none  [local(): pieces = lax.all_to_all(attended, 'y', 0, 0, tiled=True)]
    ppermute x10, starting transfers between devices: 22.2 us -> 25.3 us  [shifted(): return lax.ppermute(block, SEQ, route)]
    pallas_call x1, Pallas kernels: 1.33 us -> 3.76 us  [last_stage(): pl.pallas_call(kernel, out_shape=[jax.ShapeDtypeStruct((N_Y, WIDTH // N_Y...]
  transfers between devices with their start and end apart: 16 -> 15, of which waited for: 5 -> 6; matrix products, arithmetic and copies ran while one was open for 1% -> 1% of each run, Pallas kernels for 7% -> 14%
where the time goes in v5:
time: 92.9 us; the launch traced here: 91 us
  starting transfers between devices  27.3 us (29%)
  blocking collectives  27.1 us (29%)
  Pallas kernels  19.1 us (21%)
  waiting for transfers between devices  11.3 us (12%)
  local copies, waits for them, and re-layouts  3.82 us (4%)
  other arithmetic  1.58 us (2%)
    ppermute x10, starting transfers between devices, shifted(): return lax.ppermute(block, SEQ, route)  25.3 us
    all_to_all x1, blocking collectives, local(): lax.all_to_all(share.reshape(-1, WIDTH // N_SEQ, LANES), ('x', 'z'), 0, 0...  18.1 us
    pallas_call x3, Pallas kernels, absorb_stage(): pl.pallas_call(kernel, out_shape=list(STATE_SHAPES), compiler_params=LIMI...  10.9 us
    ppermute x10, waiting for transfers between devices, shifted(): return lax.ppermute(block, SEQ, route)  9.35 us
    all_to_all x1, blocking collectives, local(): pieces = lax.all_to_all(attended, 'y', 0, 0, tiled=True)  9.05 us
    unnamed x15, local copies, waits for them, and re-layouts  3.78 us
    pallas_call x1, Pallas kernels, last_stage(): pl.pallas_call(kernel, out_shape=[jax.ShapeDtypeStruct((N_Y, WIDTH // N_Y...  3.76 us
    pallas_call x1, Pallas kernels, normalize(): pl.pallas_call(norm_kernel, in_specs=[pl.BlockSpec(memory_space=pltpu.SME...  2.07 us
  transfers between devices with their start and end apart: 15, of which 6 were waited for; matrix products, arithmetic and copies ran while one was open for 1% of the time, Pallas kernels for 14%

profile of v5, /device:TPU:4, one launch (start us, length us, event | category | flops | bytes accessed | tf_op | source)
XLA Modules:
  0.0 91.0 jit_solution(1185869590216534081)
XLA Ops:
  0.6 2.1 %layer_norm.1 = (bf16[1040,128]{1,0:T(8,128)(2,1)}, bf16[128,512]{1,0:T(8,128)(2,1)}, bf16[128,512]{1,0:T(8,128)(2,1)}) custom-call(s32[1]{0:T(128)} %bitcast.core_ref, bf16[128,1024]{1,0:T(8,128)(2,1)} %bitcast.9, s32[1,128]{1,0:T(1,128)} %ids_hbm.1, f32[1,1024]{1,0:T(1,128)} %bitcast.13, bf16[128,1024]{1,0:T(8,128)(2,1)} %bitcast.12), custom_call_target="tpu_custom_call" | custom-call | tf_op jit(solution)/shard_map/layer_norm/pallas_call | solution.py:75
  2.7 1.7 %collective-permute-start.1 = (bf16[1040,128]{1,0:T(8,128)(2,1)}, bf16[1040,128]{1,0:T(8,128)(2,1)S(1)}, u32[]{:S(2)}, u32[]{:S(2)}) collective-permute-start(bf16[1040,128]{1,0:T(8,128)(2,1)} %get-tuple-element.47.own_ref), channel_id=1, source_target_pairs={{0,1},{1,2},{2,3},{3,4},{4,5},{5,6},{6,7},{7,8},{8,9},{9,10},{10,1... | collective-permute-start | bytes 798728 | tf_op jit(solution)/shard_map/ppermute | solution.py:32
  4.4 6.8 %collective-permute-start.3 = (bf16[1040,128]{1,0:T(8,128)(2,1)}, bf16[1040,128]{1,0:T(8,128)(2,1)S(1)}, u32[]{:S(2)}, u32[]{:S(2)}) collective-permute-start(bf16[1040,128]{1,0:T(8,128)(2,1)} %get-tuple-element.47.own_ref), channel_id=1, source_target_pairs={{0,31},{1,0},{2,1},{3,2},{4,3},{5,4},{6,5},{7,6},{8,7},{9,8},{10,9... | collective-permute-start | bytes 798728 | tf_op jit(solution)/shard_map/ppermute | solution.py:32
  11.2 3.2 %collective-permute-start.6 = (bf16[1040,128]{1,0:T(8,128)(2,1)}, bf16[1040,128]{1,0:T(8,128)(2,1)S(1)}, u32[]{:S(2)}, u32[]{:S(2)}) collective-permute-start(bf16[1040,128]{1,0:T(8,128)(2,1)} %get-tuple-element.47.own_ref), channel_id=1, source_target_pairs={{0,28},{1,29},{2,30},{3,31},{4,0},{5,1},{6,2},{7,3},{8,4},{9,5},{1... | collective-permute-start | bytes 798728 | tf_op jit(solution)/shard_map/ppermute | solution.py:32
  14.4 4.1 %collective-permute-done.1.refs_0_ = bf16[1040,128]{1,0:T(8,128)(2,1)S(1)} collective-permute-done((bf16[1040,128]{1,0:T(8,128)(2,1)}, bf16[1040,128]{1,0:T(8,128)(2,1)S(1)}, u32[]{:S(2)}, u32[]{:S(2)}) %collective-permute-start.1) | collective-permute-done | bytes 266272 | tf_op jit(solution)/shard_map/ppermute | solution.py:32
  18.5 1.9 %collective-permute-done.5.refs_1_ = bf16[1040,128]{1,0:T(8,128)(2,1)S(1)} collective-permute-done((bf16[1040,128]{1,0:T(8,128)(2,1)}, bf16[1040,128]{1,0:T(8,128)(2,1)S(1)}, u32[]{:S(2)}, u32[]{:S(2)}) %collective-permute-start.5) | collective-permute-done | bytes 266272 | tf_op jit(solution)/shard_map/ppermute | solution.py:32
  20.5 2.4 %collective-permute-done.6.refs_3_ = bf16[1040,128]{1,0:T(8,128)(2,1)S(1)} collective-permute-done((bf16[1040,128]{1,0:T(8,128)(2,1)}, bf16[1040,128]{1,0:T(8,128)(2,1)S(1)}, u32[]{:S(2)}, u32[]{:S(2)}) %collective-permute-start.6) | collective-permute-done | bytes 266272 | tf_op jit(solution)/shard_map/ppermute | solution.py:32
  23.0 3.7 %collective-permute-start.13 = (bf16[2080,128]{1,0:T(8,128)(2,1)S(1)}, bf16[2080,128]{1,0:T(8,128)(2,1)S(1)}, u32[]{:S(2)}, u32[]{:S(2)}) collective-permute-start(bf16[2080,128]{1,0:T(8,128)(2,1)S(1)} %constant_dynamic-update-slice_fusion), channel_id=1, source_target_pairs={{0,28},{1,29},{2,30},{3,31},{4,0},{5,1},{6,2},{7,3},{8,4},{9,5},{1... | collective-permute-start | bytes 1597448 | tf_op jit(solution)/shard_map/ppermute | solution.py:32
  26.7 0.9 %pad_maximum_fusion.refs_0_ = bf16[256,512]{1,0:T(8,128)(2,1)S(1)} fusion(bf16[128,512]{1,0:T(8,128)(2,1)S(1)} %collective-permute-done, bf16[128,512]{1,0:T(8,128)(2,1)} %get-tuple-element.41), kind=kLoop, calls=%fused_computation.1 | loop fusion | flops 524288 | bytes 524288 | tf_op jit(solution)/shard_map/concatenate | solution.py:330
  27.7 5.3 %collective-permute-start.4 = (bf16[1040,128]{1,0:T(8,128)(2,1)S(1)}, bf16[1040,128]{1,0:T(8,128)(2,1)S(1)}, u32[]{:S(2)}, u32[]{:S(2)}) collective-permute-start(bf16[1040,128]{1,0:T(8,128)(2,1)S(1)} %collective-permute-done.3.refs_2_), channel_id=1, source_target_pairs={{0,31},{1,0},{2,1},{3,2},{4,3},{5,4},{6,5},{7,6},{8,7},{9,8},{10,9... | collective-permute-start | bytes 798728 | tf_op jit(solution)/shard_map/ppermute | solution.py:32
  33.0 2.8 %copy-done = bf16[1024,3072]{1,0:T(8,128)(2,1)S(1)} copy-done((bf16[1024,3072]{1,0:T(8,128)(2,1)S(1)}, bf16[1024,3072]{1,0:T(8,128)(2,1)}, u32[]{:S(2)}) %copy-start) | copy-done | bytes 6291480
  35.8 0.9 %copy-done.1 = bf16[1040,128]{1,0:T(8,128)(2,1)S(1)} copy-done((bf16[1040,128]{1,0:T(8,128)(2,1)S(1)}, bf16[1040,128]{1,0:T(8,128)(2,1)}, u32[]{:S(2)}) %copy-start.1) | copy-done | bytes 266264
  36.8 1.9 %own_block.1 = (bf16[8,128,256]{2,1,0:T(8,128)(2,1)S(1)}, f32[16,128]{1,0:T(8,128)S(1)}, f32[16,128]{1,0:T(8,128)S(1)}, f32[1024,128]{1,0:T(8,128)S(1)}) custom-call(bf16[1040,128]{1,0:T(8,128)(2,1)S(1)} %copy-done.1, bf16[1024,3072]{1,0:T(8,128)(2,1)S(1)} %copy-done), custom_call_target="tpu_custom_call" | custom-call | flops 1610612736 | bytes 8388608 | tf_op jit(solution)/shard_map/own_block/pallas_call | solution.py:194
  38.7 4.2 %absorb_stage.3 = (f32[16,128]{1,0:T(8,128)S(1)}, f32[16,128]{1,0:T(8,128)S(1)}, f32[1024,128]{1,0:T(8,128)S(1)}) custom-call(bf16[1040,128]{1,0:T(8,128)(2,1)S(1)} %copy-done.1, bf16[1040,128]{1,0:T(8,128)(2,1)S(1)} %collective-permute-done.1.refs_0_, bf16[1040,128]{1,0:T(8,128)(2,1)S(1)} %collective-permute-done.5.refs_1_, ...), custom_call_target="tpu_custom_call" | custom-call | flops 2147483648 | bytes 8388608 | tf_op jit(solution)/shard_map/absorb_stage/pallas_call | solution.py:235
  42.8 0.9 collective-permute-done.2.refs_0_
  44.4 1.3 %collective-permute-start.9 = (bf16[256,512]{1,0:T(8,128)(2,1)S(1)}, bf16[256,512]{1,0:T(8,128)(2,1)S(1)}, u32[]{:S(2)}, u32[]{:S(2)}) collective-permute-start(bf16[256,512]{1,0:T(8,128)(2,1)S(1)} %pad_maximum_fusion.refs_0_), channel_id=1, source_target_pairs={{0,1},{1,2},{2,3},{3,0},{4,5},{5,6},{6,7},{7,4},{8,9},{9,10},{10,1... | collective-permute-start | bytes 786440 | tf_op jit(solution)/shard_map/ppermute | solution.py:41
  45.8 3.0 %collective-permute-start.7 = (bf16[1040,128]{1,0:T(8,128)(2,1)S(1)}, bf16[1040,128]{1,0:T(8,128)(2,1)S(1)}, u32[]{:S(2)}, u32[]{:S(2)}) collective-permute-start(bf16[1040,128]{1,0:T(8,128)(2,1)S(1)} %collective-permute-done.2.refs_0_), channel_id=1, source_target_pairs={{0,4},{1,5},{2,6},{3,7},{4,8},{5,9},{6,10},{7,11},{8,12},{9,13},{1... | collective-permute-start | bytes 798728 | tf_op jit(solution)/shard_map/ppermute | solution.py:32
  48.8 1.4 %collective-permute-start.8 = (bf16[1040,128]{1,0:T(8,128)(2,1)S(1)}, bf16[1040,128]{1,0:T(8,128)(2,1)S(1)}, u32[]{:S(2)}, u32[]{:S(2)}) collective-permute-start(bf16[1040,128]{1,0:T(8,128)(2,1)S(1)} %collective-permute-done.4.refs_1_), channel_id=1, source_target_pairs={{0,28},{1,29},{2,30},{3,31},{4,0},{5,1},{6,2},{7,3},{8,4},{9,5},{1... | collective-permute-start | bytes 798728 | tf_op jit(solution)/shard_map/ppermute | solution.py:32
  50.2 2.6 %absorb_stage.4 = (f32[16,128]{1,0:T(8,128)S(1)}, f32[16,128]{1,0:T(8,128)S(1)}, f32[1024,128]{1,0:T(8,128)S(1)}) custom-call(bf16[1040,128]{1,0:T(8,128)(2,1)S(1)} %copy-done.1, bf16[1040,128]{1,0:T(8,128)(2,1)S(1)} %collective-permute-done.2.refs_0_, bf16[1040,128]{1,0:T(8,128)(2,1)S(1)} %collective-permute-done.4.refs_1_, ...), custom_call_target="tpu_custom_call" | custom-call | flops 1073741824 | bytes 8388608 | tf_op jit(solution)/shard_map/absorb_stage/pallas_call | solution.py:235
  52.8 4.2 %absorb_stage.5 = (f32[16,128]{1,0:T(8,128)S(1)}, f32[16,128]{1,0:T(8,128)S(1)}, f32[1024,128]{1,0:T(8,128)S(1)}) custom-call(bf16[1040,128]{1,0:T(8,128)(2,1)S(1)} %copy-done.1, bf16[2080,128]{1,0:T(8,128)(2,1)S(1)} %collective-permute-done.12.refs_0_, bf16[2080,128]{1,0:T(8,128)(2,1)S(1)} %collective-permute-done.13.refs_1_, ...), custom_call_target="tpu_custom_call" | custom-call | flops 2147483648 | bytes 8388608 | tf_op jit(solution)/shard_map/absorb_stage/pallas_call | solution.py:235
  57.5 3.8 %last_stage.1 = (bf16[4,256,128]{2,1,0:T(8,128)(2,1)S(1)}, bf16[128,1024]{1,0:T(8,128)(2,1)}) custom-call(bf16[1040,128]{1,0:T(8,128)(2,1)S(1)} %copy-done.2, bf16[1040,128]{1,0:T(8,128)(2,1)S(1)} %collective-permute-done.7.refs_0_, bf16[1040,128]{1,0:T(8,128)(2,1)S(1)} %collective-permute-done.8.refs_1_, ...), custom_call_target="tpu_custom_call" | custom-call | flops 1610612736 | bytes 10485760 | tf_op jit(solution)/shard_map/last_stage/pallas_call | solution.py:272
  61.3 9.1 %all_to_all.10.own_ref = bf16[4,256,128]{2,1,0:T(8,128)(2,1)S(1)} all-to-all(bf16[4,256,128]{2,1,0:T(8,128)(2,1)S(1)} %get-tuple-element.73), channel_id=1, replica_groups=mesh['x'=4,'core'=2,'z'=8,'y'=4] {'y'}, dimensions={0} | all-to-all | bytes 524288 | tf_op jit(solution)/shard_map/all_to_all | solution.py:343
  70.3 1.5 %collective-permute-done.14.other_ref = bf16[4,256,128]{2,1,0:T(8,128)(2,1)S(1)} collective-permute-done((bf16[4,256,128]{2,1,0:T(8,128)(2,1)S(1)}, bf16[4,256,128]{2,1,0:T(8,128)(2,1)S(1)}, u32[]{:S(2)}, u32[]{:S(2)}) %collective-permute-start.14) | collective-permute-done | bytes 262176 | tf_op jit(solution)/shard_map/ppermute | solution.py:36
  72.3 18.1 %all_to_all.11 = bf16[32,32,128]{2,1,0:T(8,128)(2,1)S(1)} all-to-all(bf16[32,32,128]{2,1,0:T(8,128)(2,1)S(1)} %bitcast.11), channel_id=1, replica_groups=mesh['x'=4,'core'=2,'z'=8,'y'=4] {'x','z'}, dimensions={0} | all-to-all | bytes 524288 | tf_op jit(solution)/shard_map/all_to_all | solution.py:345
  (35 shorter events, 2.5 us)
Async XLA Ops:
  2.7 15.8 %collective-permute-start.1 = (bf16[1040,128]{1,0:T(8,128)(2,1)}, bf16[1040,128]{1,0:T(8,128)(2,1)S(1)}, u32[]{:S(2)}, u32[]{:S(2)}) collective-permute-start(bf16[1040,128]{1,0:T(8,128)(2,1)} %get-tuple-element.47.own_ref), channel_id=1, source_target_pairs={{0,1},{1,2},{2,3},{3,4},{4,5},{5,6},{6,7},{7,8},{8,9},{9,10},{10,1... | collective-permute-start | bytes 798728 | tf_op jit(solution)/shard_map/ppermute | solution.py:32
  4.4 14.2 %collective-permute-start.3 = (bf16[1040,128]{1,0:T(8,128)(2,1)}, bf16[1040,128]{1,0:T(8,128)(2,1)S(1)}, u32[]{:S(2)}, u32[]{:S(2)}) collective-permute-start(bf16[1040,128]{1,0:T(8,128)(2,1)} %get-tuple-element.47.own_ref), channel_id=1, source_target_pairs={{0,31},{1,0},{2,1},{3,2},{4,3},{5,4},{6,5},{7,6},{8,7},{9,8},{10,9... | collective-permute-start | bytes 798728 | tf_op jit(solution)/shard_map/ppermute | solution.py:32
  11.2 9.3 %collective-permute-start.5 = (bf16[1040,128]{1,0:T(8,128)(2,1)}, bf16[1040,128]{1,0:T(8,128)(2,1)S(1)}, u32[]{:S(2)}, u32[]{:S(2)}) collective-permute-start(bf16[1040,128]{1,0:T(8,128)(2,1)} %get-tuple-element.47.own_ref), channel_id=1, source_target_pairs={{0,4},{1,5},{2,6},{3,7},{4,8},{5,9},{6,10},{7,11},{8,12},{9,13},{1... | collective-permute-start | bytes 798728 | tf_op jit(solution)/shard_map/ppermute | solution.py:32
  11.2 11.7 %collective-permute-start.6 = (bf16[1040,128]{1,0:T(8,128)(2,1)}, bf16[1040,128]{1,0:T(8,128)(2,1)S(1)}, u32[]{:S(2)}, u32[]{:S(2)}) collective-permute-start(bf16[1040,128]{1,0:T(8,128)(2,1)} %get-tuple-element.47.own_ref), channel_id=1, source_target_pairs={{0,28},{1,29},{2,30},{3,31},{4,0},{5,1},{6,2},{7,3},{8,4},{9,5},{1... | collective-permute-start | bytes 798728 | tf_op jit(solution)/shard_map/ppermute | solution.py:32
  14.4 12.3 %collective-permute-start = (bf16[128,512]{1,0:T(8,128)(2,1)}, bf16[128,512]{1,0:T(8,128)(2,1)S(1)}, u32[]{:S(2)}, u32[]{:S(2)}) collective-permute-start(bf16[128,512]{1,0:T(8,128)(2,1)} %get-tuple-element.42), channel_id=1, source_target_pairs={{0,32},{32,0},{1,33},{33,1},{2,34},{34,2},{3,35},{35,3},{4,36},{36... | collective-permute-start | bytes 393224 | tf_op jit(solution)/shard_map/ppermute | solution.py:36
  22.9 22.9 %collective-permute-start.12 = (bf16[2080,128]{1,0:T(8,128)(2,1)S(1)}, bf16[2080,128]{1,0:T(8,128)(2,1)S(1)}, u32[]{:S(2)}, u32[]{:S(2)}) collective-permute-start(bf16[2080,128]{1,0:T(8,128)(2,1)S(1)} %constant_dynamic-update-slice_fusion), channel_id=1, source_target_pairs={{0,4},{1,5},{2,6},{3,7},{4,8},{5,9},{6,10},{7,11},{8,12},{9,13},{1... | collective-permute-start | bytes 1597448 | tf_op jit(solution)/shard_map/ppermute | solution.py:32
  23.0 25.8 %collective-permute-start.13 = (bf16[2080,128]{1,0:T(8,128)(2,1)S(1)}, bf16[2080,128]{1,0:T(8,128)(2,1)S(1)}, u32[]{:S(2)}, u32[]{:S(2)}) collective-permute-start(bf16[2080,128]{1,0:T(8,128)(2,1)S(1)} %constant_dynamic-update-slice_fusion), channel_id=1, source_target_pairs={{0,28},{1,29},{2,30},{3,31},{4,0},{5,1},{6,2},{7,3},{8,4},{9,5},{1... | collective-permute-start | bytes 1597448 | tf_op jit(solution)/shard_map/ppermute | solution.py:32
  27.6 16.1 %collective-permute-start.2 = (bf16[1040,128]{1,0:T(8,128)(2,1)S(1)}, bf16[1040,128]{1,0:T(8,128)(2,1)S(1)}, u32[]{:S(2)}, u32[]{:S(2)}) collective-permute-start(bf16[1040,128]{1,0:T(8,128)(2,1)S(1)} %collective-permute-done.1.refs_0_), channel_id=1, source_target_pairs={{0,1},{1,2},{2,3},{3,4},{4,5},{5,6},{6,7},{7,8},{8,9},{9,10},{10,1... | collective-permute-start | bytes 798728 | tf_op jit(solution)/shard_map/ppermute | solution.py:32
  27.7 16.1 %collective-permute-start.4 = (bf16[1040,128]{1,0:T(8,128)(2,1)S(1)}, bf16[1040,128]{1,0:T(8,128)(2,1)S(1)}, u32[]{:S(2)}, u32[]{:S(2)}) collective-permute-start(bf16[1040,128]{1,0:T(8,128)(2,1)S(1)} %collective-permute-done.3.refs_2_), channel_id=1, source_target_pairs={{0,31},{1,0},{2,1},{3,2},{4,3},{5,4},{6,5},{7,6},{8,7},{9,8},{10,9... | collective-permute-start | bytes 798728 | tf_op jit(solution)/shard_map/ppermute | solution.py:32
  33.0 2.8 %copy-start = (bf16[1024,3072]{1,0:T(8,128)(2,1)S(1)}, bf16[1024,3072]{1,0:T(8,128)(2,1)}, u32[]{:S(2)}) copy-start(bf16[1024,3072]{1,0:T(8,128)(2,1)} %refs_3_.5) | copy-start | bytes 18874372
  35.8 1.0 %copy-start.1 = (bf16[1040,128]{1,0:T(8,128)(2,1)S(1)}, bf16[1040,128]{1,0:T(8,128)(2,1)}, u32[]{:S(2)}) copy-start(bf16[1040,128]{1,0:T(8,128)(2,1)} %get-tuple-element.47.own_ref) | copy-start | bytes 798724
  43.8 13.3 %collective-permute-start.10 = (bf16[256,512]{1,0:T(8,128)(2,1)S(1)}, bf16[256,512]{1,0:T(8,128)(2,1)S(1)}, u32[]{:S(2)}, u32[]{:S(2)}) collective-permute-start(bf16[256,512]{1,0:T(8,128)(2,1)S(1)} %pad_maximum_fusion.refs_0_), channel_id=1, source_target_pairs={{0,2},{1,3},{2,0},{3,1},{4,6},{5,7},{6,4},{7,5},{8,10},{9,11},{10,... | collective-permute-start | bytes 786440 | tf_op jit(solution)/shard_map/ppermute | solution.py:41
  43.8 13.3 %collective-permute-start.11 = (bf16[256,512]{1,0:T(8,128)(2,1)S(1)}, bf16[256,512]{1,0:T(8,128)(2,1)S(1)}, u32[]{:S(2)}, u32[]{:S(2)}) collective-permute-start(bf16[256,512]{1,0:T(8,128)(2,1)S(1)} %pad_maximum_fusion.refs_0_), channel_id=1, source_target_pairs={{0,3},{1,0},{2,1},{3,2},{4,7},{5,4},{6,5},{7,6},{8,11},{9,8},{10,9... | collective-permute-start | bytes 786440 | tf_op jit(solution)/shard_map/ppermute | solution.py:41
  44.4 13.0 %collective-permute-start.9 = (bf16[256,512]{1,0:T(8,128)(2,1)S(1)}, bf16[256,512]{1,0:T(8,128)(2,1)S(1)}, u32[]{:S(2)}, u32[]{:S(2)}) collective-permute-start(bf16[256,512]{1,0:T(8,128)(2,1)S(1)} %pad_maximum_fusion.refs_0_), channel_id=1, source_target_pairs={{0,1},{1,2},{2,3},{3,0},{4,5},{5,6},{6,7},{7,4},{8,9},{9,10},{10,1... | collective-permute-start | bytes 786440 | tf_op jit(solution)/shard_map/ppermute | solution.py:41
  45.8 11.7 %collective-permute-start.7 = (bf16[1040,128]{1,0:T(8,128)(2,1)S(1)}, bf16[1040,128]{1,0:T(8,128)(2,1)S(1)}, u32[]{:S(2)}, u32[]{:S(2)}) collective-permute-start(bf16[1040,128]{1,0:T(8,128)(2,1)S(1)} %collective-permute-done.2.refs_0_), channel_id=1, source_target_pairs={{0,4},{1,5},{2,6},{3,7},{4,8},{5,9},{6,10},{7,11},{8,12},{9,13},{1... | collective-permute-start | bytes 798728 | tf_op jit(solution)/shard_map/ppermute | solution.py:32
  48.8 8.7 %collective-permute-start.8 = (bf16[1040,128]{1,0:T(8,128)(2,1)S(1)}, bf16[1040,128]{1,0:T(8,128)(2,1)S(1)}, u32[]{:S(2)}, u32[]{:S(2)}) collective-permute-start(bf16[1040,128]{1,0:T(8,128)(2,1)S(1)} %collective-permute-done.4.refs_1_), channel_id=1, source_target_pairs={{0,28},{1,29},{2,30},{3,31},{4,0},{5,1},{6,2},{7,3},{8,4},{9,5},{1... | collective-permute-start | bytes 798728 | tf_op jit(solution)/shard_map/ppermute | solution.py:32
  50.2 7.3 %slice-start = ((s8[6291456]{0:T(1024)(128)(4,1)}), s8[4194304]{0:T(1024)(128)(4,1)S(1)}, s32[]{:S(2)}) async-start(s8[6291456]{0:T(1024)(128)(4,1)} %bitcast.7), calls=%async_computation.2 | async-start | bytes 8388608
  52.8 4.7 %copy-start.2 = (bf16[1040,128]{1,0:T(8,128)(2,1)S(1)}, bf16[1040,128]{1,0:T(8,128)(2,1)}, u32[]{:S(2)}) copy-start(bf16[1040,128]{1,0:T(8,128)(2,1)} %get-tuple-element.47.own_ref) | copy-start | bytes 798724
  52.8 4.7 %copy-start.3 = (bf16[1024,1024]{1,0:T(8,128)(2,1)S(1)}, bf16[1024,1024]{1,0:T(8,128)(2,1)}, u32[]{:S(2)}) copy-start(bf16[1024,1024]{1,0:T(8,128)(2,1)} %refs_8_.1) | copy-start | bytes 6291460
  52.8 4.7 %copy-start.4 = (bf16[1,128,1024]{2,1,0:T(8,128)(2,1)S(1)}, bf16[1,128,1024]{2,1,0:T(8,128)(2,1)}, u32[]{:S(2)}) copy-start(bf16[1,128,1024]{2,1,0:T(8,128)(2,1)} %param.6) | copy-start | bytes 786436
  52.8 4.7 %slice-start.1 = ((s8[6291456]{0:T(1024)(128)(4,1)}), s8[2097152]{0:T(1024)(128)(4,1)S(1)}, s32[]{:S(2)}) async-start(s8[6291456]{0:T(1024)(128)(4,1)} %bitcast.7), calls=%async_computation.3 | async-start | bytes 4194304
  70.3 1.5 %collective-permute-start.14 = (bf16[4,256,128]{2,1,0:T(8,128)(2,1)S(1)}, bf16[4,256,128]{2,1,0:T(8,128)(2,1)S(1)}, u32[]{:S(2)}, u32[]{:S(2)}) collective-permute-start(bf16[4,256,128]{2,1,0:T(8,128)(2,1)S(1)} %all_to_all.10.own_ref), channel_id=1, source_target_pairs={{0,32},{32,0},{1,33},{33,1},{2,34},{34,2},{3,35},{35,3},{4,36},{36... | collective-permute-start | bytes 786440 | tf_op jit(solution)/shard_map/ppermute | solution.py:36

commit v6 on v5

--- a/solution.py
+++ b/solution.py
@@ -41,13 +41,12 @@
     return lax.ppermute(block, "y", [(i, (i + distance) % n) for i in range(n)])
 
 
-def norm_kernel(core_ref, frames_hbm, ids_hbm, gain_hbm, cotangent_hbm, packed_ref, mine_ref, theirs_ref, *scratch):
-    frames_ref, ids_ref, gain_ref, cotangent_ref, sems = scratch
-    pairs = zip((frames_hbm, ids_hbm, gain_hbm, cotangent_hbm), scratch)
+def norm_kernel(frames_hbm, ids_hbm, gain_hbm, packed_ref, frames_ref, ids_ref, gain_ref, sems):
+    pairs = ((frames_hbm, frames_ref), (ids_hbm, ids_ref), (gain_hbm, gain_ref))
     copies = [pltpu.make_async_copy(src, dst, sems.at[i]) for i, (src, dst) in enumerate(pairs)]
     for copy in copies:
         copy.start()
-    for copy in copies[:3]:
+    for copy in copies:
         copy.wait()
     float_frames = frames_ref[...].astype(F32)
     average = jnp.mean(float_frames, axis=-1, keepdims=True)
@@ -58,7 +57,22 @@
         packed_ref[c * ROWS : (c + 1) * ROWS, :] = normed[:, c * LANES : (c + 1) * LANES]
     ids = (ids_ref[...] + 1).astype(F32)
     packed_ref[WIDTH:PACKED, :] = jnp.broadcast_to(ids, (16, LANES)).astype(BF16)
-    copies[3].wait()
+
+
+def normalize(*operands):
+    hbm = pl.BlockSpec(memory_space=pltpu.HBM)
+    return pl.pallas_call(
+        norm_kernel,
+        in_specs=[hbm] * len(operands),
+        out_shape=jax.ShapeDtypeStruct((PACKED, LANES), BF16),
+        scratch_shapes=[pltpu.VMEM(x.shape, x.dtype) for x in operands]
+        + [pltpu.SemaphoreType.DMA((len(operands),))],
+        compiler_params=pltpu.CompilerParams(vmem_limit_bytes=60 * 1024 * 1024),
+        name="layer_norm",
+    )(*operands)
+
+
+def split_kernel(core_ref, cotangent_ref, mine_ref, theirs_ref):
     first = core_ref[0] == 0
     for c in range(CHUNKS // 2):
         even = cotangent_ref[:, 2 * c * LANES : (2 * c + 1) * LANES]
@@ -68,19 +82,15 @@
         theirs_ref[:, at] = jnp.where(first, odd, even)
 
 
-def normalize(core, frames, ids, gain, cotangent):
-    hbm = pl.BlockSpec(memory_space=pltpu.HBM)
+def split_columns(core, cotangent):
     half = jax.ShapeDtypeStruct((ROWS, WIDTH // 2), BF16)
-    operands = (frames, ids, gain, cotangent)
-    return pl.pallas_call(
-        norm_kernel,
-        in_specs=[pl.BlockSpec(memory_space=pltpu.SMEM)] + [hbm] * len(operands),
-        out_shape=[jax.ShapeDtypeStruct((PACKED, LANES), BF16), half, half],
-        scratch_shapes=[pltpu.VMEM(x.shape, x.dtype) for x in operands]
-        + [pltpu.SemaphoreType.DMA((len(operands),))],
-        compiler_params=pltpu.CompilerParams(vmem_limit_bytes=60 * 1024 * 1024),
-        name="layer_norm",
-    )(core, *operands)
+    return pl.pallas_call(
+        split_kernel,
+        in_specs=[pl.BlockSpec(memory_space=pltpu.SMEM), pl.BlockSpec(memory_space=pltpu.VMEM)],
+        out_shape=[half, half],
+        compiler_params=LIMIT,
+        name="split_columns",
+    )(core, cotangent)
 
 
 def unpacked(block):
@@ -313,27 +323,27 @@
     frames = frames[0]
     core = lax.axis_index("core").astype(jnp.int32).reshape(1)
     place = lax.axis_index("y").astype(jnp.int32).reshape(1)
-    own, mine, theirs = normalize(core, frames, segment_ids, norm_gain[None, :], cotangent[0])
+    own = normalize(frames, segment_ids, norm_gain[None, :])
 
     left1, right1 = shifted(own, 1), shifted(own, -1)
-    left4, right4 = shifted(own, 4), shifted(own, -4)
+    left2, right2 = shifted(own, 2), shifted(own, -2)
+    queries, *state = own_block(own, w_qkv)
+    left1, right1, queries = lax.optimization_barrier((left1, right1, queries))
+    trio = jnp.concatenate([left1, own, right1], axis=0)
+    left_trio, right_trio = shifted(trio, 4), shifted(trio, -4)
+    trio, cotangent = lax.optimization_barrier((trio, cotangent))
+    mine, theirs = split_columns(core, cotangent[0])
     received = core_swapped(theirs)
-    left2, right2 = shifted(left1, 1), shifted(right1, -1)
-    left4, right4, near1, near2 = lax.optimization_barrier((left4, right4, left1, right1))
-    near = jnp.concatenate([near1, near2], axis=0)
-    left_two, right_two = shifted(near, 4), shifted(near, -4)
-    held, near = lax.optimization_barrier((own, near))
-    queries, *state = own_block(held, w_qkv)
-    state = absorb_stage(
-        own, (left1, left4, right1, right4), ((0, 0), (1, 0)), ((2, 0), (3, 0)), queries, w_qkv, state
-    )
+    state = absorb_stage(own, (left1, right1), ((0, 0),), ((1, 0),), queries, w_qkv, state)
     both = jnp.concatenate([mine, received], axis=0)
     both, left2, right2, *state = lax.optimization_barrier((both, left2, right2, *state))
     left6, right6 = shifted(left2, 4), shifted(right2, -4)
+    state = absorb_stage(own, (left2, right2), ((0, 0),), ((1, 0),), queries, w_qkv, state)
+    both, *state = lax.optimization_barrier((both, *state))
     grads = [both, *[turned(both, d) for d in range(1, n_y)]]
-    state = absorb_stage(own, (left2, right2), ((0, 0),), ((1, 0),), queries, w_qkv, state)
     state = absorb_stage(
-        own, (left_two, right_two), ((0, 1), (0, 0)), ((1, 0), (1, 1)), queries, w_qkv, state
+        own, (left_trio, right_trio), ((0, 2), (0, 1), (0, 0)), ((1, 0), (1, 1), (1, 2)),
+        queries, w_qkv, state,
     )
     left6, right6, grads, state = lax.optimization_barrier((left6, right6, grads, state))
     attended, block_out = last_stage(

time: 92.9 us -> 102 us (1.098)
  the two profiles are of different devices: /device:TPU:4 before, /device:TPU:32 now
where the time goes in v6:
time: 102 us; the launch traced here: 101 us
  blocking collectives  33.1 us (32%)
  Pallas kernels  21.9 us (21%)
  starting transfers between devices  21.4 us (21%)
  waiting for transfers between devices  15.2 us (15%)
  local copies, waits for them, and re-layouts  5.59 us (5%)
  other arithmetic  2.58 us (3%)
    all_to_all x1, blocking collectives, local(): lax.all_to_all(share.reshape(-1, WIDTH // N_SEQ, LANES), ('x', 'z'), 0, 0...  24.1 us
    ppermute x8, starting transfers between devices, shifted(): return lax.ppermute(block, SEQ, route)  16.3 us
    pallas_call x3, Pallas kernels, absorb_stage(): pl.pallas_call(kernel, out_shape=list(STATE_SHAPES), compiler_params=LIMI...  14.3 us
    ppermute x8, waiting for transfers between devices, shifted(): return lax.ppermute(block, SEQ, route)  13.7 us
    all_to_all x1, blocking collectives, local(): pieces = lax.all_to_all(attended, 'y', 0, 0, tiled=True)  9.05 us
    unnamed x14, local copies, waits for them, and re-layouts  5.59 us
    ppermute x3, starting transfers between devices, turned(): return lax.ppermute(block, 'y', [(i, (i + distance) % n) for i in range(n)])  5.02 us
    pallas_call x1, Pallas kernels, own_block(): pl.pallas_call(own_kernel, out_shape=[jax.ShapeDtypeStruct((CHUNKS, LANES...  2.82 us
  transfers between devices with their start and end apart: 13, of which 5 were waited for; matrix products, arithmetic and copies ran while one was open for 0% of the time, Pallas kernels for 17%

profile of v6, /device:TPU:32, one launch (start us, length us, event | category | flops | bytes accessed | tf_op | source)
XLA Modules:
  0.0 100.7 jit_solution(11198166850871516196)
XLA Ops:
  0.6 1.9 %layer_norm.1.own_ref = bf16[1040,128]{1,0:T(8,128)(2,1)} custom-call(bf16[128,1024]{1,0:T(8,128)(2,1)} %bitcast.9, s32[1,128]{1,0:T(1,128)} %ids_hbm.1, f32[1,1024]{1,0:T(1,128)} %bitcast.13), custom_call_target="tpu_custom_call" | custom-call | tf_op jit(solution)/shard_map/layer_norm/pallas_call | solution.py:64
  2.6 1.7 %collective-permute-start = (bf16[1040,128]{1,0:T(8,128)(2,1)}, bf16[1040,128]{1,0:T(8,128)(2,1)S(1)}, u32[]{:S(2)}, u32[]{:S(2)}) collective-permute-start(bf16[1040,128]{1,0:T(8,128)(2,1)} %layer_norm.1.own_ref), channel_id=1, source_target_pairs={{0,1},{1,2},{2,3},{3,4},{4,5},{5,6},{6,7},{7,8},{8,9},{9,10},{10,1... | collective-permute-start | bytes 798728 | tf_op jit(solution)/shard_map/ppermute | solution.py:32
  4.2 2.6 %collective-permute-start.1 = (bf16[1040,128]{1,0:T(8,128)(2,1)}, bf16[1040,128]{1,0:T(8,128)(2,1)S(1)}, u32[]{:S(2)}, u32[]{:S(2)}) collective-permute-start(bf16[1040,128]{1,0:T(8,128)(2,1)} %layer_norm.1.own_ref), channel_id=1, source_target_pairs={{0,31},{1,0},{2,1},{3,2},{4,3},{5,4},{6,5},{7,6},{8,7},{9,8},{10,9... | collective-permute-start | bytes 798728 | tf_op jit(solution)/shard_map/ppermute | solution.py:32
  6.8 2.8 %copy-done = bf16[1024,3072]{1,0:T(8,128)(2,1)S(1)} copy-done((bf16[1024,3072]{1,0:T(8,128)(2,1)S(1)}, bf16[1024,3072]{1,0:T(8,128)(2,1)}, u32[]{:S(2)}) %copy-start) | copy-done | bytes 6291480
  9.6 2.8 %own_block.1 = (bf16[8,128,256]{2,1,0:T(8,128)(2,1)S(1)}, f32[16,128]{1,0:T(8,128)S(1)}, f32[16,128]{1,0:T(8,128)S(1)}, f32[1024,128]{1,0:T(8,128)S(1)}) custom-call(bf16[1040,128]{1,0:T(8,128)(2,1)} %layer_norm.1.own_ref, bf16[1024,3072]{1,0:T(8,128)(2,1)S(1)} %copy-done), custom_call_target="tpu_custom_call" | custom-call | flops 1610612736 | bytes 8388608 | tf_op jit(solution)/shard_map/own_block/pallas_call | solution.py:204
  13.1 1.9 %pad_maximum_fusion = bf16[3120,128]{1,0:T(8,128)(2,1)} fusion(bf16[1040,128]{1,0:T(8,128)(2,1)S(1)} %collective-permute-done.1.refs_1_, bf16[1040,128]{1,0:T(8,128)(2,1)} %layer_norm.1.own_ref, bf16[1040,128]{1,0:T(8,128)(2,1)S(1)} %collective-permute-done.refs_0_), kind=kLoop, calls=%fused_computation | loop fusion | flops 2396160 | bytes 1597440 | tf_op jit(solution)/shard_map/concatenate | solution.py:332
  15.0 1.9 %collective-permute-start.10 = (bf16[3120,128]{1,0:T(8,128)(2,1)}, bf16[3120,128]{1,0:T(8,128)(2,1)S(1)}, u32[]{:S(2)}, u32[]{:S(2)}) collective-permute-start(bf16[3120,128]{1,0:T(8,128)(2,1)} %pad_maximum_fusion), channel_id=1, source_target_pairs={{0,4},{1,5},{2,6},{3,7},{4,8},{5,9},{6,10},{7,11},{8,12},{9,13},{1... | collective-permute-start | bytes 2396168 | tf_op jit(solution)/shard_map/ppermute | solution.py:32
  16.9 2.6 %collective-permute-start.11 = (bf16[3120,128]{1,0:T(8,128)(2,1)}, bf16[3120,128]{1,0:T(8,128)(2,1)}, u32[]{:S(2)}, u32[]{:S(2)}) collective-permute-start(bf16[3120,128]{1,0:T(8,128)(2,1)} %pad_maximum_fusion), channel_id=1, source_target_pairs={{0,28},{1,29},{2,30},{3,31},{4,0},{5,1},{6,2},{7,3},{8,4},{9,5},{1... | collective-permute-start | bytes 2396168 | tf_op jit(solution)/shard_map/ppermute | solution.py:32
  19.6 4.4 %collective-permute-start.4 = (bf16[1040,128]{1,0:T(8,128)(2,1)}, bf16[1040,128]{1,0:T(8,128)(2,1)S(1)}, u32[]{:S(2)}, u32[]{:S(2)}) collective-permute-start(bf16[1040,128]{1,0:T(8,128)(2,1)} %layer_norm.1.own_ref), channel_id=1, source_target_pairs={{0,30},{1,31},{2,0},{3,1},{4,2},{5,3},{6,4},{7,5},{8,6},{9,7},{10,... | collective-permute-start | bytes 798728 | tf_op jit(solution)/shard_map/ppermute | solution.py:32
  24.2 2.8 %copy-done.1 = bf16[1024,3072]{1,0:T(8,128)(2,1)S(1)} copy-done((bf16[1024,3072]{1,0:T(8,128)(2,1)S(1)}, bf16[1024,3072]{1,0:T(8,128)(2,1)}, u32[]{:S(2)}) %copy-start.1) | copy-done | bytes 6291480
  27.0 3.6 %absorb_stage.3 = (f32[16,128]{1,0:T(8,128)S(1)}, f32[16,128]{1,0:T(8,128)S(1)}, f32[1024,128]{1,0:T(8,128)S(1)}) custom-call(bf16[1040,128]{1,0:T(8,128)(2,1)} %layer_norm.1.own_ref, bf16[1040,128]{1,0:T(8,128)(2,1)S(1)} %collective-permute-done.refs_0_, bf16[1040,128]{1,0:T(8,128)(2,1)S(1)} %collective-permute-done.1.refs_1_, ...), custom_call_target="tpu_custom_call" | custom-call | flops 1073741824 | bytes 8388608 | tf_op jit(solution)/shard_map/absorb_stage/pallas_call | solution.py:245
  30.6 10.3 %collective-permute-done.3.refs_0_ = bf16[1040,128]{1,0:T(8,128)(2,1)S(1)} collective-permute-done((bf16[1040,128]{1,0:T(8,128)(2,1)}, bf16[1040,128]{1,0:T(8,128)(2,1)S(1)}, u32[]{:S(2)}, u32[]{:S(2)}) %collective-permute-start.3) | collective-permute-done | bytes 266272 | tf_op jit(solution)/shard_map/ppermute | solution.py:32
  40.8 1.3 %collective-permute-done.4.refs_1_ = bf16[1040,128]{1,0:T(8,128)(2,1)S(1)} collective-permute-done((bf16[1040,128]{1,0:T(8,128)(2,1)}, bf16[1040,128]{1,0:T(8,128)(2,1)S(1)}, u32[]{:S(2)}, u32[]{:S(2)}) %collective-permute-start.4) | collective-permute-done | bytes 266272 | tf_op jit(solution)/shard_map/ppermute | solution.py:32
  42.1 3.7 %absorb_stage.4 = (f32[16,128]{1,0:T(8,128)S(1)}, f32[16,128]{1,0:T(8,128)S(1)}, f32[1024,128]{1,0:T(8,128)S(1)}) custom-call(bf16[1040,128]{1,0:T(8,128)(2,1)} %layer_norm.1.own_ref, bf16[1040,128]{1,0:T(8,128)(2,1)S(1)} %collective-permute-done.3.refs_0_, bf16[1040,128]{1,0:T(8,128)(2,1)S(1)} %collective-permute-done.4.refs_1_, ...), custom_call_target="tpu_custom_call" | custom-call | flops 1073741824 | bytes 8388608 | tf_op jit(solution)/shard_map/absorb_stage/pallas_call | solution.py:245
  45.9 1.9 %collective-permute-start.7 = (bf16[256,512]{1,0:T(8,128)(2,1)S(1)}, bf16[256,512]{1,0:T(8,128)(2,1)S(1)}, u32[]{:S(2)}, u32[]{:S(2)}) collective-permute-start(bf16[256,512]{1,0:T(8,128)(2,1)S(1)} %pad_maximum_fusion.1.refs_0_), channel_id=1, source_target_pairs={{0,1},{1,2},{2,3},{3,0},{4,5},{5,6},{6,7},{7,4},{8,9},{9,10},{10,1... | collective-permute-start | bytes 786440 | tf_op jit(solution)/shard_map/ppermute | solution.py:41
  47.7 1.6 %collective-permute-start.8 = (bf16[256,512]{1,0:T(8,128)(2,1)S(1)}, bf16[256,512]{1,0:T(8,128)(2,1)S(1)}, u32[]{:S(2)}, u32[]{:S(2)}) collective-permute-start(bf16[256,512]{1,0:T(8,128)(2,1)S(1)} %pad_maximum_fusion.1.refs_0_), channel_id=1, source_target_pairs={{0,2},{1,3},{2,0},{3,1},{4,6},{5,7},{6,4},{7,5},{8,10},{9,11},{10,... | collective-permute-start | bytes 786440 | tf_op jit(solution)/shard_map/ppermute | solution.py:41
  49.3 1.6 %collective-permute-start.9 = (bf16[256,512]{1,0:T(8,128)(2,1)S(1)}, bf16[256,512]{1,0:T(8,128)(2,1)S(1)}, u32[]{:S(2)}, u32[]{:S(2)}) collective-permute-start(bf16[256,512]{1,0:T(8,128)(2,1)S(1)} %pad_maximum_fusion.1.refs_0_), channel_id=1, source_target_pairs={{0,3},{1,0},{2,1},{3,2},{4,7},{5,4},{6,5},{7,6},{8,11},{9,8},{10,9... | collective-permute-start | bytes 786440 | tf_op jit(solution)/shard_map/ppermute | solution.py:41
  50.9 1.9 %collective-permute-start.5 = (bf16[1040,128]{1,0:T(8,128)(2,1)S(1)}, bf16[1040,128]{1,0:T(8,128)(2,1)S(1)}, u32[]{:S(2)}, u32[]{:S(2)}) collective-permute-start(bf16[1040,128]{1,0:T(8,128)(2,1)S(1)} %collective-permute-done.3.refs_0_), channel_id=1, source_target_pairs={{0,4},{1,5},{2,6},{3,7},{4,8},{5,9},{6,10},{7,11},{8,12},{9,13},{1... | collective-permute-start | bytes 798728 | tf_op jit(solution)/shard_map/ppermute | solution.py:32
  54.0 7.1 %absorb_stage.5 = (f32[16,128]{1,0:T(8,128)S(1)}, f32[16,128]{1,0:T(8,128)S(1)}, f32[1024,128]{1,0:T(8,128)S(1)}) custom-call(bf16[1040,128]{1,0:T(8,128)(2,1)} %layer_norm.1.own_ref, bf16[3120,128]{1,0:T(8,128)(2,1)S(1)} %collective-permute-done.10.refs_0_, bf16[3120,128]{1,0:T(8,128)(2,1)} %collective-permute-done.11.refs_1_, ...), custom_call_target="tpu_custom_call" | custom-call | flops 3221225472 | bytes 8388608 | tf_op jit(solution)/shard_map/absorb_stage/pallas_call | solution.py:245
  61.1 1.4 %collective-permute-done.6.refs_1_ = bf16[1040,128]{1,0:T(8,128)(2,1)S(1)} collective-permute-done((bf16[1040,128]{1,0:T(8,128)(2,1)S(1)}, bf16[1040,128]{1,0:T(8,128)(2,1)S(1)}, u32[]{:S(2)}, u32[]{:S(2)}) %collective-permute-start.6) | collective-permute-done | bytes 266272 | tf_op jit(solution)/shard_map/ppermute | solution.py:32
  62.6 2.3 %last_stage.1 = (bf16[4,256,128]{2,1,0:T(8,128)(2,1)S(1)}, bf16[128,1024]{1,0:T(8,128)(2,1)}) custom-call(bf16[1040,128]{1,0:T(8,128)(2,1)} %layer_norm.1.own_ref, bf16[1040,128]{1,0:T(8,128)(2,1)S(1)} %collective-permute-done.5.refs_0_, bf16[1040,128]{1,0:T(8,128)(2,1)S(1)} %collective-permute-done.6.refs_1_, ...), custom_call_target="tpu_custom_call" | custom-call | flops 1610612736 | bytes 10485760 | tf_op jit(solution)/shard_map/last_stage/pallas_call | solution.py:282
  64.9 9.1 %all_to_all.10.own_ref = bf16[4,256,128]{2,1,0:T(8,128)(2,1)S(1)} all-to-all(bf16[4,256,128]{2,1,0:T(8,128)(2,1)S(1)} %get-tuple-element.77), channel_id=1, replica_groups=mesh['x'=4,'core'=2,'z'=8,'y'=4] {'y'}, dimensions={0} | all-to-all | bytes 524288 | tf_op jit(solution)/shard_map/all_to_all | solution.py:353
  74.0 1.5 %collective-permute-done.12.other_ref = bf16[4,256,128]{2,1,0:T(8,128)(2,1)S(1)} collective-permute-done((bf16[4,256,128]{2,1,0:T(8,128)(2,1)S(1)}, bf16[4,256,128]{2,1,0:T(8,128)(2,1)S(1)}, u32[]{:S(2)}, u32[]{:S(2)}) %collective-permute-start.12) | collective-permute-done | bytes 262176 | tf_op jit(solution)/shard_map/ppermute | solution.py:36
  75.9 24.1 %all_to_all.11 = bf16[32,32,128]{2,1,0:T(8,128)(2,1)S(1)} all-to-all(bf16[32,32,128]{2,1,0:T(8,128)(2,1)S(1)} %bitcast.11), channel_id=1, replica_groups=mesh['x'=4,'core'=2,'z'=8,'y'=4] {'x','z'}, dimensions={0} | all-to-all | bytes 524288 | tf_op jit(solution)/shard_map/all_to_all | solution.py:355
  (31 shorter events, 3.2 us)
Async XLA Ops:
  2.6 10.5 %collective-permute-start = (bf16[1040,128]{1,0:T(8,128)(2,1)}, bf16[1040,128]{1,0:T(8,128)(2,1)S(1)}, u32[]{:S(2)}, u32[]{:S(2)}) collective-permute-start(bf16[1040,128]{1,0:T(8,128)(2,1)} %layer_norm.1.own_ref), channel_id=1, source_target_pairs={{0,1},{1,2},{2,3},{3,4},{4,5},{5,6},{6,7},{7,8},{8,9},{9,10},{10,1... | collective-permute-start | bytes 798728 | tf_op jit(solution)/shard_map/ppermute | solution.py:32
  4.2 8.9 %collective-permute-start.1 = (bf16[1040,128]{1,0:T(8,128)(2,1)}, bf16[1040,128]{1,0:T(8,128)(2,1)S(1)}, u32[]{:S(2)}, u32[]{:S(2)}) collective-permute-start(bf16[1040,128]{1,0:T(8,128)(2,1)} %layer_norm.1.own_ref), channel_id=1, source_target_pairs={{0,31},{1,0},{2,1},{3,2},{4,3},{5,4},{6,5},{7,6},{8,7},{9,8},{10,9... | collective-permute-start | bytes 798728 | tf_op jit(solution)/shard_map/ppermute | solution.py:32
  6.8 2.8 %copy-start = (bf16[1024,3072]{1,0:T(8,128)(2,1)S(1)}, bf16[1024,3072]{1,0:T(8,128)(2,1)}, u32[]{:S(2)}) copy-start(bf16[1024,3072]{1,0:T(8,128)(2,1)} %refs_3_.7) | copy-start | bytes 18874372
  12.4 11.6 %copy-start.4 = (bf16[1,128,1024]{2,1,0:T(8,128)(2,1)S(1)}, bf16[1,128,1024]{2,1,0:T(8,128)(2,1)}, u32[]{:S(2)}) copy-start(bf16[1,128,1024]{2,1,0:T(8,128)(2,1)} %param.11) | copy-start | bytes 786436
  15.0 35.9 %collective-permute-start.10 = (bf16[3120,128]{1,0:T(8,128)(2,1)}, bf16[3120,128]{1,0:T(8,128)(2,1)S(1)}, u32[]{:S(2)}, u32[]{:S(2)}) collective-permute-start(bf16[3120,128]{1,0:T(8,128)(2,1)} %pad_maximum_fusion), channel_id=1, source_target_pairs={{0,4},{1,5},{2,6},{3,7},{4,8},{5,9},{6,10},{7,11},{8,12},{9,13},{1... | collective-permute-start | bytes 2396168 | tf_op jit(solution)/shard_map/ppermute | solution.py:32
  16.9 35.9 %collective-permute-start.11 = (bf16[3120,128]{1,0:T(8,128)(2,1)}, bf16[3120,128]{1,0:T(8,128)(2,1)}, u32[]{:S(2)}, u32[]{:S(2)}) collective-permute-start(bf16[3120,128]{1,0:T(8,128)(2,1)} %pad_maximum_fusion), channel_id=1, source_target_pairs={{0,28},{1,29},{2,30},{3,31},{4,0},{5,1},{6,2},{7,3},{8,4},{9,5},{1... | collective-permute-start | bytes 2396168 | tf_op jit(solution)/shard_map/ppermute | solution.py:32
  19.6 21.2 %collective-permute-start.3 = (bf16[1040,128]{1,0:T(8,128)(2,1)}, bf16[1040,128]{1,0:T(8,128)(2,1)S(1)}, u32[]{:S(2)}, u32[]{:S(2)}) collective-permute-start(bf16[1040,128]{1,0:T(8,128)(2,1)} %layer_norm.1.own_ref), channel_id=1, source_target_pairs={{0,2},{1,3},{2,4},{3,5},{4,6},{5,7},{6,8},{7,9},{8,10},{9,11},{10,... | collective-permute-start | bytes 798728 | tf_op jit(solution)/shard_map/ppermute | solution.py:32
  19.6 22.5 %collective-permute-start.4 = (bf16[1040,128]{1,0:T(8,128)(2,1)}, bf16[1040,128]{1,0:T(8,128)(2,1)S(1)}, u32[]{:S(2)}, u32[]{:S(2)}) collective-permute-start(bf16[1040,128]{1,0:T(8,128)(2,1)} %layer_norm.1.own_ref), channel_id=1, source_target_pairs={{0,30},{1,31},{2,0},{3,1},{4,2},{5,3},{6,4},{7,5},{8,6},{9,7},{10,... | collective-permute-start | bytes 798728 | tf_op jit(solution)/shard_map/ppermute | solution.py:32
  24.1 6.5 %collective-permute-start.2 = (bf16[128,512]{1,0:T(8,128)(2,1)S(1)}, bf16[128,512]{1,0:T(8,128)(2,1)S(1)}, u32[]{:S(2)}, u32[]{:S(2)}) collective-permute-start(bf16[128,512]{1,0:T(8,128)(2,1)S(1)} %get-tuple-element.47), channel_id=1, source_target_pairs={{0,32},{32,0},{1,33},{33,1},{2,34},{34,2},{3,35},{35,3},{4,36},{36... | collective-permute-start | bytes 393224 | tf_op jit(solution)/shard_map/ppermute | solution.py:36
  24.2 2.8 %copy-start.1 = (bf16[1024,3072]{1,0:T(8,128)(2,1)S(1)}, bf16[1024,3072]{1,0:T(8,128)(2,1)}, u32[]{:S(2)}) copy-start(bf16[1024,3072]{1,0:T(8,128)(2,1)} %refs_3_.7) | copy-start | bytes 18874372
  42.1 20.4 %slice-start = ((s8[6291456]{0:T(1024)(128)(4,1)}), s8[4194304]{0:T(1024)(128)(4,1)S(1)}, s32[]{:S(2)}) async-start(s8[6291456]{0:T(1024)(128)(4,1)} %bitcast.7), calls=%async_computation.2 | async-start | bytes 8388608
  45.8 16.7 %slice-start.1 = ((s8[6291456]{0:T(1024)(128)(4,1)}), s8[2097152]{0:T(1024)(128)(4,1)S(1)}, s32[]{:S(2)}) async-start(s8[6291456]{0:T(1024)(128)(4,1)} %bitcast.7), calls=%async_computation.3 | async-start | bytes 4194304
  45.9 16.7 %copy-start.2 = (bf16[1024,1024]{1,0:T(8,128)(2,1)S(1)}, bf16[1024,1024]{1,0:T(8,128)(2,1)}, u32[]{:S(2)}) copy-start(bf16[1024,1024]{1,0:T(8,128)(2,1)} %refs_8_.1) | copy-start | bytes 6291460
  45.9 16.7 %copy-start.3 = (bf16[1,128,1024]{2,1,0:T(8,128)(2,1)S(1)}, bf16[1,128,1024]{2,1,0:T(8,128)(2,1)}, u32[]{:S(2)}) copy-start(bf16[1,128,1024]{2,1,0:T(8,128)(2,1)} %param.6) | copy-start | bytes 786436
  45.9 15.2 %collective-permute-start.7 = (bf16[256,512]{1,0:T(8,128)(2,1)S(1)}, bf16[256,512]{1,0:T(8,128)(2,1)S(1)}, u32[]{:S(2)}, u32[]{:S(2)}) collective-permute-start(bf16[256,512]{1,0:T(8,128)(2,1)S(1)} %pad_maximum_fusion.1.refs_0_), channel_id=1, source_target_pairs={{0,1},{1,2},{2,3},{3,0},{4,5},{5,6},{6,7},{7,4},{8,9},{9,10},{10,1... | collective-permute-start | bytes 786440 | tf_op jit(solution)/shard_map/ppermute | solution.py:41
  47.7 13.4 %collective-permute-start.8 = (bf16[256,512]{1,0:T(8,128)(2,1)S(1)}, bf16[256,512]{1,0:T(8,128)(2,1)S(1)}, u32[]{:S(2)}, u32[]{:S(2)}) collective-permute-start(bf16[256,512]{1,0:T(8,128)(2,1)S(1)} %pad_maximum_fusion.1.refs_0_), channel_id=1, source_target_pairs={{0,2},{1,3},{2,0},{3,1},{4,6},{5,7},{6,4},{7,5},{8,10},{9,11},{10,... | collective-permute-start | bytes 786440 | tf_op jit(solution)/shard_map/ppermute | solution.py:41
  49.3 11.8 %collective-permute-start.9 = (bf16[256,512]{1,0:T(8,128)(2,1)S(1)}, bf16[256,512]{1,0:T(8,128)(2,1)S(1)}, u32[]{:S(2)}, u32[]{:S(2)}) collective-permute-start(bf16[256,512]{1,0:T(8,128)(2,1)S(1)} %pad_maximum_fusion.1.refs_0_), channel_id=1, source_target_pairs={{0,3},{1,0},{2,1},{3,2},{4,7},{5,4},{6,5},{7,6},{8,11},{9,8},{10,9... | collective-permute-start | bytes 786440 | tf_op jit(solution)/shard_map/ppermute | solution.py:41
  50.9 10.2 %collective-permute-start.5 = (bf16[1040,128]{1,0:T(8,128)(2,1)S(1)}, bf16[1040,128]{1,0:T(8,128)(2,1)S(1)}, u32[]{:S(2)}, u32[]{:S(2)}) collective-permute-start(bf16[1040,128]{1,0:T(8,128)(2,1)S(1)} %collective-permute-done.3.refs_0_), channel_id=1, source_target_pairs={{0,4},{1,5},{2,6},{3,7},{4,8},{5,9},{6,10},{7,11},{8,12},{9,13},{1... | collective-permute-start | bytes 798728 | tf_op jit(solution)/shard_map/ppermute | solution.py:32
  52.8 9.7 %collective-permute-start.6 = (bf16[1040,128]{1,0:T(8,128)(2,1)S(1)}, bf16[1040,128]{1,0:T(8,128)(2,1)S(1)}, u32[]{:S(2)}, u32[]{:S(2)}) collective-permute-start(bf16[1040,128]{1,0:T(8,128)(2,1)S(1)} %collective-permute-done.4.refs_1_), channel_id=1, source_target_pairs={{0,28},{1,29},{2,30},{3,31},{4,0},{5,1},{6,2},{7,3},{8,4},{9,5},{1... | collective-permute-start | bytes 798728 | tf_op jit(solution)/shard_map/ppermute | solution.py:32
  74.0 1.5 %collective-permute-start.12 = (bf16[4,256,128]{2,1,0:T(8,128)(2,1)S(1)}, bf16[4,256,128]{2,1,0:T(8,128)(2,1)S(1)}, u32[]{:S(2)}, u32[]{:S(2)}) collective-permute-start(bf16[4,256,128]{2,1,0:T(8,128)(2,1)S(1)} %all_to_all.10.own_ref), channel_id=1, source_target_pairs={{0,32},{32,0},{1,33},{33,1},{2,34},{34,2},{3,35},{35,3},{4,36},{36... | collective-permute-start | bytes 786440 | tf_op jit(solution)/shard_map/ppermute | solution.py:36

commit v7 on v5

--- a/solution.py
+++ b/solution.py
@@ -23,7 +23,7 @@
 AHEAD = 2
 F32 = jnp.float32
 BF16 = jnp.bfloat16
-LIMIT = pltpu.CompilerParams(vmem_limit_bytes=40 * 1024 * 1024)
+LIMIT = pltpu.CompilerParams(vmem_limit_bytes=24 * 1024 * 1024)
 
 
 def shifted(block, distance):
@@ -318,20 +318,19 @@
     left1, right1 = shifted(own, 1), shifted(own, -1)
     left4, right4 = shifted(own, 4), shifted(own, -4)
     received = core_swapped(theirs)
-    left2, right2 = shifted(left1, 1), shifted(right1, -1)
-    left4, right4, near1, near2 = lax.optimization_barrier((left4, right4, left1, right1))
-    near = jnp.concatenate([near1, near2], axis=0)
+    queries, *state = own_block(own, w_qkv)
+    left1, right1, queries = lax.optimization_barrier((left1, right1, queries))
+    near = jnp.concatenate([left1, right1], axis=0)
     left_two, right_two = shifted(near, 4), shifted(near, -4)
-    held, near = lax.optimization_barrier((own, near))
-    queries, *state = own_block(held, w_qkv)
     state = absorb_stage(
         own, (left1, left4, right1, right4), ((0, 0), (1, 0)), ((2, 0), (3, 0)), queries, w_qkv, state
     )
     both = jnp.concatenate([mine, received], axis=0)
-    both, left2, right2, *state = lax.optimization_barrier((both, left2, right2, *state))
-    left6, right6 = shifted(left2, 4), shifted(right2, -4)
+    both, near1, near2, *state = lax.optimization_barrier((both, left1, right1, *state))
+    left2, right2 = shifted(near1, 1), shifted(near2, -1)
     grads = [both, *[turned(both, d) for d in range(1, n_y)]]
     state = absorb_stage(own, (left2, right2), ((0, 0),), ((1, 0),), queries, w_qkv, state)
+    left6, right6 = shifted(left_two[:PACKED], 1), shifted(right_two[PACKED:], -1)
     state = absorb_stage(
         own, (left_two, right_two), ((0, 1), (0, 0)), ((1, 0), (1, 1)), queries, w_qkv, state
     )

time: 92.9 us -> 94.1 us (1.013)
  the two profiles are of different devices: /device:TPU:4 before, /device:TPU:32 now
where the time goes in v7:
time: 94.1 us; the launch traced here: 93.2 us
  blocking collectives  34.8 us (37%)
  starting transfers between devices  23.9 us (25%)
  waiting for transfers between devices  16.5 us (18%)
  Pallas kernels  12.6 us (13%)
  local copies, waits for them, and re-layouts  3.86 us (4%)
    all_to_all x1, blocking collectives, local(): lax.all_to_all(share.reshape(-1, WIDTH // N_SEQ, LANES), ('x', 'z'), 0, 0...  23.2 us
    ppermute x10, starting transfers between devices, shifted(): return lax.ppermute(block, SEQ, route)  21.8 us
    all_to_all x1, blocking collectives, local(): pieces = lax.all_to_all(attended, 'y', 0, 0, tiled=True)  11.6 us
    ppermute x10, waiting for transfers between devices, shifted(): return lax.ppermute(block, SEQ, route)  10.9 us
    pallas_call x3, Pallas kernels, absorb_stage(): pl.pallas_call(kernel, out_shape=list(STATE_SHAPES), compiler_params=LIMI...  6.88 us
    ppermute x3, waiting for transfers between devices, turned(): return lax.ppermute(block, 'y', [(i, (i + distance) % n) for i in range(n)])  4.07 us
    unnamed x17, local copies, waits for them, and re-layouts  3.79 us
    ppermute x3, starting transfers between devices, turned(): return lax.ppermute(block, 'y', [(i, (i + distance) % n) for i in range(n)])  2.11 us
  transfers between devices with their start and end apart: 15, of which 6 were waited for; matrix products, arithmetic and copies ran while one was open for 0% of the time, Pallas kernels for 9%

profile of v7, /device:TPU:32, one launch (start us, length us, event | category | flops | bytes accessed | tf_op | source)
XLA Modules:
  0.0 93.2 jit_solution(17791147564113230264)
XLA Ops:
  0.6 2.1 %layer_norm.1 = (bf16[1040,128]{1,0:T(8,128)(2,1)}, bf16[128,512]{1,0:T(8,128)(2,1)}, bf16[128,512]{1,0:T(8,128)(2,1)}) custom-call(s32[1]{0:T(128)} %bitcast.core_ref, bf16[128,1024]{1,0:T(8,128)(2,1)} %bitcast.9, s32[1,128]{1,0:T(1,128)} %ids_hbm.1, f32[1,1024]{1,0:T(1,128)} %bitcast.13, bf16[128,1024]{1,0:T(8,128)(2,1)} %bitcast.12), custom_call_target="tpu_custom_call" | custom-call | tf_op jit(solution)/shard_map/layer_norm/pallas_call | solution.py:75
  2.7 1.7 %collective-permute-start = (bf16[1040,128]{1,0:T(8,128)(2,1)}, bf16[1040,128]{1,0:T(8,128)(2,1)S(1)}, u32[]{:S(2)}, u32[]{:S(2)}) collective-permute-start(bf16[1040,128]{1,0:T(8,128)(2,1)} %get-tuple-element.38.own_ref), channel_id=1, source_target_pairs={{0,1},{1,2},{2,3},{3,4},{4,5},{5,6},{6,7},{7,8},{8,9},{9,10},{10,1... | collective-permute-start | bytes 798728 | tf_op jit(solution)/shard_map/ppermute | solution.py:32
  4.4 2.6 %collective-permute-start.1 = (bf16[1040,128]{1,0:T(8,128)(2,1)}, bf16[1040,128]{1,0:T(8,128)(2,1)S(1)}, u32[]{:S(2)}, u32[]{:S(2)}) collective-permute-start(bf16[1040,128]{1,0:T(8,128)(2,1)} %get-tuple-element.38.own_ref), channel_id=1, source_target_pairs={{0,31},{1,0},{2,1},{3,2},{4,3},{5,4},{6,5},{7,6},{8,7},{9,8},{10,9... | collective-permute-start | bytes 798728 | tf_op jit(solution)/shard_map/ppermute | solution.py:32
  6.9 1.9 %collective-permute-start.7 = (bf16[1040,128]{1,0:T(8,128)(2,1)}, bf16[1040,128]{1,0:T(8,128)(2,1)S(1)}, u32[]{:S(2)}, u32[]{:S(2)}) collective-permute-start(bf16[1040,128]{1,0:T(8,128)(2,1)} %get-tuple-element.38.own_ref), channel_id=1, source_target_pairs={{0,4},{1,5},{2,6},{3,7},{4,8},{5,9},{6,10},{7,11},{8,12},{9,13},{1... | collective-permute-start | bytes 798728 | tf_op jit(solution)/shard_map/ppermute | solution.py:32
  8.8 2.5 %collective-permute-start.8 = (bf16[1040,128]{1,0:T(8,128)(2,1)}, bf16[1040,128]{1,0:T(8,128)(2,1)S(1)}, u32[]{:S(2)}, u32[]{:S(2)}) collective-permute-start(bf16[1040,128]{1,0:T(8,128)(2,1)} %get-tuple-element.38.own_ref), channel_id=1, source_target_pairs={{0,28},{1,29},{2,30},{3,31},{4,0},{5,1},{6,2},{7,3},{8,4},{9,5},{1... | collective-permute-start | bytes 798728 | tf_op jit(solution)/shard_map/ppermute | solution.py:32
  11.3 2.8 %copy-done = bf16[1024,3072]{1,0:T(8,128)(2,1)S(1)} copy-done((bf16[1024,3072]{1,0:T(8,128)(2,1)S(1)}, bf16[1024,3072]{1,0:T(8,128)(2,1)}, u32[]{:S(2)}) %copy-start) | copy-done | bytes 6291480
  14.1 0.9 %copy-done.1 = bf16[1040,128]{1,0:T(8,128)(2,1)S(1)} copy-done((bf16[1040,128]{1,0:T(8,128)(2,1)S(1)}, bf16[1040,128]{1,0:T(8,128)(2,1)}, u32[]{:S(2)}) %copy-start.1) | copy-done | bytes 266264
  15.0 1.9 %own_block.1 = (bf16[8,128,256]{2,1,0:T(8,128)(2,1)S(1)}, f32[16,128]{1,0:T(8,128)S(1)}, f32[16,128]{1,0:T(8,128)S(1)}, f32[1024,128]{1,0:T(8,128)S(1)}) custom-call(bf16[1040,128]{1,0:T(8,128)(2,1)S(1)} %copy-done.1, bf16[1024,3072]{1,0:T(8,128)(2,1)S(1)} %copy-done), custom_call_target="tpu_custom_call" | custom-call | flops 1610612736 | bytes 8388608 | tf_op jit(solution)/shard_map/own_block/pallas_call | solution.py:194
  17.1 3.3 %collective-permute-start.4 = (bf16[2080,128]{1,0:T(8,128)(2,1)S(1)}, bf16[2080,128]{1,0:T(8,128)(2,1)S(1)}, u32[]{:S(2)}, u32[]{:S(2)}) collective-permute-start(bf16[2080,128]{1,0:T(8,128)(2,1)S(1)} %constant_dynamic-update-slice_fusion), channel_id=1, source_target_pairs={{0,28},{1,29},{2,30},{3,31},{4,0},{5,1},{6,2},{7,3},{8,4},{9,5},{1... | collective-permute-start | bytes 1597448 | tf_op jit(solution)/shard_map/ppermute | solution.py:32
  20.6 4.2 %absorb_stage.3 = (f32[16,128]{1,0:T(8,128)S(1)}, f32[16,128]{1,0:T(8,128)S(1)}, f32[1024,128]{1,0:T(8,128)S(1)}) custom-call(bf16[1040,128]{1,0:T(8,128)(2,1)S(1)} %copy-done.1, bf16[1040,128]{1,0:T(8,128)(2,1)S(1)} %collective-permute-done.refs_0_, bf16[1040,128]{1,0:T(8,128)(2,1)S(1)} %collective-permute-done.7.refs_1_, ...), custom_call_target="tpu_custom_call" | custom-call | flops 2147483648 | bytes 8388608 | tf_op jit(solution)/shard_map/absorb_stage/pallas_call | solution.py:235
  24.8 4.1 %collective-permute-start.13 = (bf16[1040,128]{1,0:T(8,128)(2,1)S(1)}, bf16[1040,128]{1,0:T(8,128)(2,1)S(1)}, u32[]{:S(2)}, u32[]{:S(2)}) collective-permute-start(bf16[1040,128]{1,0:T(8,128)(2,1)S(1)} %collective-permute-done.1.refs_2_), channel_id=1, source_target_pairs={{0,31},{1,0},{2,1},{3,2},{4,3},{5,4},{6,5},{7,6},{8,7},{9,8},{10,9... | collective-permute-start | bytes 798728 | tf_op jit(solution)/shard_map/ppermute | solution.py:32
  29.0 4.1 %collective-permute-done.2.refs_0_ = bf16[2080,128]{1,0:T(8,128)(2,1)S(1)} collective-permute-done((bf16[2080,128]{1,0:T(8,128)(2,1)S(1)}, bf16[2080,128]{1,0:T(8,128)(2,1)S(1)}, u32[]{:S(2)}, u32[]{:S(2)}) %collective-permute-start.2) | collective-permute-done | bytes 532512 | tf_op jit(solution)/shard_map/ppermute | solution.py:32
  33.1 1.1 %collective-permute-start.11 = (bf16[256,512]{1,0:T(8,128)(2,1)S(1)}, bf16[256,512]{1,0:T(8,128)(2,1)S(1)}, u32[]{:S(2)}, u32[]{:S(2)}) collective-permute-start(bf16[256,512]{1,0:T(8,128)(2,1)S(1)} %pad_maximum_fusion.refs_0_), channel_id=1, source_target_pairs={{0,3},{1,0},{2,1},{3,2},{4,7},{5,4},{6,5},{7,6},{8,11},{9,8},{10,9... | collective-permute-start | bytes 786440 | tf_op jit(solution)/shard_map/ppermute | solution.py:41
  34.2 1.0 %collective-permute-start.9 = (bf16[256,512]{1,0:T(8,128)(2,1)S(1)}, bf16[256,512]{1,0:T(8,128)(2,1)S(1)}, u32[]{:S(2)}, u32[]{:S(2)}) collective-permute-start(bf16[256,512]{1,0:T(8,128)(2,1)S(1)} %pad_maximum_fusion.refs_0_), channel_id=1, source_target_pairs={{0,1},{1,2},{2,3},{3,0},{4,5},{5,6},{6,7},{7,4},{8,9},{9,10},{10,1... | collective-permute-start | bytes 786440 | tf_op jit(solution)/shard_map/ppermute | solution.py:41
  35.3 6.6 %collective-permute-done.12.refs_0_ = bf16[1040,128]{1,0:T(8,128)(2,1)S(1)} collective-permute-done((bf16[1040,128]{1,0:T(8,128)(2,1)S(1)}, bf16[1040,128]{1,0:T(8,128)(2,1)S(1)}, u32[]{:S(2)}, u32[]{:S(2)}) %collective-permute-start.12) | collective-permute-done | bytes 266272 | tf_op jit(solution)/shard_map/ppermute | solution.py:32
  41.9 5.6 %collective-permute-start.5 = (bf16[1040,128]{1,0:T(8,128)(2,1)S(1)}, bf16[1040,128]{1,0:T(8,128)(2,1)S(1)}, u32[]{:S(2)}, u32[]{:S(2)}) collective-permute-start(bf16[1040,128]{1,0:T(8,128)(2,1)S(1)} %slice.9), channel_id=1, source_target_pairs={{0,31},{1,0},{2,1},{3,2},{4,3},{5,4},{6,5},{7,6},{8,7},{9,8},{10,9... | collective-permute-start | bytes 798728 | tf_op jit(solution)/shard_map/ppermute | solution.py:32
  47.5 2.6 %absorb_stage.4 = (f32[16,128]{1,0:T(8,128)S(1)}, f32[16,128]{1,0:T(8,128)S(1)}, f32[1024,128]{1,0:T(8,128)S(1)}) custom-call(bf16[1040,128]{1,0:T(8,128)(2,1)S(1)} %copy-done.1, bf16[1040,128]{1,0:T(8,128)(2,1)S(1)} %collective-permute-done.12.refs_0_, bf16[1040,128]{1,0:T(8,128)(2,1)S(1)} %collective-permute-done.13.refs_1_, ...), custom_call_target="tpu_custom_call" | custom-call | flops 1073741824 | bytes 8388608 | tf_op jit(solution)/shard_map/absorb_stage/pallas_call | solution.py:235
  50.3 4.1 %collective-permute-done.11.refs_3_ = bf16[256,512]{1,0:T(8,128)(2,1)S(1)} collective-permute-done((bf16[256,512]{1,0:T(8,128)(2,1)S(1)}, bf16[256,512]{1,0:T(8,128)(2,1)S(1)}, u32[]{:S(2)}, u32[]{:S(2)}) %collective-permute-start.11) | collective-permute-done | bytes 262176 | tf_op jit(solution)/shard_map/ppermute | solution.py:41
  54.5 1.3 %last_stage.1 = (bf16[4,256,128]{2,1,0:T(8,128)(2,1)S(1)}, bf16[128,1024]{1,0:T(8,128)(2,1)}) custom-call(bf16[1040,128]{1,0:T(8,128)(2,1)S(1)} %copy-done.2, bf16[1040,128]{1,0:T(8,128)(2,1)S(1)} %collective-permute-done.3.refs_0_, bf16[1040,128]{1,0:T(8,128)(2,1)S(1)} %collective-permute-done.5.refs_1_, ...), custom_call_target="tpu_custom_call" | custom-call | flops 1610612736 | bytes 10485760 | tf_op jit(solution)/shard_map/last_stage/pallas_call | solution.py:272
  55.8 11.6 %all_to_all.10.own_ref = bf16[4,256,128]{2,1,0:T(8,128)(2,1)S(1)} all-to-all(bf16[4,256,128]{2,1,0:T(8,128)(2,1)S(1)} %get-tuple-element.69), channel_id=1, replica_groups=mesh['x'=4,'core'=2,'z'=8,'y'=4] {'y'}, dimensions={0} | all-to-all | bytes 524288 | tf_op jit(solution)/shard_map/all_to_all | solution.py:342
  67.4 1.5 %collective-permute-done.14.other_ref = bf16[4,256,128]{2,1,0:T(8,128)(2,1)S(1)} collective-permute-done((bf16[4,256,128]{2,1,0:T(8,128)(2,1)S(1)}, bf16[4,256,128]{2,1,0:T(8,128)(2,1)S(1)}, u32[]{:S(2)}, u32[]{:S(2)}) %collective-permute-start.14) | collective-permute-done | bytes 262176 | tf_op jit(solution)/shard_map/ppermute | solution.py:36
  68.9 0.4 grad_product.1
  69.3 23.2 %all_to_all.11 = bf16[32,32,128]{2,1,0:T(8,128)(2,1)S(1)} all-to-all(bf16[32,32,128]{2,1,0:T(8,128)(2,1)S(1)} %bitcast.11), channel_id=1, replica_groups=mesh['x'=4,'core'=2,'z'=8,'y'=4] {'x','z'}, dimensions={0} | all-to-all | bytes 524288 | tf_op jit(solution)/shard_map/all_to_all | solution.py:344
  92.6 0.6 broadcast_multiply_fusion
  (39 shorter events, 0.7 us)
Async XLA Ops:
  2.7 14.2 %collective-permute-start = (bf16[1040,128]{1,0:T(8,128)(2,1)}, bf16[1040,128]{1,0:T(8,128)(2,1)S(1)}, u32[]{:S(2)}, u32[]{:S(2)}) collective-permute-start(bf16[1040,128]{1,0:T(8,128)(2,1)} %get-tuple-element.38.own_ref), channel_id=1, source_target_pairs={{0,1},{1,2},{2,3},{3,4},{4,5},{5,6},{6,7},{7,8},{8,9},{9,10},{10,1... | collective-permute-start | bytes 798728 | tf_op jit(solution)/shard_map/ppermute | solution.py:32
  4.4 12.6 %collective-permute-start.1 = (bf16[1040,128]{1,0:T(8,128)(2,1)}, bf16[1040,128]{1,0:T(8,128)(2,1)S(1)}, u32[]{:S(2)}, u32[]{:S(2)}) collective-permute-start(bf16[1040,128]{1,0:T(8,128)(2,1)} %get-tuple-element.38.own_ref), channel_id=1, source_target_pairs={{0,31},{1,0},{2,1},{3,2},{4,3},{5,4},{6,5},{7,6},{8,7},{9,8},{10,9... | collective-permute-start | bytes 798728 | tf_op jit(solution)/shard_map/ppermute | solution.py:32
  6.9 13.5 %collective-permute-start.7 = (bf16[1040,128]{1,0:T(8,128)(2,1)}, bf16[1040,128]{1,0:T(8,128)(2,1)S(1)}, u32[]{:S(2)}, u32[]{:S(2)}) collective-permute-start(bf16[1040,128]{1,0:T(8,128)(2,1)} %get-tuple-element.38.own_ref), channel_id=1, source_target_pairs={{0,4},{1,5},{2,6},{3,7},{4,8},{5,9},{6,10},{7,11},{8,12},{9,13},{1... | collective-permute-start | bytes 798728 | tf_op jit(solution)/shard_map/ppermute | solution.py:32
  8.8 11.7 %collective-permute-start.8 = (bf16[1040,128]{1,0:T(8,128)(2,1)}, bf16[1040,128]{1,0:T(8,128)(2,1)S(1)}, u32[]{:S(2)}, u32[]{:S(2)}) collective-permute-start(bf16[1040,128]{1,0:T(8,128)(2,1)} %get-tuple-element.38.own_ref), channel_id=1, source_target_pairs={{0,28},{1,29},{2,30},{3,31},{4,0},{5,1},{6,2},{7,3},{8,4},{9,5},{1... | collective-permute-start | bytes 798728 | tf_op jit(solution)/shard_map/ppermute | solution.py:32
  11.3 9.1 %collective-permute-start.6 = (bf16[128,512]{1,0:T(8,128)(2,1)}, bf16[128,512]{1,0:T(8,128)(2,1)S(1)}, u32[]{:S(2)}, u32[]{:S(2)}) collective-permute-start(bf16[128,512]{1,0:T(8,128)(2,1)} %get-tuple-element.43), channel_id=1, source_target_pairs={{0,32},{32,0},{1,33},{33,1},{2,34},{34,2},{3,35},{35,3},{4,36},{36... | collective-permute-start | bytes 393224 | tf_op jit(solution)/shard_map/ppermute | solution.py:36
  11.3 2.8 %copy-start = (bf16[1024,3072]{1,0:T(8,128)(2,1)S(1)}, bf16[1024,3072]{1,0:T(8,128)(2,1)}, u32[]{:S(2)}) copy-start(bf16[1024,3072]{1,0:T(8,128)(2,1)} %refs_3_.5) | copy-start | bytes 18874372
  14.1 1.0 %copy-start.1 = (bf16[1040,128]{1,0:T(8,128)(2,1)S(1)}, bf16[1040,128]{1,0:T(8,128)(2,1)}, u32[]{:S(2)}) copy-start(bf16[1040,128]{1,0:T(8,128)(2,1)} %get-tuple-element.38.own_ref) | copy-start | bytes 798724
  15.0 5.4 %copy-start.5 = (bf16[128,512]{1,0:T(8,128)(2,1)S(1)}, bf16[128,512]{1,0:T(8,128)(2,1)}, u32[]{:S(2)}) copy-start(bf16[128,512]{1,0:T(8,128)(2,1)} %get-tuple-element.42) | copy-start | bytes 393220
  17.0 16.1 %collective-permute-start.2 = (bf16[2080,128]{1,0:T(8,128)(2,1)S(1)}, bf16[2080,128]{1,0:T(8,128)(2,1)S(1)}, u32[]{:S(2)}, u32[]{:S(2)}) collective-permute-start(bf16[2080,128]{1,0:T(8,128)(2,1)S(1)} %constant_dynamic-update-slice_fusion), channel_id=1, source_target_pairs={{0,4},{1,5},{2,6},{3,7},{4,8},{5,9},{6,10},{7,11},{8,12},{9,13},{1... | collective-permute-start | bytes 1597448 | tf_op jit(solution)/shard_map/ppermute | solution.py:32
  17.1 17.1 %collective-permute-start.4 = (bf16[2080,128]{1,0:T(8,128)(2,1)S(1)}, bf16[2080,128]{1,0:T(8,128)(2,1)S(1)}, u32[]{:S(2)}, u32[]{:S(2)}) collective-permute-start(bf16[2080,128]{1,0:T(8,128)(2,1)S(1)} %constant_dynamic-update-slice_fusion), channel_id=1, source_target_pairs={{0,28},{1,29},{2,30},{3,31},{4,0},{5,1},{6,2},{7,3},{8,4},{9,5},{1... | collective-permute-start | bytes 1597448 | tf_op jit(solution)/shard_map/ppermute | solution.py:32
  24.7 17.1 %collective-permute-start.12 = (bf16[1040,128]{1,0:T(8,128)(2,1)S(1)}, bf16[1040,128]{1,0:T(8,128)(2,1)S(1)}, u32[]{:S(2)}, u32[]{:S(2)}) collective-permute-start(bf16[1040,128]{1,0:T(8,128)(2,1)S(1)} %collective-permute-done.refs_0_), channel_id=1, source_target_pairs={{0,1},{1,2},{2,3},{3,4},{4,5},{5,6},{6,7},{7,8},{8,9},{9,10},{10,1... | collective-permute-start | bytes 798728 | tf_op jit(solution)/shard_map/ppermute | solution.py:32
  24.8 17.1 %collective-permute-start.13 = (bf16[1040,128]{1,0:T(8,128)(2,1)S(1)}, bf16[1040,128]{1,0:T(8,128)(2,1)S(1)}, u32[]{:S(2)}, u32[]{:S(2)}) collective-permute-start(bf16[1040,128]{1,0:T(8,128)(2,1)S(1)} %collective-permute-done.1.refs_2_), channel_id=1, source_target_pairs={{0,31},{1,0},{2,1},{3,2},{4,3},{5,4},{6,5},{7,6},{8,7},{9,8},{10,9... | collective-permute-start | bytes 798728 | tf_op jit(solution)/shard_map/ppermute | solution.py:32
  29.0 21.3 %collective-permute-start.10 = (bf16[256,512]{1,0:T(8,128)(2,1)S(1)}, bf16[256,512]{1,0:T(8,128)(2,1)S(1)}, u32[]{:S(2)}, u32[]{:S(2)}) collective-permute-start(bf16[256,512]{1,0:T(8,128)(2,1)S(1)} %pad_maximum_fusion.refs_0_), channel_id=1, source_target_pairs={{0,2},{1,3},{2,0},{3,1},{4,6},{5,7},{6,4},{7,5},{8,10},{9,11},{10,... | collective-permute-start | bytes 786440 | tf_op jit(solution)/shard_map/ppermute | solution.py:41
  33.1 21.3 %collective-permute-start.11 = (bf16[256,512]{1,0:T(8,128)(2,1)S(1)}, bf16[256,512]{1,0:T(8,128)(2,1)S(1)}, u32[]{:S(2)}, u32[]{:S(2)}) collective-permute-start(bf16[256,512]{1,0:T(8,128)(2,1)S(1)} %pad_maximum_fusion.refs_0_), channel_id=1, source_target_pairs={{0,3},{1,0},{2,1},{3,2},{4,7},{5,4},{6,5},{7,6},{8,11},{9,8},{10,9... | collective-permute-start | bytes 786440 | tf_op jit(solution)/shard_map/ppermute | solution.py:41
  34.2 20.2 %collective-permute-start.9 = (bf16[256,512]{1,0:T(8,128)(2,1)S(1)}, bf16[256,512]{1,0:T(8,128)(2,1)S(1)}, u32[]{:S(2)}, u32[]{:S(2)}) collective-permute-start(bf16[256,512]{1,0:T(8,128)(2,1)S(1)} %pad_maximum_fusion.refs_0_), channel_id=1, source_target_pairs={{0,1},{1,2},{2,3},{3,0},{4,5},{5,6},{6,7},{7,4},{8,9},{9,10},{10,1... | collective-permute-start | bytes 786440 | tf_op jit(solution)/shard_map/ppermute | solution.py:41
  41.9 12.5 %collective-permute-start.3 = (bf16[1040,128]{1,0:T(8,128)(2,1)S(1)}, bf16[1040,128]{1,0:T(8,128)(2,1)S(1)}, u32[]{:S(2)}, u32[]{:S(2)}) collective-permute-start(bf16[1040,128]{1,0:T(8,128)(2,1)S(1)} %slice.8), channel_id=1, source_target_pairs={{0,1},{1,2},{2,3},{3,4},{4,5},{5,6},{6,7},{7,8},{8,9},{9,10},{10,1... | collective-permute-start | bytes 798728 | tf_op jit(solution)/shard_map/ppermute | solution.py:32
  41.9 12.5 %collective-permute-start.5 = (bf16[1040,128]{1,0:T(8,128)(2,1)S(1)}, bf16[1040,128]{1,0:T(8,128)(2,1)S(1)}, u32[]{:S(2)}, u32[]{:S(2)}) collective-permute-start(bf16[1040,128]{1,0:T(8,128)(2,1)S(1)} %slice.9), channel_id=1, source_target_pairs={{0,31},{1,0},{2,1},{3,2},{4,3},{5,4},{6,5},{7,6},{8,7},{9,8},{10,9... | collective-permute-start | bytes 798728 | tf_op jit(solution)/shard_map/ppermute | solution.py:32
  47.5 6.9 %slice-start = ((s8[6291456]{0:T(1024)(128)(4,1)}), s8[4194304]{0:T(1024)(128)(4,1)S(1)}, s32[]{:S(2)}) async-start(s8[6291456]{0:T(1024)(128)(4,1)} %bitcast.7), calls=%async_computation.2 | async-start | bytes 8388608
  50.1 4.3 %copy-start.2 = (bf16[1040,128]{1,0:T(8,128)(2,1)S(1)}, bf16[1040,128]{1,0:T(8,128)(2,1)}, u32[]{:S(2)}) copy-start(bf16[1040,128]{1,0:T(8,128)(2,1)} %get-tuple-element.38.own_ref) | copy-start | bytes 798724
  50.1 4.3 %copy-start.3 = (bf16[1024,1024]{1,0:T(8,128)(2,1)S(1)}, bf16[1024,1024]{1,0:T(8,128)(2,1)}, u32[]{:S(2)}) copy-start(bf16[1024,1024]{1,0:T(8,128)(2,1)} %refs_8_.1) | copy-start | bytes 6291460
  50.1 4.3 %copy-start.4 = (bf16[1,128,1024]{2,1,0:T(8,128)(2,1)S(1)}, bf16[1,128,1024]{2,1,0:T(8,128)(2,1)}, u32[]{:S(2)}) copy-start(bf16[1,128,1024]{2,1,0:T(8,128)(2,1)} %param.6) | copy-start | bytes 786436
  50.2 4.3 %slice-start.1 = ((s8[6291456]{0:T(1024)(128)(4,1)}), s8[2097152]{0:T(1024)(128)(4,1)S(1)}, s32[]{:S(2)}) async-start(s8[6291456]{0:T(1024)(128)(4,1)} %bitcast.7), calls=%async_computation.3 | async-start | bytes 4194304
  67.4 1.5 %collective-permute-start.14 = (bf16[4,256,128]{2,1,0:T(8,128)(2,1)S(1)}, bf16[4,256,128]{2,1,0:T(8,128)(2,1)S(1)}, u32[]{:S(2)}, u32[]{:S(2)}) collective-permute-start(bf16[4,256,128]{2,1,0:T(8,128)(2,1)S(1)} %all_to_all.10.own_ref), channel_id=1, source_target_pairs={{0,32},{32,0},{1,33},{33,1},{2,34},{34,2},{3,35},{35,3},{4,36},{36... | collective-permute-start | bytes 786440 | tf_op jit(solution)/shard_map/ppermute | solution.py:36

commit v8 on v7

--- a/solution.py
+++ b/solution.py
@@ -325,19 +325,20 @@
     state = absorb_stage(
         own, (left1, left4, right1, right4), ((0, 0), (1, 0)), ((2, 0), (3, 0)), queries, w_qkv, state
     )
+    near1, near2, *state = lax.optimization_barrier((left1, right1, *state))
+    left2, right2 = shifted(near1, 1), shifted(near2, -1)
     both = jnp.concatenate([mine, received], axis=0)
-    both, near1, near2, *state = lax.optimization_barrier((both, left1, right1, *state))
-    left2, right2 = shifted(near1, 1), shifted(near2, -1)
+    both, left_two, right_two = lax.optimization_barrier((both, left_two, right_two))
+    left6, right6 = shifted(left_two[:PACKED], 1), shifted(right_two[PACKED:], -1)
     grads = [both, *[turned(both, d) for d in range(1, n_y)]]
     state = absorb_stage(own, (left2, right2), ((0, 0),), ((1, 0),), queries, w_qkv, state)
-    left6, right6 = shifted(left_two[:PACKED], 1), shifted(right_two[PACKED:], -1)
     state = absorb_stage(
         own, (left_two, right_two), ((0, 1), (0, 0)), ((1, 0), (1, 1)), queries, w_qkv, state
     )
-    left6, right6, grads, state = lax.optimization_barrier((left6, right6, grads, state))
     attended, block_out = last_stage(
         own, (left6, right6), ((0, 0),), ((1, 0),), queries, w_qkv, state, frames, w_out
     )
+    attended, grads = lax.optimization_barrier((attended, grads))
 
     pieces = lax.all_to_all(attended, "y", 0, 0, tiled=True)
     share = grad_product(place, pieces, core_swapped(pieces), grads)

time: 94.1 us -> 91.8 us (0.976)
  the two profiles are of different devices: /device:TPU:32 before, /device:TPU:4 now
where the time goes in v8:
time: 91.8 us; the launch traced here: 90.3 us
  blocking collectives  30.2 us (33%)
  starting transfers between devices  26.8 us (29%)
  Pallas kernels  16.6 us (18%)
  waiting for transfers between devices  11.3 us (12%)
  local copies, waits for them, and re-layouts  3.86 us (4%)
    ppermute x10, starting transfers between devices, shifted(): return lax.ppermute(block, SEQ, route)  23.4 us
    all_to_all x1, blocking collectives, local(): lax.all_to_all(share.reshape(-1, WIDTH // N_SEQ, LANES), ('x', 'z'), 0, 0...  21.1 us
    pallas_call x3, Pallas kernels, absorb_stage(): pl.pallas_call(kernel, out_shape=list(STATE_SHAPES), compiler_params=LIMI...  10.9 us
    all_to_all x1, blocking collectives, local(): pieces = lax.all_to_all(attended, 'y', 0, 0, tiled=True)  9.06 us
    ppermute x10, waiting for transfers between devices, shifted(): return lax.ppermute(block, SEQ, route)  4.74 us
    unnamed x19, local copies, waits for them, and re-layouts  3.79 us
    ppermute x3, waiting for transfers between devices, turned(): return lax.ppermute(block, 'y', [(i, (i + distance) % n) for i in range(n)])  3.7 us
    ppermute x3, starting transfers between devices, turned(): return lax.ppermute(block, 'y', [(i, (i + distance) % n) for i in range(n)])  3.31 us
  transfers between devices with their start and end apart: 15, of which 6 were waited for; matrix products, arithmetic and copies ran while one was open for 0% of the time, Pallas kernels for 16%

profile of v8, /device:TPU:4, one launch (start us, length us, event | category | flops | bytes accessed | tf_op | source)
XLA Modules:
  0.0 90.3 jit_solution(15274664645608230494)
XLA Ops:
  0.6 2.1 %layer_norm.1 = (bf16[1040,128]{1,0:T(8,128)(2,1)}, bf16[128,512]{1,0:T(8,128)(2,1)}, bf16[128,512]{1,0:T(8,128)(2,1)}) custom-call(s32[1]{0:T(128)} %bitcast.core_ref, bf16[128,1024]{1,0:T(8,128)(2,1)} %bitcast.9, s32[1,128]{1,0:T(1,128)} %ids_hbm.1, f32[1,1024]{1,0:T(1,128)} %bitcast.13, bf16[128,1024]{1,0:T(8,128)(2,1)} %bitcast.12), custom_call_target="tpu_custom_call" | custom-call | tf_op jit(solution)/shard_map/layer_norm/pallas_call | solution.py:75
  2.7 1.7 %collective-permute-start.1 = (bf16[1040,128]{1,0:T(8,128)(2,1)}, bf16[1040,128]{1,0:T(8,128)(2,1)S(1)}, u32[]{:S(2)}, u32[]{:S(2)}) collective-permute-start(bf16[1040,128]{1,0:T(8,128)(2,1)} %get-tuple-element.36.own_ref), channel_id=1, source_target_pairs={{0,1},{1,2},{2,3},{3,4},{4,5},{5,6},{6,7},{7,8},{8,9},{9,10},{10,1... | collective-permute-start | bytes 798728 | tf_op jit(solution)/shard_map/ppermute | solution.py:32
  4.4 6.8 %collective-permute-start.2 = (bf16[1040,128]{1,0:T(8,128)(2,1)}, bf16[1040,128]{1,0:T(8,128)(2,1)S(1)}, u32[]{:S(2)}, u32[]{:S(2)}) collective-permute-start(bf16[1040,128]{1,0:T(8,128)(2,1)} %get-tuple-element.36.own_ref), channel_id=1, source_target_pairs={{0,31},{1,0},{2,1},{3,2},{4,3},{5,4},{6,5},{7,6},{8,7},{9,8},{10,9... | collective-permute-start | bytes 798728 | tf_op jit(solution)/shard_map/ppermute | solution.py:32
  11.2 3.2 %collective-permute-start.8 = (bf16[1040,128]{1,0:T(8,128)(2,1)}, bf16[1040,128]{1,0:T(8,128)(2,1)S(1)}, u32[]{:S(2)}, u32[]{:S(2)}) collective-permute-start(bf16[1040,128]{1,0:T(8,128)(2,1)} %get-tuple-element.36.own_ref), channel_id=1, source_target_pairs={{0,28},{1,29},{2,30},{3,31},{4,0},{5,1},{6,2},{7,3},{8,4},{9,5},{1... | collective-permute-start | bytes 798728 | tf_op jit(solution)/shard_map/ppermute | solution.py:32
  14.4 2.8 %copy-done = bf16[1024,3072]{1,0:T(8,128)(2,1)S(1)} copy-done((bf16[1024,3072]{1,0:T(8,128)(2,1)S(1)}, bf16[1024,3072]{1,0:T(8,128)(2,1)}, u32[]{:S(2)}) %copy-start) | copy-done | bytes 6291480
  17.2 0.9 %copy-done.1 = bf16[1040,128]{1,0:T(8,128)(2,1)S(1)} copy-done((bf16[1040,128]{1,0:T(8,128)(2,1)S(1)}, bf16[1040,128]{1,0:T(8,128)(2,1)}, u32[]{:S(2)}) %copy-start.1) | copy-done | bytes 266264
  18.2 1.9 %own_block.1 = (bf16[8,128,256]{2,1,0:T(8,128)(2,1)S(1)}, f32[16,128]{1,0:T(8,128)S(1)}, f32[16,128]{1,0:T(8,128)S(1)}, f32[1024,128]{1,0:T(8,128)S(1)}) custom-call(bf16[1040,128]{1,0:T(8,128)(2,1)S(1)} %copy-done.1, bf16[1024,3072]{1,0:T(8,128)(2,1)S(1)} %copy-done), custom_call_target="tpu_custom_call" | custom-call | flops 1610612736 | bytes 8388608 | tf_op jit(solution)/shard_map/own_block/pallas_call | solution.py:194
  20.3 3.2 %collective-permute-start.4 = (bf16[2080,128]{1,0:T(8,128)(2,1)S(1)}, bf16[2080,128]{1,0:T(8,128)(2,1)S(1)}, u32[]{:S(2)}, u32[]{:S(2)}) collective-permute-start(bf16[2080,128]{1,0:T(8,128)(2,1)S(1)} %constant_dynamic-update-slice_fusion), channel_id=1, source_target_pairs={{0,28},{1,29},{2,30},{3,31},{4,0},{5,1},{6,2},{7,3},{8,4},{9,5},{1... | collective-permute-start | bytes 1597448 | tf_op jit(solution)/shard_map/ppermute | solution.py:32
  23.5 4.2 %absorb_stage.3 = (f32[16,128]{1,0:T(8,128)S(1)}, f32[16,128]{1,0:T(8,128)S(1)}, f32[1024,128]{1,0:T(8,128)S(1)}) custom-call(bf16[1040,128]{1,0:T(8,128)(2,1)S(1)} %copy-done.1, bf16[1040,128]{1,0:T(8,128)(2,1)S(1)} %collective-permute-done.1.refs_0_, bf16[1040,128]{1,0:T(8,128)(2,1)S(1)} %collective-permute-done.7.refs_1_, ...), custom_call_target="tpu_custom_call" | custom-call | flops 2147483648 | bytes 8388608 | tf_op jit(solution)/shard_map/absorb_stage/pallas_call | solution.py:235
  27.7 2.8 %collective-permute-start.10 = (bf16[1040,128]{1,0:T(8,128)(2,1)S(1)}, bf16[1040,128]{1,0:T(8,128)(2,1)S(1)}, u32[]{:S(2)}, u32[]{:S(2)}) collective-permute-start(bf16[1040,128]{1,0:T(8,128)(2,1)S(1)} %collective-permute-done.2.refs_2_), channel_id=1, source_target_pairs={{0,31},{1,0},{2,1},{3,2},{4,3},{5,4},{6,5},{7,6},{8,7},{9,8},{10,9... | collective-permute-start | bytes 798728 | tf_op jit(solution)/shard_map/ppermute | solution.py:32
  30.4 1.3 %collective-permute-done = bf16[128,512]{1,0:T(8,128)(2,1)S(1)} collective-permute-done((bf16[128,512]{1,0:T(8,128)(2,1)S(1)}, bf16[128,512]{1,0:T(8,128)(2,1)S(1)}, u32[]{:S(2)}, u32[]{:S(2)}) %collective-permute-start) | collective-permute-done | bytes 131104 | tf_op jit(solution)/shard_map/ppermute | solution.py:36
  31.8 2.6 %collective-permute-done.3.refs_0_ = bf16[2080,128]{1,0:T(8,128)(2,1)S(1)} collective-permute-done((bf16[2080,128]{1,0:T(8,128)(2,1)S(1)}, bf16[2080,128]{1,0:T(8,128)(2,1)S(1)}, u32[]{:S(2)}, u32[]{:S(2)}) %collective-permute-start.3) | collective-permute-done | bytes 532512 | tf_op jit(solution)/shard_map/ppermute | solution.py:32
  34.5 1.6 %collective-permute-done.4.refs_1_ = bf16[2080,128]{1,0:T(8,128)(2,1)S(1)} collective-permute-done((bf16[2080,128]{1,0:T(8,128)(2,1)S(1)}, bf16[2080,128]{1,0:T(8,128)(2,1)S(1)}, u32[]{:S(2)}, u32[]{:S(2)}) %collective-permute-start.4) | collective-permute-done | bytes 532512 | tf_op jit(solution)/shard_map/ppermute | solution.py:32
  36.4 5.4 %collective-permute-start.6 = (bf16[1040,128]{1,0:T(8,128)(2,1)S(1)}, bf16[1040,128]{1,0:T(8,128)(2,1)S(1)}, u32[]{:S(2)}, u32[]{:S(2)}) collective-permute-start(bf16[1040,128]{1,0:T(8,128)(2,1)S(1)} %slice.7), channel_id=1, source_target_pairs={{0,31},{1,0},{2,1},{3,2},{4,3},{5,4},{6,5},{7,6},{8,7},{9,8},{10,9... | collective-permute-start | bytes 798728 | tf_op jit(solution)/shard_map/ppermute | solution.py:32
  42.3 2.6 %absorb_stage.4 = (f32[16,128]{1,0:T(8,128)S(1)}, f32[16,128]{1,0:T(8,128)S(1)}, f32[1024,128]{1,0:T(8,128)S(1)}) custom-call(bf16[1040,128]{1,0:T(8,128)(2,1)S(1)} %copy-done.1, bf16[1040,128]{1,0:T(8,128)(2,1)S(1)} %collective-permute-done.9.refs_0_, bf16[1040,128]{1,0:T(8,128)(2,1)S(1)} %collective-permute-done.10.refs_1_, ...), custom_call_target="tpu_custom_call" | custom-call | flops 1073741824 | bytes 8388608 | tf_op jit(solution)/shard_map/absorb_stage/pallas_call | solution.py:235
  45.0 2.7 %collective-permute-start.12 = (bf16[256,512]{1,0:T(8,128)(2,1)S(1)}, bf16[256,512]{1,0:T(8,128)(2,1)S(1)}, u32[]{:S(2)}, u32[]{:S(2)}) collective-permute-start(bf16[256,512]{1,0:T(8,128)(2,1)S(1)} %pad_maximum_fusion.refs_0_), channel_id=1, source_target_pairs={{0,2},{1,3},{2,0},{3,1},{4,6},{5,7},{6,4},{7,5},{8,10},{9,11},{10,... | collective-permute-start | bytes 786440 | tf_op jit(solution)/shard_map/ppermute | solution.py:41
  47.7 0.5 collective-permute-start.13
  48.2 4.2 %absorb_stage.5 = (f32[16,128]{1,0:T(8,128)S(1)}, f32[16,128]{1,0:T(8,128)S(1)}, f32[1024,128]{1,0:T(8,128)S(1)}) custom-call(bf16[1040,128]{1,0:T(8,128)(2,1)S(1)} %copy-done.1, bf16[2080,128]{1,0:T(8,128)(2,1)S(1)} %collective-permute-done.3.refs_0_, bf16[2080,128]{1,0:T(8,128)(2,1)S(1)} %collective-permute-done.4.refs_1_, ...), custom_call_target="tpu_custom_call" | custom-call | flops 2147483648 | bytes 8388608 | tf_op jit(solution)/shard_map/absorb_stage/pallas_call | solution.py:235
  52.4 1.3 %last_stage.1 = (bf16[4,256,128]{2,1,0:T(8,128)(2,1)S(1)}, bf16[128,1024]{1,0:T(8,128)(2,1)}) custom-call(bf16[1040,128]{1,0:T(8,128)(2,1)S(1)} %copy-done.2, bf16[1040,128]{1,0:T(8,128)(2,1)S(1)} %collective-permute-done.5.refs_0_, bf16[1040,128]{1,0:T(8,128)(2,1)S(1)} %collective-permute-done.6.refs_1_, ...), custom_call_target="tpu_custom_call" | custom-call | flops 1610612736 | bytes 10485760 | tf_op jit(solution)/shard_map/last_stage/pallas_call | solution.py:272
  53.8 3.7 %collective-permute-done.11.refs_1_ = bf16[256,512]{1,0:T(8,128)(2,1)S(1)} collective-permute-done((bf16[256,512]{1,0:T(8,128)(2,1)S(1)}, bf16[256,512]{1,0:T(8,128)(2,1)S(1)}, u32[]{:S(2)}, u32[]{:S(2)}) %collective-permute-start.11) | collective-permute-done | bytes 262176 | tf_op jit(solution)/shard_map/ppermute | solution.py:41
  57.5 9.1 %all_to_all.10.own_ref = bf16[4,256,128]{2,1,0:T(8,128)(2,1)S(1)} all-to-all(bf16[4,256,128]{2,1,0:T(8,128)(2,1)S(1)} %get-tuple-element.65), channel_id=1, replica_groups=mesh['x'=4,'core'=2,'z'=8,'y'=4] {'y'}, dimensions={0} | all-to-all | bytes 524288 | tf_op jit(solution)/shard_map/all_to_all | solution.py:343
  66.5 1.5 %collective-permute-done.14.other_ref = bf16[4,256,128]{2,1,0:T(8,128)(2,1)S(1)} collective-permute-done((bf16[4,256,128]{2,1,0:T(8,128)(2,1)S(1)}, bf16[4,256,128]{2,1,0:T(8,128)(2,1)S(1)}, u32[]{:S(2)}, u32[]{:S(2)}) %collective-permute-start.14) | collective-permute-done | bytes 262176 | tf_op jit(solution)/shard_map/ppermute | solution.py:36
  68.5 21.1 %all_to_all.11 = bf16[32,32,128]{2,1,0:T(8,128)(2,1)S(1)} all-to-all(bf16[32,32,128]{2,1,0:T(8,128)(2,1)S(1)} %bitcast.11), channel_id=1, replica_groups=mesh['x'=4,'core'=2,'z'=8,'y'=4] {'x','z'}, dimensions={0} | all-to-all | bytes 524288 | tf_op jit(solution)/shard_map/all_to_all | solution.py:345
  89.7 0.6 broadcast_multiply_fusion
  (41 shorter events, 1.6 us)
Async XLA Ops:
  2.7 17.4 %collective-permute-start.1 = (bf16[1040,128]{1,0:T(8,128)(2,1)}, bf16[1040,128]{1,0:T(8,128)(2,1)S(1)}, u32[]{:S(2)}, u32[]{:S(2)}) collective-permute-start(bf16[1040,128]{1,0:T(8,128)(2,1)} %get-tuple-element.36.own_ref), channel_id=1, source_target_pairs={{0,1},{1,2},{2,3},{3,4},{4,5},{5,6},{6,7},{7,8},{8,9},{9,10},{10,1... | collective-permute-start | bytes 798728 | tf_op jit(solution)/shard_map/ppermute | solution.py:32
  4.4 15.7 %collective-permute-start.2 = (bf16[1040,128]{1,0:T(8,128)(2,1)}, bf16[1040,128]{1,0:T(8,128)(2,1)S(1)}, u32[]{:S(2)}, u32[]{:S(2)}) collective-permute-start(bf16[1040,128]{1,0:T(8,128)(2,1)} %get-tuple-element.36.own_ref), channel_id=1, source_target_pairs={{0,31},{1,0},{2,1},{3,2},{4,3},{5,4},{6,5},{7,6},{8,7},{9,8},{10,9... | collective-permute-start | bytes 798728 | tf_op jit(solution)/shard_map/ppermute | solution.py:32
  11.2 12.3 %collective-permute-start.7 = (bf16[1040,128]{1,0:T(8,128)(2,1)}, bf16[1040,128]{1,0:T(8,128)(2,1)S(1)}, u32[]{:S(2)}, u32[]{:S(2)}) collective-permute-start(bf16[1040,128]{1,0:T(8,128)(2,1)} %get-tuple-element.36.own_ref), channel_id=1, source_target_pairs={{0,4},{1,5},{2,6},{3,7},{4,8},{5,9},{6,10},{7,11},{8,12},{9,13},{1... | collective-permute-start | bytes 798728 | tf_op jit(solution)/shard_map/ppermute | solution.py:32
  11.2 12.3 %collective-permute-start.8 = (bf16[1040,128]{1,0:T(8,128)(2,1)}, bf16[1040,128]{1,0:T(8,128)(2,1)S(1)}, u32[]{:S(2)}, u32[]{:S(2)}) collective-permute-start(bf16[1040,128]{1,0:T(8,128)(2,1)} %get-tuple-element.36.own_ref), channel_id=1, source_target_pairs={{0,28},{1,29},{2,30},{3,31},{4,0},{5,1},{6,2},{7,3},{8,4},{9,5},{1... | collective-permute-start | bytes 798728 | tf_op jit(solution)/shard_map/ppermute | solution.py:32
  14.4 2.8 %copy-start = (bf16[1024,3072]{1,0:T(8,128)(2,1)S(1)}, bf16[1024,3072]{1,0:T(8,128)(2,1)}, u32[]{:S(2)}) copy-start(bf16[1024,3072]{1,0:T(8,128)(2,1)} %refs_3_.5) | copy-start | bytes 18874372
  17.2 1.0 %copy-start.1 = (bf16[1040,128]{1,0:T(8,128)(2,1)S(1)}, bf16[1040,128]{1,0:T(8,128)(2,1)}, u32[]{:S(2)}) copy-start(bf16[1040,128]{1,0:T(8,128)(2,1)} %get-tuple-element.36.own_ref) | copy-start | bytes 798724
  20.1 10.4 %copy-start.6 = (bf16[128,512]{1,0:T(8,128)(2,1)S(1)}, bf16[128,512]{1,0:T(8,128)(2,1)}, u32[]{:S(2)}) copy-start(bf16[128,512]{1,0:T(8,128)(2,1)} %get-tuple-element.38) | copy-start | bytes 393220
  20.1 11.7 %copy-start.5 = (bf16[128,512]{1,0:T(8,128)(2,1)S(1)}, bf16[128,512]{1,0:T(8,128)(2,1)}, u32[]{:S(2)}) copy-start(bf16[128,512]{1,0:T(8,128)(2,1)} %get-tuple-element.37) | copy-start | bytes 393220
  20.2 14.3 %collective-permute-start.3 = (bf16[2080,128]{1,0:T(8,128)(2,1)S(1)}, bf16[2080,128]{1,0:T(8,128)(2,1)S(1)}, u32[]{:S(2)}, u32[]{:S(2)}) collective-permute-start(bf16[2080,128]{1,0:T(8,128)(2,1)S(1)} %constant_dynamic-update-slice_fusion), channel_id=1, source_target_pairs={{0,4},{1,5},{2,6},{3,7},{4,8},{5,9},{6,10},{7,11},{8,12},{9,13},{1... | collective-permute-start | bytes 1597448 | tf_op jit(solution)/shard_map/ppermute | solution.py:32
  20.3 15.8 %collective-permute-start.4 = (bf16[2080,128]{1,0:T(8,128)(2,1)S(1)}, bf16[2080,128]{1,0:T(8,128)(2,1)S(1)}, u32[]{:S(2)}, u32[]{:S(2)}) collective-permute-start(bf16[2080,128]{1,0:T(8,128)(2,1)S(1)} %constant_dynamic-update-slice_fusion), channel_id=1, source_target_pairs={{0,28},{1,29},{2,30},{3,31},{4,0},{5,1},{6,2},{7,3},{8,4},{9,5},{1... | collective-permute-start | bytes 1597448 | tf_op jit(solution)/shard_map/ppermute | solution.py:32
  27.7 14.1 %collective-permute-start.10 = (bf16[1040,128]{1,0:T(8,128)(2,1)S(1)}, bf16[1040,128]{1,0:T(8,128)(2,1)S(1)}, u32[]{:S(2)}, u32[]{:S(2)}) collective-permute-start(bf16[1040,128]{1,0:T(8,128)(2,1)S(1)} %collective-permute-done.2.refs_2_), channel_id=1, source_target_pairs={{0,31},{1,0},{2,1},{3,2},{4,3},{5,4},{6,5},{7,6},{8,7},{9,8},{10,9... | collective-permute-start | bytes 798728 | tf_op jit(solution)/shard_map/ppermute | solution.py:32
  30.4 11.8 %collective-permute-start.9 = (bf16[1040,128]{1,0:T(8,128)(2,1)S(1)}, bf16[1040,128]{1,0:T(8,128)(2,1)S(1)}, u32[]{:S(2)}, u32[]{:S(2)}) collective-permute-start(bf16[1040,128]{1,0:T(8,128)(2,1)S(1)} %collective-permute-done.1.refs_0_), channel_id=1, source_target_pairs={{0,1},{1,2},{2,3},{3,4},{4,5},{5,6},{6,7},{7,8},{8,9},{9,10},{10,1... | collective-permute-start | bytes 798728 | tf_op jit(solution)/shard_map/ppermute | solution.py:32
  30.4 1.3 %collective-permute-start = (bf16[128,512]{1,0:T(8,128)(2,1)S(1)}, bf16[128,512]{1,0:T(8,128)(2,1)S(1)}, u32[]{:S(2)}, u32[]{:S(2)}) collective-permute-start(bf16[128,512]{1,0:T(8,128)(2,1)S(1)} %copy-done.6), channel_id=1, source_target_pairs={{0,32},{32,0},{1,33},{33,1},{2,34},{34,2},{3,35},{35,3},{4,36},{36... | collective-permute-start | bytes 393224 | tf_op jit(solution)/shard_map/ppermute | solution.py:36
  36.1 16.3 %collective-permute-start.5 = (bf16[1040,128]{1,0:T(8,128)(2,1)S(1)}, bf16[1040,128]{1,0:T(8,128)(2,1)S(1)}, u32[]{:S(2)}, u32[]{:S(2)}) collective-permute-start(bf16[1040,128]{1,0:T(8,128)(2,1)S(1)} %slice.6), channel_id=1, source_target_pairs={{0,1},{1,2},{2,3},{3,4},{4,5},{5,6},{6,7},{7,8},{8,9},{9,10},{10,1... | collective-permute-start | bytes 798728 | tf_op jit(solution)/shard_map/ppermute | solution.py:32
  36.4 16.0 %collective-permute-start.6 = (bf16[1040,128]{1,0:T(8,128)(2,1)S(1)}, bf16[1040,128]{1,0:T(8,128)(2,1)S(1)}, u32[]{:S(2)}, u32[]{:S(2)}) collective-permute-start(bf16[1040,128]{1,0:T(8,128)(2,1)S(1)} %slice.7), channel_id=1, source_target_pairs={{0,31},{1,0},{2,1},{3,2},{4,3},{5,4},{6,5},{7,6},{8,7},{9,8},{10,9... | collective-permute-start | bytes 798728 | tf_op jit(solution)/shard_map/ppermute | solution.py:32
  42.3 10.1 %slice-start = ((s8[6291456]{0:T(1024)(128)(4,1)}), s8[4194304]{0:T(1024)(128)(4,1)S(1)}, s32[]{:S(2)}) async-start(s8[6291456]{0:T(1024)(128)(4,1)} %bitcast.7), calls=%async_computation.2 | async-start | bytes 8388608
  44.8 7.6 %copy-start.2 = (bf16[1040,128]{1,0:T(8,128)(2,1)S(1)}, bf16[1040,128]{1,0:T(8,128)(2,1)}, u32[]{:S(2)}) copy-start(bf16[1040,128]{1,0:T(8,128)(2,1)} %get-tuple-element.36.own_ref) | copy-start | bytes 798724
  44.8 7.6 %copy-start.3 = (bf16[1024,1024]{1,0:T(8,128)(2,1)S(1)}, bf16[1024,1024]{1,0:T(8,128)(2,1)}, u32[]{:S(2)}) copy-start(bf16[1024,1024]{1,0:T(8,128)(2,1)} %refs_8_.1) | copy-start | bytes 6291460
  44.9 7.6 %copy-start.4 = (bf16[1,128,1024]{2,1,0:T(8,128)(2,1)S(1)}, bf16[1,128,1024]{2,1,0:T(8,128)(2,1)}, u32[]{:S(2)}) copy-start(bf16[1,128,1024]{2,1,0:T(8,128)(2,1)} %param.6) | copy-start | bytes 786436
  44.9 12.6 %collective-permute-start.11 = (bf16[256,512]{1,0:T(8,128)(2,1)S(1)}, bf16[256,512]{1,0:T(8,128)(2,1)S(1)}, u32[]{:S(2)}, u32[]{:S(2)}) collective-permute-start(bf16[256,512]{1,0:T(8,128)(2,1)S(1)} %pad_maximum_fusion.refs_0_), channel_id=1, source_target_pairs={{0,1},{1,2},{2,3},{3,0},{4,5},{5,6},{6,7},{7,4},{8,9},{9,10},{10,1... | collective-permute-start | bytes 786440 | tf_op jit(solution)/shard_map/ppermute | solution.py:41
  45.0 12.5 %collective-permute-start.12 = (bf16[256,512]{1,0:T(8,128)(2,1)S(1)}, bf16[256,512]{1,0:T(8,128)(2,1)S(1)}, u32[]{:S(2)}, u32[]{:S(2)}) collective-permute-start(bf16[256,512]{1,0:T(8,128)(2,1)S(1)} %pad_maximum_fusion.refs_0_), channel_id=1, source_target_pairs={{0,2},{1,3},{2,0},{3,1},{4,6},{5,7},{6,4},{7,5},{8,10},{9,11},{10,... | collective-permute-start | bytes 786440 | tf_op jit(solution)/shard_map/ppermute | solution.py:41
  47.7 9.8 %collective-permute-start.13 = (bf16[256,512]{1,0:T(8,128)(2,1)S(1)}, bf16[256,512]{1,0:T(8,128)(2,1)S(1)}, u32[]{:S(2)}, u32[]{:S(2)}) collective-permute-start(bf16[256,512]{1,0:T(8,128)(2,1)S(1)} %pad_maximum_fusion.refs_0_), channel_id=1, source_target_pairs={{0,3},{1,0},{2,1},{3,2},{4,7},{5,4},{6,5},{7,6},{8,11},{9,8},{10,9... | collective-permute-start | bytes 786440 | tf_op jit(solution)/shard_map/ppermute | solution.py:41
  48.2 4.2 %slice-start.1 = ((s8[6291456]{0:T(1024)(128)(4,1)}), s8[2097152]{0:T(1024)(128)(4,1)S(1)}, s32[]{:S(2)}) async-start(s8[6291456]{0:T(1024)(128)(4,1)} %bitcast.7), calls=%async_computation.3 | async-start | bytes 4194304
  66.5 1.5 %collective-permute-start.14 = (bf16[4,256,128]{2,1,0:T(8,128)(2,1)S(1)}, bf16[4,256,128]{2,1,0:T(8,128)(2,1)S(1)}, u32[]{:S(2)}, u32[]{:S(2)}) collective-permute-start(bf16[4,256,128]{2,1,0:T(8,128)(2,1)S(1)} %all_to_all.10.own_ref), channel_id=1, source_target_pairs={{0,32},{32,0},{1,33},{33,1},{2,34},{34,2},{3,35},{35,3},{4,36},{36... | collective-permute-start | bytes 786440 | tf_op jit(solution)/shard_map/ppermute | solution.py:36

commit v9 on v8

--- a/solution.py
+++ b/solution.py
@@ -241,21 +241,20 @@
     )(own, *blocks, queries, w_qkv, *state)
 
 
-def last_stage(own, blocks, left, right, queries, w_qkv, state, frames, w_out):
+def last_stage(own, blocks, left, right, queries, w_qkv, state):
     count = len(blocks)
 
     def kernel(own_ref, *refs):
         block_refs, refs = refs[:count], refs[count:]
         queries_ref, weight_ref = refs[:2]
-        frames_ref, wout_ref, attended_ref, out_ref = refs[5:9]
-        state_refs = refs[9:12]
+        attended_ref, natural_ref = refs[5:7]
+        state_refs = refs[7:10]
         copied(refs[2:5], state_refs)
         absorb_both(
             own_ref, located(block_refs, left), located(block_refs, right), queries_ref, weight_ref, state_refs
         )
         _, sums_ref, acc_ref = state_refs
         n_y, rows = attended_ref.shape[0], WIDTH // N_SEQ
-        chunks = []
         for c in range(CHUNKS):
             parts = []
             for h in (2 * c, 2 * c + 1):
@@ -264,10 +263,7 @@
             for k in range(LANES // rows):
                 z, y = divmod(c * (LANES // rows) + k, n_y)
                 attended_ref[y, z * rows : (z + 1) * rows, :] = chunk[k * rows : (k + 1) * rows, :]
-            chunks.append(jnp.transpose(chunk))
-        attended = jnp.concatenate(chunks, axis=1)
-        product = jnp.dot(attended, wout_ref[...], preferred_element_type=F32)
-        out_ref[...] = (frames_ref[...].astype(F32) + product).astype(BF16)
+            natural_ref[:, c * LANES : (c + 1) * LANES] = jnp.transpose(chunk)
 
     return pl.pallas_call(
         kernel,
@@ -279,7 +275,24 @@
         compiler_params=LIMIT,
         cost_estimate=cost(len(left) + len(right) + 1, 10),
         name="last_stage",
-    )(own, *blocks, queries, w_qkv, *state, frames, w_out)
+    )(own, *blocks, queries, w_qkv, *state)
+
+
+def project_kernel(attended_ref, wout_ref, frames_ref, out_ref):
+    product = jnp.dot(attended_ref[...], wout_ref[...], preferred_element_type=F32)
+    out_ref[...] = (frames_ref[...].astype(F32) + product).astype(BF16)
+
+
+def project(attended, w_out, frames):
+    return pl.pallas_call(
+        project_kernel,
+        out_shape=jax.ShapeDtypeStruct((ROWS, WIDTH), BF16),
+        compiler_params=LIMIT,
+        cost_estimate=pl.CostEstimate(
+            flops=2 * ROWS * WIDTH * WIDTH, bytes_accessed=3 << 20, transcendentals=0
+        ),
+        name="project",
+    )(attended, w_out, frames)
 
 
 def grad_kernel(place_ref, own_ref, other_ref, *refs):
@@ -335,11 +348,10 @@
     state = absorb_stage(
         own, (left_two, right_two), ((0, 1), (0, 0)), ((1, 0), (1, 1)), queries, w_qkv, state
     )
-    attended, block_out = last_stage(
-        own, (left6, right6), ((0, 0),), ((1, 0),), queries, w_qkv, state, frames, w_out
-    )
+    attended, natural = last_stage(own, (left6, right6), ((0, 0),), ((1, 0),), queries, w_qkv, state)
     attended, grads = lax.optimization_barrier((attended, grads))
 
+    block_out = project(natural, w_out, frames)
     pieces = lax.all_to_all(attended, "y", 0, 0, tiled=True)
     share = grad_product(place, pieces, core_swapped(pieces), grads)
     parts = lax.all_to_all(share.reshape(-1, WIDTH // N_SEQ, LANES), ("x", "z"), 0, 0, tiled=True)

time: 91.8 us -> 95.4 us (1.039)
  blocking collectives: 30.2 us -> 9.05 us
  waiting for transfers between devices: 11.3 us -> 25.2 us
  starting transfers between devices: 26.8 us -> 38.8 us
  Pallas kernels: 16.6 us -> 11.9 us
  local copies, waits for them, and re-layouts: 3.86 us -> 7.16 us
    all_to_all x1 -> x0, blocking collectives: 21.1 us -> none  [local(): lax.all_to_all(share.reshape(-1, WIDTH // N_SEQ, LANES), ('x', 'z'), 0, 0...]
    all_to_all x0 -> x1, starting transfers between devices: none -> 10.1 us  [local(): lax.all_to_all(share.reshape(-1, WIDTH // N_SEQ, LANES), ('x', 'z'), 0, 0...]
    all_to_all x0 -> x1, waiting for transfers between devices: none -> 8.83 us  [local(): lax.all_to_all(share.reshape(-1, WIDTH // N_SEQ, LANES), ('x', 'z'), 0, 0...]
    pallas_call x3, Pallas kernels: 10.9 us -> 4.43 us  [absorb_stage(): pl.pallas_call(kernel, out_shape=list(STATE_SHAPES), compiler_params=LIMI...]
    ppermute x3, waiting for transfers between devices: 3.7 us -> 8.67 us  [turned(): return lax.ppermute(block, 'y', [(i, (i + distance) % n) for i in range(n)])]
    unnamed x19 -> x21, local copies, waits for them, and re-layouts: 3.79 us -> 7.09 us
    ppermute x3, starting transfers between devices: 3.31 us -> 5.25 us  [turned(): return lax.ppermute(block, 'y', [(i, (i + distance) % n) for i in range(n)])]
    pallas_call x1, Pallas kernels: 0.43 us -> 2.1 us  [grad_product(): pl.pallas_call(grad_kernel, in_specs=[pl.BlockSpec(memory_space=pltpu.SME...]
  transfers between devices with their start and end apart: 15 -> 16, of which waited for: 6 -> 7; matrix products, arithmetic and copies ran while one was open for 0% -> 0% of each run, Pallas kernels for 16% -> 8%
where the time goes in v9:
time: 95.4 us; the launch traced here: 93.7 us
  starting transfers between devices  38.8 us (41%)
  waiting for transfers between devices  25.2 us (26%)
  Pallas kernels  11.9 us (12%)
  blocking collectives  9.05 us (9%)
  local copies, waits for them, and re-layouts  7.16 us (8%)
    ppermute x10, starting transfers between devices, shifted(): return lax.ppermute(block, SEQ, route)  23.4 us
    all_to_all x1, starting transfers between devices, local(): lax.all_to_all(share.reshape(-1, WIDTH // N_SEQ, LANES), ('x', 'z'), 0, 0...  10.1 us
    all_to_all x1, blocking collectives, local(): pieces = lax.all_to_all(attended, 'y', 0, 0, tiled=True)  9.05 us
    all_to_all x1, waiting for transfers between devices, local(): lax.all_to_all(share.reshape(-1, WIDTH // N_SEQ, LANES), ('x', 'z'), 0, 0...  8.83 us
    ppermute x3, waiting for transfers between devices, turned(): return lax.ppermute(block, 'y', [(i, (i + distance) % n) for i in range(n)])  8.67 us
    unnamed x21, local copies, waits for them, and re-layouts  7.09 us
    ppermute x3, starting transfers between devices, turned(): return lax.ppermute(block, 'y', [(i, (i + distance) % n) for i in range(n)])  5.25 us
    ppermute x10, waiting for transfers between devices, shifted(): return lax.ppermute(block, SEQ, route)  4.74 us
  transfers between devices with their start and end apart: 16, of which 7 were waited for; matrix products, arithmetic and copies ran while one was open for 0% of the time, Pallas kernels for 8%

profile of v9, /device:TPU:4, one launch (start us, length us, event | category | flops | bytes accessed | tf_op | source)
XLA Modules:
  0.0 93.7 jit_solution(11640482277753395712)
XLA Ops:
  0.6 2.1 %layer_norm.1 = (bf16[1040,128]{1,0:T(8,128)(2,1)}, bf16[128,512]{1,0:T(8,128)(2,1)}, bf16[128,512]{1,0:T(8,128)(2,1)}) custom-call(s32[1]{0:T(128)} %bitcast.core_ref, bf16[128,1024]{1,0:T(8,128)(2,1)} %bitcast.7, s32[1,128]{1,0:T(1,128)} %ids_hbm.1, f32[1,1024]{1,0:T(1,128)} %bitcast.11, bf16[128,1024]{1,0:T(8,128)(2,1)} %bitcast.9), custom_call_target="tpu_custom_call" | custom-call | tf_op jit(solution)/shard_map/layer_norm/pallas_call | solution.py:75
  2.7 1.7 %collective-permute-start.1 = (bf16[1040,128]{1,0:T(8,128)(2,1)}, bf16[1040,128]{1,0:T(8,128)(2,1)S(1)}, u32[]{:S(2)}, u32[]{:S(2)}) collective-permute-start(bf16[1040,128]{1,0:T(8,128)(2,1)} %get-tuple-element.36.own_ref), channel_id=1, source_target_pairs={{0,1},{1,2},{2,3},{3,4},{4,5},{5,6},{6,7},{7,8},{8,9},{9,10},{10,1... | collective-permute-start | bytes 798728 | tf_op jit(solution)/shard_map/ppermute | solution.py:32
  4.4 6.8 %collective-permute-start.2 = (bf16[1040,128]{1,0:T(8,128)(2,1)}, bf16[1040,128]{1,0:T(8,128)(2,1)S(1)}, u32[]{:S(2)}, u32[]{:S(2)}) collective-permute-start(bf16[1040,128]{1,0:T(8,128)(2,1)} %get-tuple-element.36.own_ref), channel_id=1, source_target_pairs={{0,31},{1,0},{2,1},{3,2},{4,3},{5,4},{6,5},{7,6},{8,7},{9,8},{10,9... | collective-permute-start | bytes 798728 | tf_op jit(solution)/shard_map/ppermute | solution.py:32
  11.2 3.2 %collective-permute-start.8 = (bf16[1040,128]{1,0:T(8,128)(2,1)}, bf16[1040,128]{1,0:T(8,128)(2,1)S(1)}, u32[]{:S(2)}, u32[]{:S(2)}) collective-permute-start(bf16[1040,128]{1,0:T(8,128)(2,1)} %get-tuple-element.36.own_ref), channel_id=1, source_target_pairs={{0,28},{1,29},{2,30},{3,31},{4,0},{5,1},{6,2},{7,3},{8,4},{9,5},{1... | collective-permute-start | bytes 798728 | tf_op jit(solution)/shard_map/ppermute | solution.py:32
  14.4 2.8 %copy-done = bf16[1024,3072]{1,0:T(8,128)(2,1)S(1)} copy-done((bf16[1024,3072]{1,0:T(8,128)(2,1)S(1)}, bf16[1024,3072]{1,0:T(8,128)(2,1)}, u32[]{:S(2)}) %copy-start) | copy-done | bytes 6291480
  17.2 0.9 %copy-done.1 = bf16[1040,128]{1,0:T(8,128)(2,1)S(1)} copy-done((bf16[1040,128]{1,0:T(8,128)(2,1)S(1)}, bf16[1040,128]{1,0:T(8,128)(2,1)}, u32[]{:S(2)}) %copy-start.1) | copy-done | bytes 266264
  18.2 1.9 %own_block.1 = (bf16[8,128,256]{2,1,0:T(8,128)(2,1)S(1)}, f32[16,128]{1,0:T(8,128)S(1)}, f32[16,128]{1,0:T(8,128)S(1)}, f32[1024,128]{1,0:T(8,128)S(1)}) custom-call(bf16[1040,128]{1,0:T(8,128)(2,1)S(1)} %copy-done.1, bf16[1024,3072]{1,0:T(8,128)(2,1)S(1)} %copy-done), custom_call_target="tpu_custom_call" | custom-call | flops 1610612736 | bytes 8388608 | tf_op jit(solution)/shard_map/own_block/pallas_call | solution.py:194
  20.3 3.2 %collective-permute-start.4 = (bf16[2080,128]{1,0:T(8,128)(2,1)S(1)}, bf16[2080,128]{1,0:T(8,128)(2,1)S(1)}, u32[]{:S(2)}, u32[]{:S(2)}) collective-permute-start(bf16[2080,128]{1,0:T(8,128)(2,1)S(1)} %constant_dynamic-update-slice_fusion), channel_id=1, source_target_pairs={{0,28},{1,29},{2,30},{3,31},{4,0},{5,1},{6,2},{7,3},{8,4},{9,5},{1... | collective-permute-start | bytes 1597448 | tf_op jit(solution)/shard_map/ppermute | solution.py:32
  23.5 4.2 %absorb_stage.3 = (f32[16,128]{1,0:T(8,128)S(1)}, f32[16,128]{1,0:T(8,128)S(1)}, f32[1024,128]{1,0:T(8,128)S(1)}) custom-call(bf16[1040,128]{1,0:T(8,128)(2,1)S(1)} %copy-done.1, bf16[1040,128]{1,0:T(8,128)(2,1)S(1)} %collective-permute-done.1.refs_0_, bf16[1040,128]{1,0:T(8,128)(2,1)S(1)} %collective-permute-done.7.refs_1_, ...), custom_call_target="tpu_custom_call" | custom-call | flops 2147483648 | bytes 8388608 | tf_op jit(solution)/shard_map/absorb_stage/pallas_call | solution.py:235
  27.7 2.8 %collective-permute-start.10 = (bf16[1040,128]{1,0:T(8,128)(2,1)S(1)}, bf16[1040,128]{1,0:T(8,128)(2,1)S(1)}, u32[]{:S(2)}, u32[]{:S(2)}) collective-permute-start(bf16[1040,128]{1,0:T(8,128)(2,1)S(1)} %collective-permute-done.2.refs_2_), channel_id=1, source_target_pairs={{0,31},{1,0},{2,1},{3,2},{4,3},{5,4},{6,5},{7,6},{8,7},{9,8},{10,9... | collective-permute-start | bytes 798728 | tf_op jit(solution)/shard_map/ppermute | solution.py:32
  30.4 1.3 %collective-permute-done = bf16[128,512]{1,0:T(8,128)(2,1)S(1)} collective-permute-done((bf16[128,512]{1,0:T(8,128)(2,1)S(1)}, bf16[128,512]{1,0:T(8,128)(2,1)S(1)}, u32[]{:S(2)}, u32[]{:S(2)}) %collective-permute-start) | collective-permute-done | bytes 131104 | tf_op jit(solution)/shard_map/ppermute | solution.py:36
  31.8 2.6 %collective-permute-done.3.refs_0_ = bf16[2080,128]{1,0:T(8,128)(2,1)S(1)} collective-permute-done((bf16[2080,128]{1,0:T(8,128)(2,1)S(1)}, bf16[2080,128]{1,0:T(8,128)(2,1)S(1)}, u32[]{:S(2)}, u32[]{:S(2)}) %collective-permute-start.3) | collective-permute-done | bytes 532512 | tf_op jit(solution)/shard_map/ppermute | solution.py:32
  34.5 1.6 %collective-permute-done.4.refs_1_ = bf16[2080,128]{1,0:T(8,128)(2,1)S(1)} collective-permute-done((bf16[2080,128]{1,0:T(8,128)(2,1)S(1)}, bf16[2080,128]{1,0:T(8,128)(2,1)S(1)}, u32[]{:S(2)}, u32[]{:S(2)}) %collective-permute-start.4) | collective-permute-done | bytes 532512 | tf_op jit(solution)/shard_map/ppermute | solution.py:32
  36.4 5.4 %collective-permute-start.6 = (bf16[1040,128]{1,0:T(8,128)(2,1)S(1)}, bf16[1040,128]{1,0:T(8,128)(2,1)S(1)}, u32[]{:S(2)}, u32[]{:S(2)}) collective-permute-start(bf16[1040,128]{1,0:T(8,128)(2,1)S(1)} %slice.7), channel_id=1, source_target_pairs={{0,31},{1,0},{2,1},{3,2},{4,3},{5,4},{6,5},{7,6},{8,7},{9,8},{10,9... | collective-permute-start | bytes 798728 | tf_op jit(solution)/shard_map/ppermute | solution.py:32
  42.5 5.2 %collective-permute-start.12 = (bf16[256,512]{1,0:T(8,128)(2,1)S(1)}, bf16[256,512]{1,0:T(8,128)(2,1)S(1)}, u32[]{:S(2)}, u32[]{:S(2)}) collective-permute-start(bf16[256,512]{1,0:T(8,128)(2,1)S(1)} %pad_maximum_fusion.refs_0_), channel_id=1, source_target_pairs={{0,2},{1,3},{2,0},{3,1},{4,6},{5,7},{6,4},{7,5},{8,10},{9,11},{10,... | collective-permute-start | bytes 786440 | tf_op jit(solution)/shard_map/ppermute | solution.py:41
  48.8 8.7 %collective-permute-done.11.refs_1_ = bf16[256,512]{1,0:T(8,128)(2,1)S(1)} collective-permute-done((bf16[256,512]{1,0:T(8,128)(2,1)S(1)}, bf16[256,512]{1,0:T(8,128)(2,1)S(1)}, u32[]{:S(2)}, u32[]{:S(2)}) %collective-permute-start.11) | collective-permute-done | bytes 262176 | tf_op jit(solution)/shard_map/ppermute | solution.py:41
  58.2 9.1 %all_to_all.10.own_ref = bf16[4,256,128]{2,1,0:T(8,128)(2,1)S(1)} all-to-all(bf16[4,256,128]{2,1,0:T(8,128)(2,1)S(1)} %get-tuple-element.65), channel_id=1, replica_groups=mesh['x'=4,'core'=2,'z'=8,'y'=4] {'y'}, dimensions={0} | all-to-all | bytes 524288 | tf_op jit(solution)/shard_map/all_to_all | solution.py:355
  67.2 1.7 %collective-permute-done.14.other_ref = bf16[4,256,128]{2,1,0:T(8,128)(2,1)} collective-permute-done((bf16[4,256,128]{2,1,0:T(8,128)(2,1)S(1)}, bf16[4,256,128]{2,1,0:T(8,128)(2,1)}, u32[]{:S(2)}, u32[]{:S(2)}) %collective-permute-start.14) | collective-permute-done | bytes 262176 | tf_op jit(solution)/shard_map/ppermute | solution.py:36
  68.9 0.9 %copy-done.5 = bf16[256,512]{1,0:T(8,128)(2,1)S(1)} copy-done((bf16[256,512]{1,0:T(8,128)(2,1)S(1)}, bf16[256,512]{1,0:T(8,128)(2,1)}, u32[]{:S(2)}) %copy-start.5) | copy-done | bytes 262168
  69.9 2.1 %grad_product.1 = bf16[4,256,128]{2,1,0:T(8,128)(2,1)} custom-call(s32[1]{0:T(128)} %bitcast.5.place_ref, bf16[4,256,128]{2,1,0:T(8,128)(2,1)S(1)} %all_to_all.10.own_ref, bf16[4,256,128]{2,1,0:T(8,128)(2,1)} %collective-permute-done.14.other_ref, bf16[256,512]{1,0:T(8,128)(2,1)S(1)} %pad_maximum_fusion.refs_0_, ...), custom_call_target="tpu_custom_call" | custom-call | tf_op jit(solution)/shard_map/grad_product/pallas_call | solution.py:315
  72.0 10.1 %all-to-all-start.1 = ((bf16[32,32,128]{2,1,0:T(8,128)(2,1)}), bf16[32,32,128]{2,1,0:T(8,128)(2,1)S(1)}, u32[]{:S(2)}, u32[]{:S(2)}) async-start(bf16[32,32,128]{2,1,0:T(8,128)(2,1)} %bitcast.6), calls=%async_computation.1 | async-start | bytes 524288 | tf_op jit(solution)/shard_map/all_to_all | solution.py:357
  82.1 0.9 %copy-done.7 = bf16[128,1024]{1,0:T(8,128)(2,1)S(1)} copy-done((bf16[128,1024]{1,0:T(8,128)(2,1)S(1)}, bf16[128,1024]{1,0:T(8,128)(2,1)}, u32[]{:S(2)}) %copy-start.7) | copy-done | bytes 262168
  83.1 1.1 %project.1 = bf16[128,1024]{1,0:T(8,128)(2,1)} custom-call(bf16[128,1024]{1,0:T(8,128)(2,1)S(1)} %copy-done.7, bf16[1024,1024]{1,0:T(8,128)(2,1)S(1)} %copy-done.2, bf16[128,1024]{1,0:T(8,128)(2,1)S(1)} %bitcast.8), custom_call_target="tpu_custom_call" | custom-call | flops 268435456 | bytes 3145728 | tf_op jit(solution)/shard_map/project/pallas_call | solution.py:287
  84.2 8.8 %all-to-all-done.1 = bf16[32,32,128]{2,1,0:T(8,128)(2,1)S(1)} async-done(((bf16[32,32,128]{2,1,0:T(8,128)(2,1)}), bf16[32,32,128]{2,1,0:T(8,128)(2,1)S(1)}, u32[]{:S(2)}, u32[]{:S(2)}) %all-to-all-start.1) | async-done | bytes 262176 | tf_op jit(solution)/shard_map/all_to_all | solution.py:357
  (44 shorter events, 3.7 us)
Async XLA Ops:
  2.7 17.4 %collective-permute-start.1 = (bf16[1040,128]{1,0:T(8,128)(2,1)}, bf16[1040,128]{1,0:T(8,128)(2,1)S(1)}, u32[]{:S(2)}, u32[]{:S(2)}) collective-permute-start(bf16[1040,128]{1,0:T(8,128)(2,1)} %get-tuple-element.36.own_ref), channel_id=1, source_target_pairs={{0,1},{1,2},{2,3},{3,4},{4,5},{5,6},{6,7},{7,8},{8,9},{9,10},{10,1... | collective-permute-start | bytes 798728 | tf_op jit(solution)/shard_map/ppermute | solution.py:32
  4.4 15.7 %collective-permute-start.2 = (bf16[1040,128]{1,0:T(8,128)(2,1)}, bf16[1040,128]{1,0:T(8,128)(2,1)S(1)}, u32[]{:S(2)}, u32[]{:S(2)}) collective-permute-start(bf16[1040,128]{1,0:T(8,128)(2,1)} %get-tuple-element.36.own_ref), channel_id=1, source_target_pairs={{0,31},{1,0},{2,1},{3,2},{4,3},{5,4},{6,5},{7,6},{8,7},{9,8},{10,9... | collective-permute-start | bytes 798728 | tf_op jit(solution)/shard_map/ppermute | solution.py:32
  11.2 12.3 %collective-permute-start.7 = (bf16[1040,128]{1,0:T(8,128)(2,1)}, bf16[1040,128]{1,0:T(8,128)(2,1)S(1)}, u32[]{:S(2)}, u32[]{:S(2)}) collective-permute-start(bf16[1040,128]{1,0:T(8,128)(2,1)} %get-tuple-element.36.own_ref), channel_id=1, source_target_pairs={{0,4},{1,5},{2,6},{3,7},{4,8},{5,9},{6,10},{7,11},{8,12},{9,13},{1... | collective-permute-start | bytes 798728 | tf_op jit(solution)/shard_map/ppermute | solution.py:32
  11.2 12.3 %collective-permute-start.8 = (bf16[1040,128]{1,0:T(8,128)(2,1)}, bf16[1040,128]{1,0:T(8,128)(2,1)S(1)}, u32[]{:S(2)}, u32[]{:S(2)}) collective-permute-start(bf16[1040,128]{1,0:T(8,128)(2,1)} %get-tuple-element.36.own_ref), channel_id=1, source_target_pairs={{0,28},{1,29},{2,30},{3,31},{4,0},{5,1},{6,2},{7,3},{8,4},{9,5},{1... | collective-permute-start | bytes 798728 | tf_op jit(solution)/shard_map/ppermute | solution.py:32
  14.4 2.8 %copy-start = (bf16[1024,3072]{1,0:T(8,128)(2,1)S(1)}, bf16[1024,3072]{1,0:T(8,128)(2,1)}, u32[]{:S(2)}) copy-start(bf16[1024,3072]{1,0:T(8,128)(2,1)} %refs_3_.5) | copy-start | bytes 18874372
  17.2 1.0 %copy-start.1 = (bf16[1040,128]{1,0:T(8,128)(2,1)S(1)}, bf16[1040,128]{1,0:T(8,128)(2,1)}, u32[]{:S(2)}) copy-start(bf16[1040,128]{1,0:T(8,128)(2,1)} %get-tuple-element.36.own_ref) | copy-start | bytes 798724
  20.1 10.4 %copy-start.9 = (bf16[128,512]{1,0:T(8,128)(2,1)S(1)}, bf16[128,512]{1,0:T(8,128)(2,1)}, u32[]{:S(2)}) copy-start(bf16[128,512]{1,0:T(8,128)(2,1)} %get-tuple-element.38) | copy-start | bytes 393220
  20.1 11.7 %copy-start.8 = (bf16[128,512]{1,0:T(8,128)(2,1)S(1)}, bf16[128,512]{1,0:T(8,128)(2,1)}, u32[]{:S(2)}) copy-start(bf16[128,512]{1,0:T(8,128)(2,1)} %get-tuple-element.37) | copy-start | bytes 393220
  20.2 14.3 %collective-permute-start.3 = (bf16[2080,128]{1,0:T(8,128)(2,1)S(1)}, bf16[2080,128]{1,0:T(8,128)(2,1)S(1)}, u32[]{:S(2)}, u32[]{:S(2)}) collective-permute-start(bf16[2080,128]{1,0:T(8,128)(2,1)S(1)} %constant_dynamic-update-slice_fusion), channel_id=1, source_target_pairs={{0,4},{1,5},{2,6},{3,7},{4,8},{5,9},{6,10},{7,11},{8,12},{9,13},{1... | collective-permute-start | bytes 1597448 | tf_op jit(solution)/shard_map/ppermute | solution.py:32
  20.3 15.8 %collective-permute-start.4 = (bf16[2080,128]{1,0:T(8,128)(2,1)S(1)}, bf16[2080,128]{1,0:T(8,128)(2,1)S(1)}, u32[]{:S(2)}, u32[]{:S(2)}) collective-permute-start(bf16[2080,128]{1,0:T(8,128)(2,1)S(1)} %constant_dynamic-update-slice_fusion), channel_id=1, source_target_pairs={{0,28},{1,29},{2,30},{3,31},{4,0},{5,1},{6,2},{7,3},{8,4},{9,5},{1... | collective-permute-start | bytes 1597448 | tf_op jit(solution)/shard_map/ppermute | solution.py:32
  27.7 14.1 %collective-permute-start.10 = (bf16[1040,128]{1,0:T(8,128)(2,1)S(1)}, bf16[1040,128]{1,0:T(8,128)(2,1)S(1)}, u32[]{:S(2)}, u32[]{:S(2)}) collective-permute-start(bf16[1040,128]{1,0:T(8,128)(2,1)S(1)} %collective-permute-done.2.refs_2_), channel_id=1, source_target_pairs={{0,31},{1,0},{2,1},{3,2},{4,3},{5,4},{6,5},{7,6},{8,7},{9,8},{10,9... | collective-permute-start | bytes 798728 | tf_op jit(solution)/shard_map/ppermute | solution.py:32
  30.4 11.8 %collective-permute-start.9 = (bf16[1040,128]{1,0:T(8,128)(2,1)S(1)}, bf16[1040,128]{1,0:T(8,128)(2,1)S(1)}, u32[]{:S(2)}, u32[]{:S(2)}) collective-permute-start(bf16[1040,128]{1,0:T(8,128)(2,1)S(1)} %collective-permute-done.1.refs_0_), channel_id=1, source_target_pairs={{0,1},{1,2},{2,3},{3,4},{4,5},{5,6},{6,7},{7,8},{8,9},{9,10},{10,1... | collective-permute-start | bytes 798728 | tf_op jit(solution)/shard_map/ppermute | solution.py:32
  30.4 1.3 %collective-permute-start = (bf16[128,512]{1,0:T(8,128)(2,1)S(1)}, bf16[128,512]{1,0:T(8,128)(2,1)S(1)}, u32[]{:S(2)}, u32[]{:S(2)}) collective-permute-start(bf16[128,512]{1,0:T(8,128)(2,1)S(1)} %copy-done.9), channel_id=1, source_target_pairs={{0,32},{32,0},{1,33},{33,1},{2,34},{34,2},{3,35},{35,3},{4,36},{36... | collective-permute-start | bytes 393224 | tf_op jit(solution)/shard_map/ppermute | solution.py:36
  36.1 11.8 %collective-permute-start.5 = (bf16[1040,128]{1,0:T(8,128)(2,1)S(1)}, bf16[1040,128]{1,0:T(8,128)(2,1)S(1)}, u32[]{:S(2)}, u32[]{:S(2)}) collective-permute-start(bf16[1040,128]{1,0:T(8,128)(2,1)S(1)} %slice.6), channel_id=1, source_target_pairs={{0,1},{1,2},{2,3},{3,4},{4,5},{5,6},{6,7},{7,8},{8,9},{9,10},{10,1... | collective-permute-start | bytes 798728 | tf_op jit(solution)/shard_map/ppermute | solution.py:32
  36.4 11.5 %collective-permute-start.6 = (bf16[1040,128]{1,0:T(8,128)(2,1)S(1)}, bf16[1040,128]{1,0:T(8,128)(2,1)S(1)}, u32[]{:S(2)}, u32[]{:S(2)}) collective-permute-start(bf16[1040,128]{1,0:T(8,128)(2,1)S(1)} %slice.7), channel_id=1, source_target_pairs={{0,31},{1,0},{2,1},{3,2},{4,3},{5,4},{6,5},{7,6},{8,7},{9,8},{10,9... | collective-permute-start | bytes 798728 | tf_op jit(solution)/shard_map/ppermute | solution.py:32
  42.4 15.1 %collective-permute-start.11 = (bf16[256,512]{1,0:T(8,128)(2,1)S(1)}, bf16[256,512]{1,0:T(8,128)(2,1)S(1)}, u32[]{:S(2)}, u32[]{:S(2)}) collective-permute-start(bf16[256,512]{1,0:T(8,128)(2,1)S(1)} %pad_maximum_fusion.refs_0_), channel_id=1, source_target_pairs={{0,1},{1,2},{2,3},{3,0},{4,5},{5,6},{6,7},{7,4},{8,9},{9,10},{10,1... | collective-permute-start | bytes 786440 | tf_op jit(solution)/shard_map/ppermute | solution.py:41
  42.5 15.0 %collective-permute-start.12 = (bf16[256,512]{1,0:T(8,128)(2,1)S(1)}, bf16[256,512]{1,0:T(8,128)(2,1)S(1)}, u32[]{:S(2)}, u32[]{:S(2)}) collective-permute-start(bf16[256,512]{1,0:T(8,128)(2,1)S(1)} %pad_maximum_fusion.refs_0_), channel_id=1, source_target_pairs={{0,2},{1,3},{2,0},{3,1},{4,6},{5,7},{6,4},{7,5},{8,10},{9,11},{10,... | collective-permute-start | bytes 786440 | tf_op jit(solution)/shard_map/ppermute | solution.py:41
  47.6 9.8 %collective-permute-start.13 = (bf16[256,512]{1,0:T(8,128)(2,1)S(1)}, bf16[256,512]{1,0:T(8,128)(2,1)S(1)}, u32[]{:S(2)}, u32[]{:S(2)}) collective-permute-start(bf16[256,512]{1,0:T(8,128)(2,1)S(1)} %pad_maximum_fusion.refs_0_), channel_id=1, source_target_pairs={{0,3},{1,0},{2,1},{3,2},{4,7},{5,4},{6,5},{7,6},{8,11},{9,8},{10,9... | collective-permute-start | bytes 786440 | tf_op jit(solution)/shard_map/ppermute | solution.py:41
  47.8 34.3 %copy-start.2 = (bf16[1024,1024]{1,0:T(8,128)(2,1)S(1)}, bf16[1024,1024]{1,0:T(8,128)(2,1)}, u32[]{:S(2)}) copy-start(bf16[1024,1024]{1,0:T(8,128)(2,1)} %wout_ref.1) | copy-start | bytes 6291460
  47.8 34.3 %copy-start.3 = (bf16[1,128,1024]{2,1,0:T(8,128)(2,1)S(1)}, bf16[1,128,1024]{2,1,0:T(8,128)(2,1)}, u32[]{:S(2)}) copy-start(bf16[1,128,1024]{2,1,0:T(8,128)(2,1)} %param.6) | copy-start | bytes 786436
  67.2 1.7 %collective-permute-start.14 = (bf16[4,256,128]{2,1,0:T(8,128)(2,1)S(1)}, bf16[4,256,128]{2,1,0:T(8,128)(2,1)}, u32[]{:S(2)}, u32[]{:S(2)}) collective-permute-start(bf16[4,256,128]{2,1,0:T(8,128)(2,1)S(1)} %all_to_all.10.own_ref), channel_id=1, source_target_pairs={{0,32},{32,0},{1,33},{33,1},{2,34},{34,2},{3,35},{35,3},{4,36},{36... | collective-permute-start | bytes 786440 | tf_op jit(solution)/shard_map/ppermute | solution.py:36
  68.9 1.0 %copy-start.5 = (bf16[256,512]{1,0:T(8,128)(2,1)S(1)}, bf16[256,512]{1,0:T(8,128)(2,1)}, u32[]{:S(2)}) copy-start(bf16[256,512]{1,0:T(8,128)(2,1)} %copy-done.4) | copy-start | bytes 786436
  72.0 21.1 %all-to-all-start.1 = ((bf16[32,32,128]{2,1,0:T(8,128)(2,1)}), bf16[32,32,128]{2,1,0:T(8,128)(2,1)S(1)}, u32[]{:S(2)}, u32[]{:S(2)}) async-start(bf16[32,32,128]{2,1,0:T(8,128)(2,1)} %bitcast.6), calls=%async_computation.1 | async-start | bytes 524288 | tf_op jit(solution)/shard_map/all_to_all | solution.py:357
  82.1 1.0 %copy-start.7 = (bf16[128,1024]{1,0:T(8,128)(2,1)S(1)}, bf16[128,1024]{1,0:T(8,128)(2,1)}, u32[]{:S(2)}) copy-start(bf16[128,1024]{1,0:T(8,128)(2,1)} %copy-done.6) | copy-start | bytes 786436
  (2 other events, 1.4 us)
